TPU v7x, 32 devices: a whole 2x2x4 slice. The times are simulated.
32 devices in a mesh: dp: 4 (over x, core), seq: 8 (over z, y).
Axes of the slice: x: 2, y: 2, z: 4, core: 2. Of those that a mesh axis runs over, the one named last changes fastest.
Arguments:
- qkv: bfloat16 [3, 4, 1024, 16, 128], P(None, 'dp', 'seq'), may hold values from -6 to 6
- tile_mask: int32 [8, 8, 8], replicated, may hold values from 0 to 1, as said below
- d_out: bfloat16 [4, 1024, 3072], P('dp', 'seq'), may hold values from -6 to 6
- w_out: bfloat16 [16, 128, 3072], P('seq'), may hold values from -0.109375 to 0.109375
- momentum: float32 [16, 128, 3072], P('seq'), may hold values from -170 to 170
Outputs:
- grad_qkv: bfloat16 [3, 4, 1024, 16, 128], P(None, 'dp', 'seq')
- synced_momentum: bfloat16 [16, 128, 3072], P('seq')
- worker_error: float32 [4, 16, 128, 3072], P('dp', 'seq')
- server_error: float32 [16, 128, 3072], P('seq', 'dp')
Inputs may be any that keep to these rules, and one draw needn't show every extreme that they name: tile_mask[g, i, j] is 1 exactly when tiles i and j, numbered frame by frame over 2 frames of 2 by 2 tiles, differ by at most a per-group reach in frames (0 to 2), in tile rows (0 or 1) and in tile columns (0 or 1); every tile sees itself.
All inputs are finite; a program needn't handle non-finite values. Where the computation divides by a largest or mean magnitude, that divisor is 1e-20 or more.
Results may differ from a plain program's by a relative error of at most 0.0085.
Values may be sent and summed in bfloat16 or wider, within the bound.
No kernel may reach another device: no remote copies, remote signals or barrier semaphores. Data moves between devices by JAX's collectives and lax.ppermute only.
A program may use at most 128 MiB of HBM per device.

v0:
```python
import math

import jax
import jax.numpy as jnp
from jax import lax
from jax.sharding import PartitionSpec as P

HEADS = 16
GROUPS = 8
TILE = 128


def body(qkv, tile_mask, d_out, w_out, momentum):
    seq_count = lax.axis_size("seq")
    worker_count = lax.axis_size("dp")
    tokens_here = qkv.shape[2]
    head_size = qkv.shape[4]
    length = tokens_here * seq_count
    heads_here = HEADS // seq_count
    inv_root = 1.0 / math.sqrt(head_size)
    block_rows = min(512, length)
    block_count = length // block_rows
    block_tiles = block_rows // TILE
    local = lax.all_to_all(qkv, "seq", split_axis=3, concat_axis=2, tiled=True)
    queries = local[0, 0]
    keys = local[1, 0]
    values = local[2, 0]
    head_ids = lax.axis_index("seq") * heads_here + jnp.arange(heads_here)
    group_ids = head_ids // (HEADS // GROUPS)
    picks = (group_ids[:, None] == jnp.arange(GROUPS)[None, :]).astype(jnp.int32)
    head_tiles = jnp.sum(picks[:, :, None, None] * tile_mask[None], axis=1)

    def block_probs(query_block, block_index):
        scores = (
            jnp.einsum("qhe,khe->hqk", query_block, keys, preferred_element_type=jnp.float32)
            * inv_root
        )
        row_tiles = lax.dynamic_slice_in_dim(head_tiles, block_index * block_tiles, block_tiles, 1)
        visible = jnp.repeat(jnp.repeat(row_tiles, TILE, axis=1), TILE, axis=2) > 0
        scores = jnp.where(visible, scores, -jnp.inf)
        row_top = jnp.max(scores, axis=-1, keepdims=True)
        expo = jnp.exp(scores - row_top)
        return expo / jnp.sum(expo, axis=-1, keepdims=True)

    def attend(probs):
        return jnp.einsum(
            "hqk,khe->qhe", probs.astype(jnp.bfloat16), values, preferred_element_type=jnp.float32
        ).astype(jnp.bfloat16)

    query_blocks = queries.reshape(block_count, block_rows, heads_here, head_size)
    block_ids = jnp.arange(block_count, dtype=jnp.int32)

    def forward_plain(inputs):
        return attend(block_probs(inputs[0], inputs[1]))

    attended_blocks = lax.map(forward_plain, (query_blocks, block_ids))
    attended = attended_blocks.reshape(length, heads_here, head_size)
    cot_local = d_out[0]
    segment = lax.all_gather(cot_local, "seq", axis=0, tiled=True)
    weight_grad = jnp.einsum("lhe,ld->hed", attended, segment, preferred_element_type=jnp.float32)
    projected = jnp.einsum("ld,hed->lhe", segment, w_out, preferred_element_type=jnp.float32)
    cotangent = projected
    weight_grad, cotangent = (weight_grad, cotangent)
    head_cot = cotangent.astype(jnp.bfloat16)
    cot_blocks = head_cot.reshape(block_count, block_rows, heads_here, head_size)
    out_blocks = attended.reshape(block_count, block_rows, heads_here, head_size)

    def backward_plain(running, inputs):
        query_block, cot_block, out_block, block_index = inputs
        key_grad, value_grad = running
        probs = block_probs(query_block, block_index)
        probs_b = probs.astype(jnp.bfloat16)
        delta = jnp.sum(cot_block.astype(jnp.float32) * out_block.astype(jnp.float32), axis=-1)
        dprobs = jnp.einsum("qhe,khe->hqk", cot_block, values, preferred_element_type=jnp.float32)
        dscores = (probs * (dprobs - jnp.transpose(delta)[:, :, None])).astype(jnp.bfloat16)
        query_grad = (
            jnp.einsum("hqk,khe->qhe", dscores, keys, preferred_element_type=jnp.float32) * inv_root
        ).astype(jnp.bfloat16)
        key_grad = key_grad + jnp.einsum(
            "hqk,qhe->khe", dscores, query_block, preferred_element_type=jnp.float32
        )
        value_grad = value_grad + jnp.einsum(
            "hqk,qhe->khe", probs_b, cot_block, preferred_element_type=jnp.float32
        )
        return ((key_grad, value_grad), query_grad)

    start_pair = (
        jnp.zeros((length, heads_here, head_size), jnp.float32),
        jnp.zeros((length, heads_here, head_size), jnp.float32),
    )
    (key_grad, value_grad), query_grads = lax.scan(
        backward_plain, start_pair, (query_blocks, cot_blocks, out_blocks, block_ids)
    )
    head_grads = jnp.stack(
        [
            query_grads.reshape(length, heads_here, head_size),
            (key_grad * inv_root).astype(jnp.bfloat16),
            value_grad.astype(jnp.bfloat16),
        ]
    )[:, None]
    grad_qkv = lax.all_to_all(head_grads, "seq", split_axis=2, concat_axis=3, tiled=True)
    worker_mom = 0.9 * momentum + 0.1 * weight_grad
    worker_scale = jnp.mean(jnp.abs(worker_mom), axis=(1, 2), keepdims=True) + 1e-06
    sent = (worker_scale * jnp.tanh(worker_mom / worker_scale)).astype(jnp.bfloat16)
    worker_error = (worker_mom - sent.astype(jnp.float32))[None]
    received = lax.all_to_all(sent[None], "dp", split_axis=2, concat_axis=0, tiled=True)
    averaged = jnp.sum(received.astype(jnp.float32), axis=0) / worker_count
    server_scale = jnp.mean(jnp.abs(averaged), axis=(1, 2), keepdims=True) + 1e-06
    server_sent = (server_scale * jnp.tanh(averaged / server_scale)).astype(jnp.bfloat16)
    server_error = averaged - server_sent.astype(jnp.float32)
    synced_momentum = lax.all_gather(server_sent, "dp", axis=1, tiled=True)
    return (grad_qkv, synced_momentum, worker_error, server_error)


def solution(mesh):
    placed = (
        P(None, "dp", "seq", None, None),
        P(),
        P("dp", "seq", None),
        P("seq", None, None),
        P("seq", None, None),
    )
    return jax.shard_map(
        body,
        mesh=mesh,
        in_specs=placed,
        out_specs=(
            P(None, "dp", "seq", None, None),
            P("seq", None, None),
            P("dp", "seq", None, None),
            P("seq", "dp", None),
        ),
        check_vma=False,
    )
```

profile of v0, /device:TPU:9, one launch (start us, length us, event | category | flops | bytes accessed | tf_op | source)
XLA Modules:
  0.0 264.4 jit_solution(1458972170751866023)
XLA Ops:
  7.2 0.0 all-gather.6.cloned.1.call-start
  7.2 0.7 all-gather.6.cloned.1.call-update
  7.9 3.0 %copy.113 = bf16[3,1,128,16,128]{4,2,0,1,3:T(8,128)(2,1)} copy(bf16[3,1,128,16,128]{4,3,2,1,0:T(8,128)(2,1)} %param.9) | data formatting | bytes 3145728 | tf_op args[0]
  10.9 5.7 %all-to-all-start = ((bf16[3,1,128,16,128]{4,2,0,1,3:T(8,128)(2,1)}), bf16[3,1,128,16,128]{4,2,0,1,3:T(8,128)(2,1)S(1)}, u32[]{:S(2)}, u32[]{:S(2)}) async-start(bf16[3,1,128,16,128]{4,2,0,1,3:T(8,128)(2,1)} %copy.113), calls=%async_computation | async-start | bytes 3145728 | tf_op jit(solution)/shard_map/all_to_all | solution.py:24
  16.6 0.1 compare_convert_fusion
  16.7 0.1 multiply_reduce_fusion
  16.8 59.3 %all-to-all-done = bf16[3,1,128,16,128]{4,2,0,1,3:T(8,128)(2,1)S(1)} async-done(((bf16[3,1,128,16,128]{4,2,0,1,3:T(8,128)(2,1)}), bf16[3,1,128,16,128]{4,2,0,1,3:T(8,128)(2,1)S(1)}, u32[]{:S(2)}, u32[]{:S(2)}) %all-to-all-start) | async-done | bytes 1572896 | tf_op jit(solution)/shard_map/all_to_all | solution.py:24
  76.0 0.2 copy.114
  76.2 0.1 fusion.108
  76.4 0.9 copy.117
  77.3 0.8 copy.116
  78.1 28.9 %while.25 = (s32[]{:T(128)}, bf16[2,512,2,128]{3,1,2,0:T(8,128)(2,1)}, s32[2]{0:T(128)S(1)}, s32[2,8,8]{2,1,0:T(8,128)S(1)}, bf16[2,512,2,128]{3,1,2,0:T(8,128)(...) while((s32[]{:T(128)}, ...), condition=%wide.region_4.5_spmd, body=%wide.region_1.4_spmd.sunk | while | flops 814877760 | bytes 11822667 | solution.py:56
  78.1 0.6 dynamic_slice.93
  79.4 3.5 %broadcast_in_dim.86 = pred[2,512,8,128]{3,2,1,0:T(8,128)(4,1)S(1)} broadcast(pred[2,512,8]{2,1,0:T(8,128)(4,1)S(1)} %bitcast.177), dimensions={0,1,2} | broadcast | bytes 1056768 | tf_op jit(solution)/shard_map/while/body/eval_jaxpr/broadcast_in_dim | solution.py:39
  82.9 2.3 gt.32
  85.2 3.1 %fusion.149 = f32[2,512]{1,0:T(2,128)S(1)} fusion(pred[2,512,1024]{2,1,0:T(32,128)(4,1)} %gt.32, bf16[1024,2,128]{2,0,1:T(8,128)(2,1)} %get-tuple-element.477, bf16[2,512,2,128]{3,1,2,0:T(8,128)(2,1)S(1)} %get-tuple-element.476, s32[]{:T(128)} %get-tuple-element.461), kind=kOutput, calls=%fused_computation.94.clone.1 | convolution fusion | flops 272630784 | bytes 1839108 | tf_op jit(solution)/shard_map/while/body/eval_jaxpr/sub | solution.py:42
  88.2 4.3 %fusion.150 = bf16[2,512,2,128]{3,1,2,0:T(8,128)(2,1)} fusion(bf16[2,512,2,128]{3,1,2,0:T(8,128)(2,1)} %get-tuple-element.462, s32[]{:T(128)} %get-tuple-element.461, bf16[1024,2,128]{2,0,1:T(8,128)(2,1)} %get-tuple-element.478, f32[2,512]{1,0:T(2,128)S(1)} %fusion.149, pred[2,512,1024]{2,1,0:T(32,128)(4,1)S(1)} %copy-done.4, ...), kind=kOutput, calls=%fused_computation.10.clone.1 | convolution fusion | flops 542246912 | bytes 2626560 | tf_op jit(solution)/shard_map/while/body/eval_jaxpr/hqk,khe->qhe/dot_general | solution.py:46
  92.6 0.6 dynamic_slice.93
  93.9 3.5 %broadcast_in_dim.86 = pred[2,512,8,128]{3,2,1,0:T(8,128)(4,1)S(1)} broadcast(pred[2,512,8]{2,1,0:T(8,128)(4,1)S(1)} %bitcast.177), dimensions={0,1,2} | broadcast | bytes 1056768 | tf_op jit(solution)/shard_map/while/body/eval_jaxpr/broadcast_in_dim | solution.py:39
  97.3 2.3 gt.32
  99.6 3.1 %fusion.149 = f32[2,512]{1,0:T(2,128)S(1)} fusion(pred[2,512,1024]{2,1,0:T(32,128)(4,1)} %gt.32, bf16[1024,2,128]{2,0,1:T(8,128)(2,1)} %get-tuple-element.477, bf16[2,512,2,128]{3,1,2,0:T(8,128)(2,1)S(1)} %get-tuple-element.476, s32[]{:T(128)} %get-tuple-element.461), kind=kOutput, calls=%fused_computation.94.clone.1 | convolution fusion | flops 272630784 | bytes 1839108 | tf_op jit(solution)/shard_map/while/body/eval_jaxpr/sub | solution.py:42
  102.7 4.3 %fusion.150 = bf16[2,512,2,128]{3,1,2,0:T(8,128)(2,1)} fusion(bf16[2,512,2,128]{3,1,2,0:T(8,128)(2,1)} %get-tuple-element.462, s32[]{:T(128)} %get-tuple-element.461, bf16[1024,2,128]{2,0,1:T(8,128)(2,1)} %get-tuple-element.478, f32[2,512]{1,0:T(2,128)S(1)} %fusion.149, pred[2,512,1024]{2,1,0:T(32,128)(4,1)S(1)} %copy-done.4, ...), kind=kOutput, calls=%fused_computation.10.clone.1 | convolution fusion | flops 542246912 | bytes 2626560 | tf_op jit(solution)/shard_map/while/body/eval_jaxpr/hqk,khe->qhe/dot_general | solution.py:46
  107.0 1.1 copy.126
  108.1 27.4 %all-gather.6.cloned.1.call-done = bf16[1,1024,3072]{2,1,0:T(8,128)(2,1)} async-done(((bf16[1,128,3072]{2,1,0:T(8,128)(2,1)}), bf16[1,1024,3072]{2,1,0:T(8,128)(2,1)}) %all-gather.6.cloned.1.call-update) | async-done | bytes 6291472 | tf_op jit(solution)/shard_map/all_gather | solution.py:59
  135.5 6.3 %abs_reduce_fusion = (f32[2]{0:T(128)S(1)}, f32[2,128,3072]{2,1,0:T(8,128)S(1)}) fusion(bf16[1024,2,128]{2,0,1:T(8,128)(2,1)S(1)} %bitcast.182, bf16[1,1024,3072]{2,1,0:T(8,128)(2,1)} %all-gather.6.cloned.1.call-done, f32[2,128,3072]{2,1,0:T(8,128)} %param.13), kind=kOutput, calls=%fused_computation.76 | convolution fusion | flops 1614544896 | bytes 13107208 | tf_op jit(solution)/shard_map/lhe,ld->hed/dot_general | solution.py:60
  141.8 2.3 subtract_bitcast_fusion
  144.1 2.8 %copy.128 = bf16[1,2,128,3072]{3,1,0,2:T(2,128)(2,1)} copy(bf16[1,2,128,3072]{3,2,1,0:T(8,128)(2,1)S(1)} %get-tuple-element.330) | data formatting | bytes 3145728 | tf_op jit(solution)/shard_map/broadcast_in_dim | solution.py:106
  146.8 5.9 %all-to-all-start.2 = ((bf16[1,2,128,3072]{3,1,0,2:T(2,128)(2,1)}), bf16[1,2,128,3072]{3,1,0,2:T(2,128)(2,1)}, u32[]{:S(2)}, u32[]{:S(2)}) async-start(bf16[1,2,128,3072]{3,1,0,2:T(2,128)(2,1)} %copy.128), calls=%async_computation.2 | async-start | bytes 3145728 | tf_op jit(solution)/shard_map/all_to_all | solution.py:106
  152.7 4.8 %fusion.97 = bf16[1024,2,128]{2,0,1:T(8,128)(2,1)} fusion(bf16[2,128,3072]{2,1,0:T(8,128)(2,1)S(1)} %copy-done, bf16[1,1024,3072]{2,1,0:T(8,128)(2,1)} %all-gather.6.cloned.1.call-done), kind=kOutput, calls=%fused_computation.78 | convolution fusion | flops 1610874880 | bytes 8388608 | tf_op jit(solution)/shard_map/ld,hed->lhe/dot_general | solution.py:61
  157.5 47.2 %while.26 = (s32[]{:T(128)}, f32[1024,2,128]{0,2,1:T(8,128)}, f32[1024,2,128]{0,2,1:T(8,128)}, bf16[2,512,2,128]{3,1,0,2:T(8,128)(2,1)}, bf16[2,512,2,128]{3,1,2...) while((s32[]{:T(128)}, f32[1024,2,128]{0,2,1:T(8,128)}, ...), condition=%wide.region_9.10_spmd.clone, body=%wide.region_5.9_spmd.clone.sunk | while | flops 1626081280 | bytes 43031248 | solution.py:91
  157.5 0.6 dynamic_slice.102
  158.8 3.5 %broadcast_in_dim.90 = pred[2,512,8,128]{3,2,1,0:T(8,128)(4,1)S(1)} broadcast(pred[2,512,8]{2,1,0:T(8,128)(4,1)S(1)} %bitcast.178), dimensions={0,1,2} | broadcast | bytes 1056768 | tf_op jit(solution)/shard_map/while/body/eval_jaxpr/broadcast_in_dim | solution.py:39
  162.3 2.3 gt.34
  164.5 4.9 %fusion.164 = (f32[2,512]{1,0:T(2,128)S(1)}, f32[2,512,1024]{2,1,0:T(8,128)}) fusion(pred[2,512,1024]{2,1,0:T(32,128)(4,1)} %gt.34, bf16[1024,2,128]{2,0,1:T(8,128)(2,1)} %get-tuple-element.520, bf16[2,512,2,128]{3,1,2,0:T(8,128)(2,1)S(1)} %get-tuple-element.517, s32[]{:T(128)} %get-tuple-element.498), kind=kOutput, calls=%fused_computation.95.clone.1 | convolution fusion | flops 272630784 | bytes 6033412 | tf_op jit(solution)/shard_map/while/body/eval_jaxpr/sub | solution.py:42
  169.4 4.5 %fusion.166 = f32[1024,2,128]{0,2,1:T(8,128)} fusion(f32[2,512]{1,0:T(2,128)S(1)} %get-tuple-element.449, f32[1024,2,128]{0,2,1:T(8,128)} %get-tuple-element.500, pred[]{:T(512)S(6)} %compare.10, bf16[2,512,2,128]{3,1,0,2:T(8,128)(2,1)} %get-tuple-element.521, s32[]{:T(128)} %get-tuple-element.498, pred[2,512,1024]{2,1,0:T(32,128)(4,1)S(1)} %copy-done.3, ...), kind=kOutput, calls=%fused_computation.38.clone.1 | convolution fusion | flops 542640128 | bytes 4199425 | tf_op jit(solution)/shard_map/while/body/eval_jaxpr/hqk,qhe->khe/dot_general | solution.py:82
  174.0 1.2 fusion.163
  175.2 3.2 %multiply_convert_fusion.6 = bf16[2,512,1024]{2,1,0:T(8,128)(2,1)S(1)} fusion(bf16[1024,2,128]{2,0,1:T(8,128)(2,1)} %get-tuple-element.522, f32[2,512]{1,0:T(2,128)S(1)} %bitcast.188, f32[2,512,1024]{2,1,0:T(8,128)} %get-tuple-element.448, f32[2,512]{1,0:T(2,128)S(1)} %get-tuple-element.449, bf16[2,512,2,128]{3,1,0,2:T(8,128)(2,1)} %get-tuple-element.521, ...), kind=kOutput, calls=%fused_computation.26.clone.1 | convolution fusion | flops 272629760 | bytes 7086592 | tf_op jit(solution)/shard_map/while/body/eval_jaxpr/qhe,khe->hqk/dot_general | solution.py:74
  178.5 0.6 fusion.165
  179.2 0.4 copy-done.5
  179.5 1.4 fusion.167
  180.9 0.6 dynamic_slice.102
  182.2 3.5 %broadcast_in_dim.90 = pred[2,512,8,128]{3,2,1,0:T(8,128)(4,1)S(1)} broadcast(pred[2,512,8]{2,1,0:T(8,128)(4,1)S(1)} %bitcast.178), dimensions={0,1,2} | broadcast | bytes 1056768 | tf_op jit(solution)/shard_map/while/body/eval_jaxpr/broadcast_in_dim | solution.py:39
  185.7 2.3 gt.34
  188.0 4.9 %fusion.164 = (f32[2,512]{1,0:T(2,128)S(1)}, f32[2,512,1024]{2,1,0:T(8,128)}) fusion(pred[2,512,1024]{2,1,0:T(32,128)(4,1)} %gt.34, bf16[1024,2,128]{2,0,1:T(8,128)(2,1)} %get-tuple-element.520, bf16[2,512,2,128]{3,1,2,0:T(8,128)(2,1)S(1)} %get-tuple-element.517, s32[]{:T(128)} %get-tuple-element.498), kind=kOutput, calls=%fused_computation.95.clone.1 | convolution fusion | flops 272630784 | bytes 6033412 | tf_op jit(solution)/shard_map/while/body/eval_jaxpr/sub | solution.py:42
  192.9 4.9 %fusion.166 = f32[1024,2,128]{0,2,1:T(8,128)} fusion(f32[2,512]{1,0:T(2,128)S(1)} %get-tuple-element.449, f32[1024,2,128]{0,2,1:T(8,128)} %get-tuple-element.500, pred[]{:T(512)S(6)} %compare.10, bf16[2,512,2,128]{3,1,0,2:T(8,128)(2,1)} %get-tuple-element.521, s32[]{:T(128)} %get-tuple-element.498, pred[2,512,1024]{2,1,0:T(32,128)(4,1)S(1)} %copy-done.3, ...), kind=kOutput, calls=%fused_computation.38.clone.1 | convolution fusion | flops 542640128 | bytes 4199425 | tf_op jit(solution)/shard_map/while/body/eval_jaxpr/hqk,qhe->khe/dot_general | solution.py:82
  197.8 1.2 fusion.163
  199.0 3.2 %multiply_convert_fusion.6 = bf16[2,512,1024]{2,1,0:T(8,128)(2,1)S(1)} fusion(bf16[1024,2,128]{2,0,1:T(8,128)(2,1)} %get-tuple-element.522, f32[2,512]{1,0:T(2,128)S(1)} %bitcast.188, f32[2,512,1024]{2,1,0:T(8,128)} %get-tuple-element.448, f32[2,512]{1,0:T(2,128)S(1)} %get-tuple-element.449, bf16[2,512,2,128]{3,1,0,2:T(8,128)(2,1)} %get-tuple-element.521, ...), kind=kOutput, calls=%fused_computation.26.clone.1 | convolution fusion | flops 272629760 | bytes 7086592 | tf_op jit(solution)/shard_map/while/body/eval_jaxpr/qhe,khe->hqk/dot_general | solution.py:74
  202.3 0.6 fusion.165
  202.9 0.4 copy-done.5
  203.3 1.4 fusion.167
  204.7 1.5 copy.122
  206.3 1.5 copy.123
  207.8 0.1 fusion.100
  207.9 1.2 maximum_bitcast_fusion
  209.1 2.8 %copy.124 = bf16[3,1,1024,2,128]{4,3,0,1,2:T(2,128)(2,1)} copy(bf16[3,1,1024,2,128]{4,2,3,0,1:T(8,128)(2,1)S(1)} %maximum_bitcast_fusion) | data formatting | bytes 3145728 | tf_op jit(solution)/shard_map/broadcast_in_dim | solution.py:94
  211.9 5.2 %all-to-all-start.1 = ((bf16[3,1,1024,2,128]{4,3,0,1,2:T(2,128)(2,1)}), bf16[3,1,1024,2,128]{4,3,0,1,2:T(2,128)(2,1)S(1)}, u32[]{:S(2)}, u32[]{:S(2)}) async-start(bf16[3,1,1024,2,128]{4,3,0,1,2:T(2,128)(2,1)} %copy.124), calls=%async_computation.1 | async-start | bytes 3145728 | tf_op jit(solution)/shard_map/all_to_all | solution.py:101
  217.1 3.3 %convert_reduce_fusion = f32[2,32,3072]{2,0,1:T(2,128)S(1)} fusion(bf16[2,4,32,3072]{3,0,2,1:T(2,128)(2,1)} %bitcast.37), kind=kLoop, calls=%fused_computation.73 | loop fusion | flops 1376256 | bytes 2359296 | tf_op jit(solution)/shard_map/reduce_sum | solution.py:107
  220.4 0.9 abs_reduce_fusion.1
  221.3 1.7 convert_subtract_fusion
  223.0 0.0 all-gather.4.cloned.1.call-update
  223.1 2.3 copy.130
  225.3 27.1 %all-to-all-done.1 = bf16[3,1,1024,2,128]{4,3,0,1,2:T(2,128)(2,1)S(1)} async-done(((bf16[3,1,1024,2,128]{4,3,0,1,2:T(2,128)(2,1)}), bf16[3,1,1024,2,128]{4,3,0,1,2:T(2,128)(2,1)S(1)}, u32[]{:S(2)}, u32[]{:S(2)}) %all-to-all-start.1) | async-done | bytes 1572896 | tf_op jit(solution)/shard_map/all_to_all | solution.py:101
  252.4 2.2 copy.125
  254.7 2.9 %copy.129 = bf16[2,128,3072]{2,1,0:T(8,128)(2,1)} copy(bf16[2,128,3072]{2,0,1:T(2,128)(2,1)} %all-gather.4.cloned.1.call-done) | data formatting | bytes 3145728
  (44 shorter events, 0.4 us)
Async XLA Ops:
  7.2 145.5 %copy-start = (bf16[2,128,3072]{2,1,0:T(8,128)(2,1)S(1)}, bf16[2,128,3072]{2,1,0:T(8,128)(2,1)}, u32[]{:S(2)}) copy-start(bf16[2,128,3072]{2,1,0:T(8,128)(2,1)} %param.12) | copy-start | bytes 4718596
  7.2 128.3 %all-gather.6.cloned.1.call-start = ((), (), s32[]{:S(2)}) async-start(), calls=%async_computation.4 | async-start | bytes 7077888 | tf_op jit(solution)/shard_map/all_gather | solution.py:59
  7.9 8.8 %copy-start.6 = (s32[8,8,8]{2,1,0:T(8,128)S(1)}, s32[8,8,8]{2,1,0:T(8,128)}, u32[]{:S(2)}) copy-start(s32[8,8,8]{2,1,0:T(8,128)} %param.10) | copy-start | bytes 6148
  10.9 65.1 %all-to-all-start = ((bf16[3,1,128,16,128]{4,2,0,1,3:T(8,128)(2,1)}), bf16[3,1,128,16,128]{4,2,0,1,3:T(8,128)(2,1)S(1)}, u32[]{:S(2)}, u32[]{:S(2)}) async-start(bf16[3,1,128,16,128]{4,2,0,1,3:T(8,128)(2,1)} %copy.113), calls=%async_computation | async-start | bytes 3145728 | tf_op jit(solution)/shard_map/all_to_all | solution.py:24
  85.2 3.1 %copy-start.4 = (pred[2,512,1024]{2,1,0:T(32,128)(4,1)S(1)}, pred[2,512,1024]{2,1,0:T(32,128)(4,1)}, u32[]{:S(2)}) copy-start(pred[2,512,1024]{2,1,0:T(32,128)(4,1)} %gt.32) | copy-start | bytes 3145732 | tf_op jit(solution)/shard_map/while
  99.6 3.1 %copy-start.4 = (pred[2,512,1024]{2,1,0:T(32,128)(4,1)S(1)}, pred[2,512,1024]{2,1,0:T(32,128)(4,1)}, u32[]{:S(2)}) copy-start(pred[2,512,1024]{2,1,0:T(32,128)(4,1)} %gt.32) | copy-start | bytes 3145732 | tf_op jit(solution)/shard_map/while
  146.8 65.1 %all-to-all-start.2 = ((bf16[1,2,128,3072]{3,1,0,2:T(2,128)(2,1)}), bf16[1,2,128,3072]{3,1,0,2:T(2,128)(2,1)}, u32[]{:S(2)}, u32[]{:S(2)}) async-start(bf16[1,2,128,3072]{3,1,0,2:T(2,128)(2,1)} %copy.128), calls=%async_computation.2 | async-start | bytes 3145728 | tf_op jit(solution)/shard_map/all_to_all | solution.py:106
  164.5 4.9 %copy-start.3 = (pred[2,512,1024]{2,1,0:T(32,128)(4,1)S(1)}, pred[2,512,1024]{2,1,0:T(32,128)(4,1)}, u32[]{:S(2)}) copy-start(pred[2,512,1024]{2,1,0:T(32,128)(4,1)} %gt.34) | copy-start | bytes 3145732 | tf_op jit(solution)/shard_map/while
  175.2 3.3 %copy-start.1 = (f32[1024,2,128]{0,2,1:T(8,128)S(1)}, f32[1024,2,128]{0,2,1:T(8,128)}, u32[]{:S(2)}) copy-start(f32[1024,2,128]{0,2,1:T(8,128)} %get-tuple-element.499) | copy-start | bytes 3145732 | tf_op jit(solution)/shard_map/while
  178.5 1.0 copy-start.5
  179.1 1.8 copy-start.2
  188.0 4.9 %copy-start.3 = (pred[2,512,1024]{2,1,0:T(32,128)(4,1)S(1)}, pred[2,512,1024]{2,1,0:T(32,128)(4,1)}, u32[]{:S(2)}) copy-start(pred[2,512,1024]{2,1,0:T(32,128)(4,1)} %gt.34) | copy-start | bytes 3145732 | tf_op jit(solution)/shard_map/while
  199.0 3.3 %copy-start.1 = (f32[1024,2,128]{0,2,1:T(8,128)S(1)}, f32[1024,2,128]{0,2,1:T(8,128)}, u32[]{:S(2)}) copy-start(f32[1024,2,128]{0,2,1:T(8,128)} %get-tuple-element.499) | copy-start | bytes 3145732 | tf_op jit(solution)/shard_map/while
  202.3 1.0 copy-start.5
  202.9 1.8 copy-start.2
  211.9 40.5 %all-to-all-start.1 = ((bf16[3,1,1024,2,128]{4,3,0,1,2:T(2,128)(2,1)}), bf16[3,1,1024,2,128]{4,3,0,1,2:T(2,128)(2,1)S(1)}, u32[]{:S(2)}, u32[]{:S(2)}) async-start(bf16[3,1,1024,2,128]{4,3,0,1,2:T(2,128)(2,1)} %copy.124), calls=%async_computation.1 | async-start | bytes 3145728 | tf_op jit(solution)/shard_map/all_to_all | solution.py:101
  217.1 37.6 %all-gather.4.cloned.1.call-start = ((), (), s32[]{:S(2)}) async-start(), calls=%async_computation.3 | async-start | bytes 1966080 | tf_op jit(solution)/shard_map/all_gather | solution.py:111
Sparse Core Ops, SparseCore 0:
  10.2 125.2 all-gather.5
  223.2 21.0 all-gather.3
where the time goes:
time: 269 us; the launch traced here: 264 us
  waiting for transfers between devices  114 us (42%)
  matrix products  55.7 us (21%)
  local copies, waits for them, and re-layouts  48.2 us (18%)
  starting transfers between devices  16.8 us (6%)
  between operations  14.1 us (5%)
  other arithmetic  12.3 us (5%)
  loops' own time  2.85 us (1%)
    all_to_all x1, waiting for transfers between devices, body(): local = lax.all_to_all(qkv, 'seq', split_axis=3, concat_axis=2, tiled=True)  59.3 us
    all_gather x1, waiting for transfers between devices, body(): segment = lax.all_gather(cot_local, 'seq', axis=0, tiled=True)  27.4 us
    all_to_all x1, waiting for transfers between devices, body(): lax.all_to_all(head_grads, 'seq', split_axis=2, concat_axis=3, tiled=True)  27.1 us
    sub x4, matrix products, block_probs(): expo = jnp.exp(scores - row_top)  15.9 us
    broadcast_in_dim x8, local copies, waits for them, and re-layouts, block_probs(): visible = jnp.repeat(jnp.repeat(row_tiles, TILE, axis=1), TILE, axis=2) > 0  14 us
    dot_general x2, matrix products, backward_plain(): jnp.einsum('hqk,qhe->khe', probs_b, cot_block, preferred_element_type=jnp...  9.41 us
    gt x4, local copies, waits for them, and re-layouts, block_probs(): visible = jnp.repeat(jnp.repeat(row_tiles, TILE, axis=1), TILE, axis=2) > 0  9.06 us
    dot_general x2, matrix products, attend(): jnp.einsum('hqk,khe->qhe', probs.astype(jnp.bfloat16), values, preferred_...  8.67 us
  transfers between devices with their start and end apart: 5, of which 3 were waited for; matrix products, arithmetic and copies ran while one was open for 38% of the time, Pallas kernels for 0%

commit v1 on v0

v1 whole, which is shorter than its diff:
```python
import functools
import math

import jax
import jax.numpy as jnp
from jax import lax
from jax.experimental import pallas as pl
from jax.experimental.pallas import tpu as pltpu
from jax.sharding import PartitionSpec as P

VMEM_LIMIT = 44 * 1024 * 1024
F32 = jnp.float32
BF16 = jnp.bfloat16


def params():
    return pltpu.CompilerParams(vmem_limit_bytes=VMEM_LIMIT)


def cost(flops, moved):
    return pl.CostEstimate(flops=flops, bytes_accessed=moved, transcendentals=0)


def ring_order(n):
    return [i for i in range(n) if i % 2 == 0] + [i for i in reversed(range(n)) if i % 2]


def ring_member(place, n):
    return jnp.where(place < n // 2, 2 * place, 2 * n - 1 - 2 * place)


def ring_place(member, n):
    return jnp.where(member % 2 == 0, member // 2, (2 * n - 1 - member) // 2)


def dot_nt(a, b):
    return lax.dot_general(a, b, (((1,), (1,)), ((), ())), preferred_element_type=F32)


def dot_tn(a, b):
    return lax.dot_general(a, b, (((0,), (0,)), ((), ())), preferred_element_type=F32)


def pack_kernel(n, x_ref, *refs):
    outs, parts = refs[:n], refs[n]
    me = lax.axis_index("seq")
    rows, heads, size = x_ref.shape
    wide = heads * size // n
    x = x_ref[...].reshape(rows, heads * size)
    for d in range(n):
        parts[d] = x[:, d * wide : (d + 1) * wide]
    for k in range(n):
        outs[k][...] = parts[me ^ k]


def unpack_kernel(n, *refs):
    blocks, out_ref, parts = refs[:n], refs[n], refs[n + 1]
    me = lax.axis_index("seq")
    for k in range(n):
        parts[me ^ k] = blocks[k][...]
    out_ref[...] = jnp.concatenate([parts[d] for d in range(n)], axis=1).reshape(out_ref.shape)


def attend_kernel(n, heads_here, per_group, groups, offsets, pieces, first, last, *refs):
    refs = list(refs)
    count = len(offsets)
    take = lambda m: [refs.pop(0) for _ in range(m)]
    (mask_ref,) = take(1)
    tiles = [take(pieces) for _ in range(count)]
    (w_ref,) = take(1)
    blocks = take(n)
    if not first:
        key_in, value_in = take(2)
    if not first and not last:
        (weight_in,) = take(1)
    if last:
        query_parts = take(2)
        outs = take(n)
        (att_ref,) = take(1)
    else:
        query_out, key_out, value_out, weight_out = take(4)
    q_all, k_all, v_all, cot_all, att_all, tile_ids = take(6)
    if last:
        key_out, value_out, grads, query_out = take(4)

    me = lax.axis_index("seq")
    tokens = blocks[0].shape[0] // 3
    wide = blocks[0].shape[1]
    size = wide // heads_here
    inv_root = 1.0 / math.sqrt(size)
    place = ring_place(me, n)
    for i, offset in enumerate(offsets):
        tile_ids[i] = ring_member(lax.rem(place + offset + n, n), n)
    for k in range(n):
        rows = slice(k * tokens, (k + 1) * tokens)
        q_all[k] = blocks[k][0:tokens]
        k_all[rows] = blocks[k][tokens : 2 * tokens]
        v_all[rows] = blocks[k][2 * tokens : 3 * tokens]
    for i in range(count):
        part = tokens // pieces
        for j in range(pieces):
            cot_all[i, j * part : (j + 1) * part] = dot_nt(tiles[i][j][...], w_ref[...]).astype(BF16)
    if first:
        key_out[...] = jnp.zeros_like(key_out)
        value_out[...] = jnp.zeros_like(value_out)
    else:
        key_out[...] = key_in[...]
        value_out[...] = value_in[...]

    def one_tile(i, carry):
        tile = tile_ids[i]
        slot = tile ^ me
        for h in range(heads_here):
            cols = slice(h * size, (h + 1) * size)
            group = (me * heads_here + h) // per_group
            base = (group * n + tile) * n
            bias = jnp.concatenate(
                [
                    jnp.full(
                        (1, tokens), jnp.where(mask_ref[base + (me ^ k)] == 1, 0.0, -jnp.inf), F32
                    )
                    for k in range(n)
                ],
                axis=1,
            )
            query = q_all[slot, :, cols]
            keys = k_all[:, cols]
            values = v_all[:, cols]
            cot = cot_all[i, :, cols]
            scores = dot_nt(query, keys) * inv_root + bias
            expo = jnp.exp(scores - jnp.max(scores, axis=1, keepdims=True))
            probs = expo * (1.0 / jnp.sum(expo, axis=1, keepdims=True))
            probs_b = probs.astype(BF16)
            att = jnp.dot(probs_b, values, preferred_element_type=F32).astype(BF16)
            att_all[i, :, cols] = att
            delta = jnp.sum(cot.astype(F32) * att.astype(F32), axis=1, keepdims=True)
            dprobs = dot_nt(cot, values)
            dscores = (probs * (dprobs - delta)).astype(BF16)
            query_out[i, :, cols] = (
                jnp.dot(dscores, keys, preferred_element_type=F32) * inv_root
            ).astype(BF16)
            key_out[:, cols] += dot_tn(dscores, query)
            value_out[:, cols] += dot_tn(probs_b, cot)
        return carry

    if count == 1:
        one_tile(0, 0)
    else:
        lax.fori_loop(0, count, one_tile, 0)

    if last:
        att_ref[...] = att_all[0]
        for part, listed in zip(query_parts, LISTED(n)):
            for i, offset in enumerate(listed):
                tile = ring_member(lax.rem(place + offset + n, n), n)
                grads[tile ^ me, 0:tokens] = part[i]
        grads[tile_ids[0] ^ me, 0:tokens] = query_out[0]
        for k in range(n):
            rows = slice(k * tokens, (k + 1) * tokens)
            outs[k][0:tokens] = grads[k, 0:tokens]
            outs[k][tokens : 2 * tokens] = (key_out[rows] * inv_root).astype(BF16)
            outs[k][2 * tokens : 3 * tokens] = value_out[rows].astype(BF16)
    else:
        wide_d = w_ref.shape[1]
        chunk = math.gcd(wide_d, 512)
        for c in range(0, wide_d, chunk):
            cols = slice(c, c + chunk)
            total = None if first else weight_in[:, cols]
            for i in range(count):
                term = dot_tn(att_all[i], tiles[i][0][:, cols])
                total = term if total is None else total + term
            weight_out[:, cols] = total


def LISTED(n):
    half = n // 2
    early = [0] + [o for s in range(1, half - 1) for o in (-s, s)]
    return early, [-(half - 1), half - 1]


def worker_kernel(heads_here, workers, mom_ref, weight_ref, att_ref, *refs):
    pieces, error_ref, outs, sent_ref = refs[:-workers - 2], refs[-workers - 2], refs[-workers - 1 : -1], refs[-1]
    me = lax.axis_index("dp")
    tokens, wide = att_ref.shape
    size = wide // heads_here
    wide_d = mom_ref.shape[1]
    chunk = math.gcd(wide_d, 512)
    part = tokens // len(pieces)
    totals = [jnp.zeros((size, chunk), F32) for _ in range(heads_here)]
    for c in range(0, wide_d, chunk):
        cols = slice(c, c + chunk)
        tile = jnp.concatenate([p[:, cols] for p in pieces], axis=0)
        grad = weight_ref[:, cols] + dot_tn(att_ref[...], tile)
        mom = 0.9 * mom_ref[:, cols] + 0.1 * grad
        error_ref[:, cols] = mom
        for h in range(heads_here):
            totals[h] = totals[h] + jnp.abs(mom[h * size : (h + 1) * size])
    for h in range(heads_here):
        rows = slice(h * size, (h + 1) * size)
        scale = jnp.sum(totals[h], keepdims=True) * (1.0 / (size * wide_d)) + 1e-06
        inverse = 1.0 / scale
        for c in range(0, wide_d, chunk):
            cols = slice(c, c + chunk)
            mom = error_ref[rows, cols]
            sent = (scale * jnp.tanh(mom * inverse)).astype(BF16)
            sent_ref[h, :, cols] = sent
            error_ref[rows, cols] = mom - sent.astype(F32)
    block = size // workers
    for k in range(workers):
        start = pl.multiple_of((me ^ k) * block, block)
        outs[k][...] = sent_ref[:, pl.ds(start, block), :]


def server_kernel(workers, *refs):
    blocks, synced_ref, error_ref = refs[:workers], refs[workers], refs[workers + 1]
    heads_here, block, wide_d = synced_ref.shape
    for h in range(heads_here):
        total = blocks[0][h].astype(F32)
        for k in range(1, workers):
            total = total + blocks[k][h].astype(F32)
        averaged = total * (1.0 / workers)
        scale = jnp.sum(jnp.abs(averaged), keepdims=True) * (1.0 / (block * wide_d)) + 1e-06
        synced = (scale * jnp.tanh(averaged * (1.0 / scale))).astype(BF16)
        synced_ref[h] = synced
        error_ref[h] = averaged - synced.astype(F32)


def join_kernel(workers, *refs):
    blocks, out_ref = refs[:workers], refs[workers]
    me = lax.axis_index("dp")
    block = blocks[0].shape[1]
    for k in range(workers):
        start = pl.multiple_of((me ^ k) * block, block)
        out_ref[:, pl.ds(start, block), :] = blocks[k][...]


def body(qkv, tile_mask, d_out, w_out, momentum):
    n = lax.axis_size("seq")
    workers = lax.axis_size("dp")
    tokens, heads, size = qkv.shape[2:]
    heads_here = w_out.shape[0]
    groups = tile_mask.shape[0]
    per_group = heads // groups
    wide = heads_here * size
    wide_d = d_out.shape[2]
    half = n // 2
    shape = jax.ShapeDtypeStruct

    ring = ring_order(n)
    ahead = [(ring[i], ring[(i + 1) % n]) for i in range(n)]
    back = [(b, a) for a, b in ahead]
    own = d_out[0]
    fore, aft = [own], [own]
    for s in range(1, half):
        fore.append(lax.ppermute(fore[-1], "seq", ahead))
        aft.append(lax.ppermute(aft[-1], "seq", back))
    far = [
        lax.ppermute(fore[-1][: tokens // 2], "seq", ahead),
        lax.ppermute(aft[-1][tokens // 2 :], "seq", back),
    ]

    packed = pl.pallas_call(
        functools.partial(pack_kernel, n),
        out_shape=[shape((3 * tokens, wide), BF16)] * n,
        scratch_shapes=[pltpu.VMEM((n, 3 * tokens, wide), BF16)],
        compiler_params=params(),
        cost_estimate=cost(0, 4 * qkv.size),
        name="pack",
    )(qkv.reshape(3 * tokens, heads, size))

    def swap(blocks, axis):
        return [blocks[0]] + [
            lax.ppermute(blocks[k], axis, [(i, i ^ k) for i in range(len(blocks))])
            for k in range(1, len(blocks))
        ]

    blocks = swap(packed, "seq")
    mask = tile_mask.reshape(-1)
    w_flat = w_out.reshape(wide, wide_d)
    early, late = LISTED(n)
    vmem = pl.BlockSpec(memory_space=pltpu.VMEM)
    smem = pl.BlockSpec(memory_space=pltpu.SMEM)
    length = n * tokens

    def attend(offsets, tiles, carried, last=False, parts=()):
        count, pieces = len(offsets), len(tiles[0])
        first = not carried
        pair = [shape((length, wide), F32)] * 2
        operands = [mask, *[p for t in tiles for p in t], w_flat, *blocks, *carried, *parts]
        if last:
            outs = [shape((3 * tokens, wide), BF16)] * n + [shape((tokens, wide), BF16)]
        else:
            outs = [shape((count, tokens, wide), BF16), *pair, shape((wide, wide_d), F32)]
        scratch = [
            pltpu.VMEM((n, tokens, wide), BF16),
            pltpu.VMEM((length, wide), BF16),
            pltpu.VMEM((length, wide), BF16),
            pltpu.VMEM((count, tokens, wide), BF16),
            pltpu.VMEM((count, tokens, wide), BF16),
            pltpu.SMEM((count,), jnp.int32),
        ]
        if last:
            scratch += [
                pltpu.VMEM((length, wide), F32),
                pltpu.VMEM((length, wide), F32),
                pltpu.VMEM((n, tokens, wide), BF16),
                pltpu.VMEM((1, tokens, wide), BF16),
            ]
        flops = count * (14 * tokens * length * wide + 4 * tokens * wide * wide_d)
        return pl.pallas_call(
            functools.partial(
                attend_kernel, n, heads_here, per_group, groups, offsets, pieces, first, last
            ),
            in_specs=[smem] + [vmem] * (len(operands) - 1),
            out_shape=outs,
            scratch_shapes=scratch,
            compiler_params=params(),
            cost_estimate=cost(flops, 2**23),
            name="attend",
        )(*operands)

    by_offset = {0: own}
    for s in range(1, half):
        by_offset[-s], by_offset[s] = fore[s], aft[s]
    query_a, key_a, value_a, weight_a = attend(early, [[by_offset[o]] for o in early], [])
    query_b, key_b, value_b, weight_b = attend(
        late, [[by_offset[o]] for o in late], [key_a, value_a, weight_a]
    )
    *grads, att = attend([half], [far], [key_b, value_b], True, [query_a, query_b])
    returned = swap(grads, "seq")

    error, *sent = pl.pallas_call(
        functools.partial(worker_kernel, heads_here, workers),
        out_shape=[shape((wide, wide_d), F32)]
        + [shape((heads_here, size // workers, wide_d), BF16)] * workers,
        scratch_shapes=[pltpu.VMEM((heads_here, size, wide_d), BF16)],
        compiler_params=params(),
        cost_estimate=cost(2 * tokens * wide * wide_d, 2**24),
        name="worker",
    )(momentum.reshape(wide, wide_d), weight_b, att, *far)
    received = swap(sent, "dp")

    synced, server_error = pl.pallas_call(
        functools.partial(server_kernel, workers),
        out_shape=[
            shape((heads_here, size // workers, wide_d), BF16),
            shape((heads_here, size // workers, wide_d), F32),
        ],
        compiler_params=params(),
        cost_estimate=cost(0, 2**22),
        name="server",
    )(*received)
    gathered = [synced] + [None] * (workers - 1)
    for k in range(1, workers):
        source, step = (synced, k) if k == 1 or k % 2 == 0 else (gathered[k - 1], 1)
        gathered[k] = lax.ppermute(source, "dp", [(i, i ^ step) for i in range(workers)])

    grad_rows = pl.pallas_call(
        functools.partial(unpack_kernel, n),
        out_shape=shape((3 * tokens, heads, size), BF16),
        scratch_shapes=[pltpu.VMEM((n, 3 * tokens, wide), BF16)],
        compiler_params=params(),
        cost_estimate=cost(0, 4 * qkv.size),
        name="unpack",
    )(*returned)
    synced_momentum = pl.pallas_call(
        functools.partial(join_kernel, workers),
        out_shape=shape((heads_here, size, wide_d), BF16),
        compiler_params=params(),
        cost_estimate=cost(0, 4 * w_out.size),
        name="join",
    )(*gathered)
    return (
        grad_rows.reshape(qkv.shape),
        synced_momentum,
        error.reshape(1, heads_here, size, wide_d),
        server_error,
    )


def solution(mesh):
    placed = (
        P(None, "dp", "seq", None, None),
        P(),
        P("dp", "seq", None),
        P("seq", None, None),
        P("seq", None, None),
    )
    return jax.shard_map(
        body,
        mesh=mesh,
        in_specs=placed,
        out_specs=(
            P(None, "dp", "seq", None, None),
            P("seq", None, None),
            P("dp", "seq", None, None),
            P("seq", "dp", None),
        ),
        check_vma=False,
    )
```

time: 269 us -> 206 us (0.77); the launches traced: 264 us -> 206 us
  matrix products: 55.7 us -> 0 us
  Pallas kernels: 0 us -> 41.5 us
  local copies, waits for them, and re-layouts: 48.2 us -> 11.5 us
  starting transfers between devices: 16.8 us -> 33.9 us
  between operations: 14.1 us -> 0.78 us
  other arithmetic: 12.3 us -> 0 us
  waiting for transfers between devices: 114 us -> 118 us
  loops' own time: 2.85 us -> 0 us
    ppermute x0 -> x28, waiting for transfers between devices: none -> 118 us  [the longest x17 84.9 us: swap(): lax.ppermute(blocks[k], axis, [(i, i ^ k) for i in range(len(blocks))])]
    all_to_all x3 -> x0, waiting for transfers between devices: 86.4 us -> none  [the longest x1 59.3 us: body(): local = lax.all_to_all(qkv, 'seq', split_axis=3, concat_axis=2, tiled=True)]
    pallas_call x0 -> x8, Pallas kernels: none -> 41.5 us  [the longest x3 31.8 us: attend(): pl.pallas_call(functools.partial(attend_kernel, n, heads_here, per_group,...]
    dot_general x12 -> x0, matrix products: 39.8 us -> none  [the longest x2 9.41 us: backward_plain(): jnp.einsum('hqk,qhe->khe', probs_b, cot_block, preferred_element_type=jnp...]
    ppermute x0 -> x28, starting transfers between devices: none -> 33.9 us  [the longest x17 26 us: swap(): lax.ppermute(blocks[k], axis, [(i, i ^ k) for i in range(len(blocks))])]
    all_gather x2 -> x0, waiting for transfers between devices: 27.4 us -> none  [the longest x1 27.4 us: body(): segment = lax.all_gather(cot_local, 'seq', axis=0, tiled=True)]
    broadcast_in_dim x10 -> x0, local copies, waits for them, and re-layouts: 19.5 us -> none  [the longest x8 14 us: block_probs(): visible = jnp.repeat(jnp.repeat(row_tiles, TILE, axis=1), TILE, axis=2) > 0]
    all_to_all x3 -> x0, starting transfers between devices: 16.8 us -> none  [the longest x1 5.85 us: body(): lax.all_to_all(sent[None], 'dp', split_axis=2, concat_axis=0, tiled=True)]
  transfers between devices with their start and end apart: 5 -> 28, of which waited for: 3 -> 17; matrix products, arithmetic and copies ran while one was open for 38% -> 0% of each run, Pallas kernels for 0% -> 15%
where the time goes in v1:
time: 206 us
  waiting for transfers between devices  118 us (57%)
  Pallas kernels  41.5 us (20%)
  starting transfers between devices  33.9 us (16%)
  local copies, waits for them, and re-layouts  11.5 us (6%)
    ppermute x17, waiting for transfers between devices, swap(): lax.ppermute(blocks[k], axis, [(i, i ^ k) for i in range(len(blocks))])  84.9 us
    pallas_call x3, Pallas kernels, attend(): pl.pallas_call(functools.partial(attend_kernel, n, heads_here, per_group,...  31.8 us
    ppermute x3, waiting for transfers between devices, body(): fore.append(lax.ppermute(fore[-1], 'seq', ahead))  31.4 us
    ppermute x17, starting transfers between devices, swap(): lax.ppermute(blocks[k], axis, [(i, i ^ k) for i in range(len(blocks))])  26 us
    unnamed x30, local copies, waits for them, and re-layouts  10.6 us
  transfers between devices with their start and end apart: 28, of which 17 were waited for; matrix products, arithmetic and copies ran while one was open for 0% of the time, Pallas kernels for 15%

profile of v1, /device:TPU:9, one launch (start us, length us, event | category | flops | bytes accessed | tf_op | source)
XLA Modules:
  0.0 205.5 jit_solution(466710195414681920)
XLA Ops:
  0.6 1.3 collective-permute-start
  2.0 0.2 collective-permute-start.4
  2.2 17.2 %collective-permute-done.refs_2_ = bf16[128,3072]{1,0:T(8,128)(2,1)S(1)} collective-permute-done((bf16[128,3072]{1,0:T(8,128)(2,1)}, bf16[128,3072]{1,0:T(8,128)(2,1)S(1)}, u32[]{:S(2)}, u32[]{:S(2)}) %collective-permute-start) | collective-permute-done | bytes 786464 | tf_op jit(solution)/shard_map/ppermute | solution.py:255
  19.3 1.3 collective-permute-start.1
  20.6 0.9 copy-done.7
  21.5 0.2 collective-permute-start.5
  21.7 0.9 copy-done.9
  22.5 14.3 %collective-permute-done.1.refs_4_ = bf16[128,3072]{1,0:T(8,128)(2,1)S(1)} collective-permute-done((bf16[128,3072]{1,0:T(8,128)(2,1)S(1)}, bf16[128,3072]{1,0:T(8,128)(2,1)S(1)}, u32[]{:S(2)}, u32[]{:S(2)}) %collective-permute-start.1) | collective-permute-done | bytes 786464 | tf_op jit(solution)/shard_map/ppermute | solution.py:255
  36.8 1.3 collective-permute-start.2
  38.1 0.6 collective-permute-done.5.refs_5_
  38.7 0.2 collective-permute-start.6
  38.9 1.5 copy-done.3
  40.4 1.4 pack.1
  41.8 1.0 collective-permute-start.10
  42.8 2.3 %collective-permute-start.11 = (bf16[384,256]{1,0:T(8,128)(2,1)S(1)}, bf16[384,256]{1,0:T(8,128)(2,1)S(1)}, u32[]{:S(2)}, u32[]{:S(2)}) collective-permute-start(bf16[384,256]{1,0:T(8,128)(2,1)S(1)} %get-tuple-element.40), channel_id=1, source_target_pairs={{0,4},{1,5},{2,6},{3,7},{4,0},{5,1},{6,2},{7,3},{8,12},{9,13},{10,... | collective-permute-start | bytes 589832 | tf_op jit(solution)/shard_map/ppermute | solution.py:273
  45.1 0.4 collective-permute-start.12
  45.5 14.2 %collective-permute-done.10.refs_10_.refs_7_ = bf16[384,256]{1,0:T(8,128)(2,1)S(1)} collective-permute-done((bf16[384,256]{1,0:T(8,128)(2,1)S(1)}, bf16[384,256]{1,0:T(8,128)(2,1)S(1)}, u32[]{:S(2)}, u32[]{:S(2)}) %collective-permute-start.10) | collective-permute-done | bytes 196640 | tf_op jit(solution)/shard_map/ppermute | solution.py:273
  59.7 0.8 collective-permute-start.13
  60.5 3.9 %collective-permute-done.11.refs_11_.refs_8_ = bf16[384,256]{1,0:T(8,128)(2,1)S(1)} collective-permute-done((bf16[384,256]{1,0:T(8,128)(2,1)S(1)}, bf16[384,256]{1,0:T(8,128)(2,1)S(1)}, u32[]{:S(2)}, u32[]{:S(2)}) %collective-permute-start.11) | collective-permute-done | bytes 196640 | tf_op jit(solution)/shard_map/ppermute | solution.py:273
  64.4 0.7 copy-done.4
  65.1 0.0 collective-permute-start.14
  65.1 0.0 collective-permute-done.2.refs_1_
  65.2 2.1 %collective-permute-start.9 = (bf16[384,256]{1,0:T(8,128)(2,1)}, bf16[384,256]{1,0:T(8,128)(2,1)}, u32[]{:S(2)}, u32[]{:S(2)}) collective-permute-start(bf16[384,256]{1,0:T(8,128)(2,1)} %get-tuple-element.38), channel_id=1, source_target_pairs={{0,2},{1,3},{2,0},{3,1},{4,6},{5,7},{6,4},{7,5},{8,10},{9,11},{10,... | collective-permute-start | bytes 589832 | tf_op jit(solution)/shard_map/ppermute | solution.py:273
  67.3 0.8 reshape.26.refs_0_
  68.2 7.2 %collective-permute-done.12.refs_12_.refs_9_ = bf16[384,256]{1,0:T(8,128)(2,1)} collective-permute-done((bf16[384,256]{1,0:T(8,128)(2,1)}, bf16[384,256]{1,0:T(8,128)(2,1)}, u32[]{:S(2)}, u32[]{:S(2)}) %collective-permute-start.12) | collective-permute-done | bytes 196640 | tf_op jit(solution)/shard_map/ppermute | solution.py:273
  75.4 0.0 collective-permute-start.3
  75.4 6.8 %collective-permute-done.13.refs_13_.refs_10_ = bf16[384,256]{1,0:T(8,128)(2,1)} collective-permute-done((bf16[384,256]{1,0:T(8,128)(2,1)}, bf16[384,256]{1,0:T(8,128)(2,1)}, u32[]{:S(2)}, u32[]{:S(2)}) %collective-permute-start.13) | collective-permute-done | bytes 196640 | tf_op jit(solution)/shard_map/ppermute | solution.py:273
  82.2 3.6 %collective-permute-done.14.refs_14_.refs_11_ = bf16[384,256]{1,0:T(8,128)(2,1)} collective-permute-done((bf16[384,256]{1,0:T(8,128)(2,1)}, bf16[384,256]{1,0:T(8,128)(2,1)}, u32[]{:S(2)}, u32[]{:S(2)}) %collective-permute-start.14) | collective-permute-done | bytes 196640 | tf_op jit(solution)/shard_map/ppermute | solution.py:273
  85.8 0.9 copy-done.5
  86.7 1.1 copy-done.6
  87.8 1.1 copy-done.8
  89.0 1.1 copy-done.10
  90.1 1.1 copy-done.12
  91.2 1.1 copy-done.14
  92.4 17.4 %attend.3 = (bf16[5,128,256]{2,1,0:T(8,128)(2,1)S(1)}, f32[1024,256]{1,0:T(8,128)S(1)}, f32[1024,256]{1,0:T(8,128)S(1)}, f32[256,3072]{1,0:T(8,128)}) custom-call(s32[512]{0:T(512)S(1)} %reshape.26.refs_0_, bf16[128,3072]{1,0:T(8,128)(2,1)S(1)} %bitcast.15, bf16[128,3072]{1,0:T(8,128)(2,1)S(1)} %copy-done.8, bf16[128,3072]{1,0:T(8,128)(2,1)S(1)} %copy-done.10, ...), custom_call_target="tpu_custom_call" | custom-call | flops 4362076160 | bytes 8388608 | tf_op jit(solution)/shard_map/attend/pallas_call | solution.py:310
  109.8 10.0 %attend.4 = (bf16[2,128,256]{2,1,0:T(8,128)(2,1)S(1)}, f32[1024,256]{1,0:T(8,128)S(1)}, f32[1024,256]{1,0:T(8,128)S(1)}, f32[256,3072]{1,0:T(8,128)}) custom-call(s32[512]{0:T(512)S(1)} %reshape.26.refs_0_, bf16[128,3072]{1,0:T(8,128)(2,1)S(1)} %collective-permute-done.2.refs_1_, bf16[128,3072]{1,0:T(8,128)(2,1)S(1)} %collective-permute-done.6.refs_2_, ...), custom_call_target="tpu_custom_call" | custom-call | flops 1744830464 | bytes 8388608 | tf_op jit(solution)/shard_map/attend/pallas_call | solution.py:310
  119.8 0.0 collective-permute-done.3.refs_1_.refs_0_
  119.8 0.0 copy-start.1
  119.8 4.3 %attend.5 = (bf16[384,256]{1,0:T(8,128)(2,1)S(1)}, bf16[384,256]{1,0:T(8,128)(2,1)S(1)}, bf16[384,256]{1,0:T(8,128)(2,1)S(1)}, bf16[384,256]{1,0:T(8,128)(2,1)S(...) custom-call(s32[512]{0:T(512)S(1)} %reshape.26.refs_0_, ...), custom_call_target="tpu_custom_call" | custom-call | flops 872415232 | bytes 8388608 | tf_op jit(solution)/shard_map/attend/pallas_call | solution.py:310
  124.2 3.8 %worker.1 = (f32[256,3072]{1,0:T(8,128)}, bf16[2,32,3072]{2,1,0:T(8,128)(2,1)S(1)}, bf16[2,32,3072]{2,1,0:T(8,128)(2,1)S(1)}, bf16[2,32,3072]{2,1,0:T(8,128)(2,1)S(1)}, bf16[2,32,3072]{2,1,0:T(8,128)(2,1)S(1)}) custom-call(f32[256,3072]{1,0:T(8,128)S(1)} %bitcast.11, f32[256,3072]{1,0:T(8,128)S(1)} %copy-done.2, ...), custom_call_target="tpu_custom_call" | custom-call | flops 201326592 | bytes 16777216 | tf_op jit(solution)/shard_map/worker/pallas_call | solution.py:332
  128.0 8.8 %collective-permute-start.22 = (bf16[2,32,3072]{2,1,0:T(8,128)(2,1)S(1)}, bf16[2,32,3072]{2,1,0:T(8,128)(2,1)S(1)}, u32[]{:S(2)}, u32[]{:S(2)}) collective-permute-start(bf16[2,32,3072]{2,1,0:T(8,128)(2,1)S(1)} %get-tuple-element.62), channel_id=1, source_target_pairs={{0,8},{8,0},{16,24},{24,16},{1,9},{9,1},{17,25},{25,17},{2,10},{10... | collective-permute-start | bytes 1179656 | tf_op jit(solution)/shard_map/ppermute | solution.py:273
  136.8 1.2 collective-permute-start.23
  138.0 0.4 collective-permute-start.24
  138.4 9.1 %collective-permute-done.23.refs_2_ = bf16[2,32,3072]{2,1,0:T(8,128)(2,1)S(1)} collective-permute-done((bf16[2,32,3072]{2,1,0:T(8,128)(2,1)S(1)}, bf16[2,32,3072]{2,1,0:T(8,128)(2,1)S(1)}, u32[]{:S(2)}, u32[]{:S(2)}) %collective-permute-start.23) | collective-permute-done | bytes 393248 | tf_op jit(solution)/shard_map/ppermute | solution.py:273
  147.5 8.5 %collective-permute-done.24.refs_3_ = bf16[2,32,3072]{2,1,0:T(8,128)(2,1)S(1)} collective-permute-done((bf16[2,32,3072]{2,1,0:T(8,128)(2,1)S(1)}, bf16[2,32,3072]{2,1,0:T(8,128)(2,1)S(1)}, u32[]{:S(2)}, u32[]{:S(2)}) %collective-permute-start.24) | collective-permute-done | bytes 393248 | tf_op jit(solution)/shard_map/ppermute | solution.py:273
  156.1 1.5 server.1
  157.5 1.2 collective-permute-start.26
  158.7 2.4 %collective-permute-start.15 = (bf16[384,256]{1,0:T(8,128)(2,1)S(1)}, bf16[384,256]{1,0:T(8,128)(2,1)S(1)}, u32[]{:S(2)}, u32[]{:S(2)}) collective-permute-start(bf16[384,256]{1,0:T(8,128)(2,1)S(1)} %get-tuple-element.52), channel_id=1, source_target_pairs={{0,1},{1,0},{2,3},{3,2},{4,5},{5,4},{6,7},{7,6},{8,9},{9,8},{10,11... | collective-permute-start | bytes 589832 | tf_op jit(solution)/shard_map/ppermute | solution.py:273
  161.1 1.2 collective-permute-start.17
  162.3 1.1 collective-permute-start.18
  163.4 2.4 %collective-permute-done.15.refs_1_ = bf16[384,256]{1,0:T(8,128)(2,1)S(1)} collective-permute-done((bf16[384,256]{1,0:T(8,128)(2,1)S(1)}, bf16[384,256]{1,0:T(8,128)(2,1)S(1)}, u32[]{:S(2)}, u32[]{:S(2)}) %collective-permute-start.15) | collective-permute-done | bytes 196640 | tf_op jit(solution)/shard_map/ppermute | solution.py:273
  165.8 1.1 collective-permute-start.25
  166.9 1.0 collective-permute-done.26.refs_2_
  167.9 1.1 collective-permute-start.27
  169.0 3.0 %collective-permute-start.19 = (bf16[384,256]{1,0:T(8,128)(2,1)S(1)}, bf16[384,256]{1,0:T(8,128)(2,1)S(1)}, u32[]{:S(2)}, u32[]{:S(2)}) collective-permute-start(bf16[384,256]{1,0:T(8,128)(2,1)S(1)} %get-tuple-element.56), channel_id=1, source_target_pairs={{0,5},{1,4},{2,7},{3,6},{4,1},{5,0},{6,3},{7,2},{8,13},{9,12},{10,... | collective-permute-start | bytes 589832 | tf_op jit(solution)/shard_map/ppermute | solution.py:273
  172.0 1.4 collective-permute-done.17.refs_3_
  173.5 0.0 collective-permute-start.20
  173.5 1.6 collective-permute-done.18.refs_4_
  175.1 1.2 collective-permute-start.21
  176.3 15.8 %collective-permute-done.19.refs_5_ = bf16[384,256]{1,0:T(8,128)(2,1)S(1)} collective-permute-done((bf16[384,256]{1,0:T(8,128)(2,1)S(1)}, bf16[384,256]{1,0:T(8,128)(2,1)S(1)}, u32[]{:S(2)}, u32[]{:S(2)}) %collective-permute-start.19) | collective-permute-done | bytes 196640 | tf_op jit(solution)/shard_map/ppermute | solution.py:273
  192.1 4.6 %collective-permute-done.20.refs_6_ = bf16[384,256]{1,0:T(8,128)(2,1)S(1)} collective-permute-done((bf16[384,256]{1,0:T(8,128)(2,1)S(1)}, bf16[384,256]{1,0:T(8,128)(2,1)S(1)}, u32[]{:S(2)}, u32[]{:S(2)}) %collective-permute-start.20) | collective-permute-done | bytes 196640 | tf_op jit(solution)/shard_map/ppermute | solution.py:273
  196.7 5.7 %collective-permute-done.21.refs_7_ = bf16[384,256]{1,0:T(8,128)(2,1)S(1)} collective-permute-done((bf16[384,256]{1,0:T(8,128)(2,1)S(1)}, bf16[384,256]{1,0:T(8,128)(2,1)S(1)}, u32[]{:S(2)}, u32[]{:S(2)}) %collective-permute-start.21) | collective-permute-done | bytes 196640 | tf_op jit(solution)/shard_map/ppermute | solution.py:273
  202.5 1.8 unpack.1
  204.3 1.3 join.1
  (33 shorter events, 0.1 us)
Async XLA Ops:
  0.6 85.1 %copy-start = (bf16[2,128,3072]{2,1,0:T(8,128)(2,1)S(1)}, bf16[2,128,3072]{2,1,0:T(8,128)(2,1)}, u32[]{:S(2)}) copy-start(bf16[2,128,3072]{2,1,0:T(8,128)(2,1)} %param.8) | copy-start | bytes 4718596
  0.6 18.7 %collective-permute-start = (bf16[128,3072]{1,0:T(8,128)(2,1)}, bf16[128,3072]{1,0:T(8,128)(2,1)S(1)}, u32[]{:S(2)}, u32[]{:S(2)}) collective-permute-start(bf16[128,3072]{1,0:T(8,128)(2,1)} %bitcast.13), channel_id=1, source_target_pairs={{0,2},{2,4},{4,6},{6,7},{7,5},{5,3},{3,1},{1,0},{8,10},{10,12},{12... | collective-permute-start | bytes 2359304 | tf_op jit(solution)/shard_map/ppermute | solution.py:255
  2.0 19.5 %collective-permute-start.4 = (bf16[128,3072]{1,0:T(8,128)(2,1)}, bf16[128,3072]{1,0:T(8,128)(2,1)S(1)}, u32[]{:S(2)}, u32[]{:S(2)}) collective-permute-start(bf16[128,3072]{1,0:T(8,128)(2,1)} %bitcast.14), channel_id=1, source_target_pairs={{2,0},{4,2},{6,4},{7,6},{5,7},{3,5},{1,3},{0,1},{10,8},{12,10},{14... | collective-permute-start | bytes 2359304 | tf_op jit(solution)/shard_map/ppermute | solution.py:256
  19.3 17.5 %collective-permute-start.1 = (bf16[128,3072]{1,0:T(8,128)(2,1)S(1)}, bf16[128,3072]{1,0:T(8,128)(2,1)S(1)}, u32[]{:S(2)}, u32[]{:S(2)}) collective-permute-start(bf16[128,3072]{1,0:T(8,128)(2,1)S(1)} %collective-permute-done.refs_2_), channel_id=1, source_target_pairs={{0,2},{2,4},{4,6},{6,7},{7,5},{5,3},{3,1},{1,0},{8,10},{10,12},{12... | collective-permute-start | bytes 2359304 | tf_op jit(solution)/shard_map/ppermute | solution.py:255
  20.6 0.9 copy-start.7
  21.5 17.2 %collective-permute-start.5 = (bf16[128,3072]{1,0:T(8,128)(2,1)S(1)}, bf16[128,3072]{1,0:T(8,128)(2,1)S(1)}, u32[]{:S(2)}, u32[]{:S(2)}) collective-permute-start(bf16[128,3072]{1,0:T(8,128)(2,1)S(1)} %collective-permute-done.4.refs_3_), channel_id=1, source_target_pairs={{2,0},{4,2},{6,4},{7,6},{5,7},{3,5},{1,3},{0,1},{10,8},{12,10},{14... | collective-permute-start | bytes 2359304 | tf_op jit(solution)/shard_map/ppermute | solution.py:256
  21.7 0.9 copy-start.9
  36.8 28.3 %copy-start.11 = (bf16[128,3072]{1,0:T(8,128)(2,1)}, bf16[128,3072]{1,0:T(8,128)(2,1)S(1)}, u32[]{:S(2)}) copy-start(bf16[128,3072]{1,0:T(8,128)(2,1)S(1)} %collective-permute-done.1.refs_4_) | copy-start | bytes 2359300
  36.8 28.3 %collective-permute-start.2 = (bf16[128,3072]{1,0:T(8,128)(2,1)S(1)}, bf16[128,3072]{1,0:T(8,128)(2,1)S(1)}, u32[]{:S(2)}, u32[]{:S(2)}) collective-permute-start(bf16[128,3072]{1,0:T(8,128)(2,1)S(1)} %collective-permute-done.1.refs_4_), channel_id=1, source_target_pairs={{0,2},{2,4},{4,6},{6,7},{7,5},{5,3},{3,1},{1,0},{8,10},{10,12},{12... | collective-permute-start | bytes 2359304 | tf_op jit(solution)/shard_map/ppermute | solution.py:255
  38.7 26.4 %copy-start.13 = (bf16[128,3072]{1,0:T(8,128)(2,1)}, bf16[128,3072]{1,0:T(8,128)(2,1)S(1)}, u32[]{:S(2)}) copy-start(bf16[128,3072]{1,0:T(8,128)(2,1)S(1)} %collective-permute-done.5.refs_5_) | copy-start | bytes 2359300
  38.7 26.4 %collective-permute-start.6 = (bf16[128,3072]{1,0:T(8,128)(2,1)S(1)}, bf16[128,3072]{1,0:T(8,128)(2,1)S(1)}, u32[]{:S(2)}, u32[]{:S(2)}) collective-permute-start(bf16[128,3072]{1,0:T(8,128)(2,1)S(1)} %collective-permute-done.5.refs_5_), channel_id=1, source_target_pairs={{2,0},{4,2},{6,4},{7,6},{5,7},{3,5},{1,3},{0,1},{10,8},{12,10},{14... | collective-permute-start | bytes 2359304 | tf_op jit(solution)/shard_map/ppermute | solution.py:256
  38.9 1.5 copy-start.3
  41.8 17.9 %collective-permute-start.10 = (bf16[384,256]{1,0:T(8,128)(2,1)S(1)}, bf16[384,256]{1,0:T(8,128)(2,1)S(1)}, u32[]{:S(2)}, u32[]{:S(2)}) collective-permute-start(bf16[384,256]{1,0:T(8,128)(2,1)S(1)} %get-tuple-element.39), channel_id=1, source_target_pairs={{0,3},{1,2},{2,1},{3,0},{4,7},{5,6},{6,5},{7,4},{8,11},{9,10},{10,... | collective-permute-start | bytes 589832 | tf_op jit(solution)/shard_map/ppermute | solution.py:273
  42.8 21.6 %collective-permute-start.11 = (bf16[384,256]{1,0:T(8,128)(2,1)S(1)}, bf16[384,256]{1,0:T(8,128)(2,1)S(1)}, u32[]{:S(2)}, u32[]{:S(2)}) collective-permute-start(bf16[384,256]{1,0:T(8,128)(2,1)S(1)} %get-tuple-element.40), channel_id=1, source_target_pairs={{0,4},{1,5},{2,6},{3,7},{4,0},{5,1},{6,2},{7,3},{8,12},{9,13},{10,... | collective-permute-start | bytes 589832 | tf_op jit(solution)/shard_map/ppermute | solution.py:273
  45.1 30.2 %collective-permute-start.12 = (bf16[384,256]{1,0:T(8,128)(2,1)}, bf16[384,256]{1,0:T(8,128)(2,1)}, u32[]{:S(2)}, u32[]{:S(2)}) collective-permute-start(bf16[384,256]{1,0:T(8,128)(2,1)} %get-tuple-element.41), channel_id=1, source_target_pairs={{0,5},{1,4},{2,7},{3,6},{4,1},{5,0},{6,3},{7,2},{8,13},{9,12},{10,... | collective-permute-start | bytes 589832 | tf_op jit(solution)/shard_map/ppermute | solution.py:273
  59.7 22.5 %collective-permute-start.13 = (bf16[384,256]{1,0:T(8,128)(2,1)}, bf16[384,256]{1,0:T(8,128)(2,1)}, u32[]{:S(2)}, u32[]{:S(2)}) collective-permute-start(bf16[384,256]{1,0:T(8,128)(2,1)} %get-tuple-element.42), channel_id=1, source_target_pairs={{0,6},{1,7},{2,4},{3,5},{4,2},{5,3},{6,0},{7,1},{8,14},{9,15},{10,... | collective-permute-start | bytes 589832 | tf_op jit(solution)/shard_map/ppermute | solution.py:273
  64.4 0.7 copy-start.4
  65.1 20.7 %collective-permute-start.14 = (bf16[384,256]{1,0:T(8,128)(2,1)}, bf16[384,256]{1,0:T(8,128)(2,1)}, u32[]{:S(2)}, u32[]{:S(2)}) collective-permute-start(bf16[384,256]{1,0:T(8,128)(2,1)} %get-tuple-element.43), channel_id=1, source_target_pairs={{0,7},{1,6},{2,5},{3,4},{4,3},{5,2},{6,1},{7,0},{8,15},{9,14},{10,... | collective-permute-start | bytes 589832 | tf_op jit(solution)/shard_map/ppermute | solution.py:273
  65.1 20.7 %collective-permute-start.8 = (bf16[384,256]{1,0:T(8,128)(2,1)}, bf16[384,256]{1,0:T(8,128)(2,1)}, u32[]{:S(2)}, u32[]{:S(2)}) collective-permute-start(bf16[384,256]{1,0:T(8,128)(2,1)} %get-tuple-element.37), channel_id=1, source_target_pairs={{0,1},{1,0},{2,3},{3,2},{4,5},{5,4},{6,7},{7,6},{8,9},{9,8},{10,11... | collective-permute-start | bytes 589832 | tf_op jit(solution)/shard_map/ppermute | solution.py:273
  65.2 20.6 %collective-permute-start.9 = (bf16[384,256]{1,0:T(8,128)(2,1)}, bf16[384,256]{1,0:T(8,128)(2,1)}, u32[]{:S(2)}, u32[]{:S(2)}) collective-permute-start(bf16[384,256]{1,0:T(8,128)(2,1)} %get-tuple-element.38), channel_id=1, source_target_pairs={{0,2},{1,3},{2,0},{3,1},{4,6},{5,7},{6,4},{7,5},{8,10},{9,11},{10,... | collective-permute-start | bytes 589832 | tf_op jit(solution)/shard_map/ppermute | solution.py:273
  75.4 44.4 %collective-permute-start.3 = (bf16[64,3072]{1,0:T(8,128)(2,1)S(1)}, bf16[64,3072]{1,0:T(8,128)(2,1)S(1)}, u32[]{:S(2)}, u32[]{:S(2)}) collective-permute-start(bf16[64,3072]{1,0:T(8,128)(2,1)S(1)} %slice.8), channel_id=1, source_target_pairs={{0,2},{2,4},{4,6},{6,7},{7,5},{5,3},{3,1},{1,0},{8,10},{10,12},{12... | collective-permute-start | bytes 1179656 | tf_op jit(solution)/shard_map/ppermute | solution.py:258
  82.2 37.6 %collective-permute-start.7 = (bf16[64,3072]{1,0:T(8,128)(2,1)S(1)}, bf16[64,3072]{1,0:T(8,128)(2,1)S(1)}, u32[]{:S(2)}, u32[]{:S(2)}) collective-permute-start(bf16[64,3072]{1,0:T(8,128)(2,1)S(1)} %slice.9), channel_id=1, source_target_pairs={{2,0},{4,2},{6,4},{7,6},{5,7},{3,5},{1,3},{0,1},{10,8},{12,10},{14... | collective-permute-start | bytes 1179656 | tf_op jit(solution)/shard_map/ppermute | solution.py:259
  85.8 0.9 copy-start.5
  86.7 1.1 copy-start.6
  87.8 1.1 copy-start.8
  89.0 1.1 copy-start.10
  90.1 1.1 copy-start.12
  91.2 1.1 copy-start.14
  119.8 4.4 %copy-start.1 = (f32[2,128,3072]{2,1,0:T(8,128)S(1)}, f32[2,128,3072]{2,1,0:T(8,128)}, u32[]{:S(2)}) copy-start(f32[2,128,3072]{2,1,0:T(8,128)} %param.9) | copy-start | bytes 9437188
  119.8 4.4 %copy-start.2 = (f32[256,3072]{1,0:T(8,128)S(1)}, f32[256,3072]{1,0:T(8,128)}, u32[]{:S(2)}) copy-start(f32[256,3072]{1,0:T(8,128)} %get-tuple-element.59.weight_ref) | copy-start | bytes 9437188
  128.0 10.4 %collective-permute-start.22 = (bf16[2,32,3072]{2,1,0:T(8,128)(2,1)S(1)}, bf16[2,32,3072]{2,1,0:T(8,128)(2,1)S(1)}, u32[]{:S(2)}, u32[]{:S(2)}) collective-permute-start(bf16[2,32,3072]{2,1,0:T(8,128)(2,1)S(1)} %get-tuple-element.62), channel_id=1, source_target_pairs={{0,8},{8,0},{16,24},{24,16},{1,9},{9,1},{17,25},{25,17},{2,10},{10... | collective-permute-start | bytes 1179656 | tf_op jit(solution)/shard_map/ppermute | solution.py:273
  136.8 10.7 %collective-permute-start.23 = (bf16[2,32,3072]{2,1,0:T(8,128)(2,1)S(1)}, bf16[2,32,3072]{2,1,0:T(8,128)(2,1)S(1)}, u32[]{:S(2)}, u32[]{:S(2)}) collective-permute-start(bf16[2,32,3072]{2,1,0:T(8,128)(2,1)S(1)} %get-tuple-element.63), channel_id=1, source_target_pairs={{0,16},{8,24},{16,0},{24,8},{1,17},{9,25},{17,1},{25,9},{2,18},{10... | collective-permute-start | bytes 1179656 | tf_op jit(solution)/shard_map/ppermute | solution.py:273
  138.0 18.1 %collective-permute-start.24 = (bf16[2,32,3072]{2,1,0:T(8,128)(2,1)S(1)}, bf16[2,32,3072]{2,1,0:T(8,128)(2,1)S(1)}, u32[]{:S(2)}, u32[]{:S(2)}) collective-permute-start(bf16[2,32,3072]{2,1,0:T(8,128)(2,1)S(1)} %get-tuple-element.64), channel_id=1, source_target_pairs={{0,24},{8,16},{16,8},{24,0},{1,25},{9,17},{17,9},{25,1},{2,26},{10... | collective-permute-start | bytes 1179656 | tf_op jit(solution)/shard_map/ppermute | solution.py:273
  157.5 10.4 %collective-permute-start.26 = (bf16[2,32,3072]{2,1,0:T(8,128)(2,1)S(1)}, bf16[2,32,3072]{2,1,0:T(8,128)(2,1)S(1)}, u32[]{:S(2)}, u32[]{:S(2)}) collective-permute-start(bf16[2,32,3072]{2,1,0:T(8,128)(2,1)S(1)} %get-tuple-element.65.refs_0_), channel_id=1, source_target_pairs={{0,16},{8,24},{16,0},{24,8},{1,17},{9,25},{17,1},{25,9},{2,18},{10... | collective-permute-start | bytes 1179656 | tf_op jit(solution)/shard_map/ppermute | solution.py:356
  158.7 7.1 %collective-permute-start.15 = (bf16[384,256]{1,0:T(8,128)(2,1)S(1)}, bf16[384,256]{1,0:T(8,128)(2,1)S(1)}, u32[]{:S(2)}, u32[]{:S(2)}) collective-permute-start(bf16[384,256]{1,0:T(8,128)(2,1)S(1)} %get-tuple-element.52), channel_id=1, source_target_pairs={{0,1},{1,0},{2,3},{3,2},{4,5},{5,4},{6,7},{7,6},{8,9},{9,8},{10,11... | collective-permute-start | bytes 589832 | tf_op jit(solution)/shard_map/ppermute | solution.py:273
  161.1 7.9 %collective-permute-start.16 = (bf16[384,256]{1,0:T(8,128)(2,1)S(1)}, bf16[384,256]{1,0:T(8,128)(2,1)S(1)}, u32[]{:S(2)}, u32[]{:S(2)}) collective-permute-start(bf16[384,256]{1,0:T(8,128)(2,1)S(1)} %get-tuple-element.53), channel_id=1, source_target_pairs={{0,2},{1,3},{2,0},{3,1},{4,6},{5,7},{6,4},{7,5},{8,10},{9,11},{10,... | collective-permute-start | bytes 589832 | tf_op jit(solution)/shard_map/ppermute | solution.py:273
  161.1 12.4 %collective-permute-start.17 = (bf16[384,256]{1,0:T(8,128)(2,1)S(1)}, bf16[384,256]{1,0:T(8,128)(2,1)S(1)}, u32[]{:S(2)}, u32[]{:S(2)}) collective-permute-start(bf16[384,256]{1,0:T(8,128)(2,1)S(1)} %get-tuple-element.54), channel_id=1, source_target_pairs={{0,3},{1,2},{2,1},{3,0},{4,7},{5,6},{6,5},{7,4},{8,11},{9,10},{10,... | collective-permute-start | bytes 589832 | tf_op jit(solution)/shard_map/ppermute | solution.py:273
  162.3 12.8 %collective-permute-start.18 = (bf16[384,256]{1,0:T(8,128)(2,1)S(1)}, bf16[384,256]{1,0:T(8,128)(2,1)S(1)}, u32[]{:S(2)}, u32[]{:S(2)}) collective-permute-start(bf16[384,256]{1,0:T(8,128)(2,1)S(1)} %get-tuple-element.55), channel_id=1, source_target_pairs={{0,4},{1,5},{2,6},{3,7},{4,0},{5,1},{6,2},{7,3},{8,12},{9,13},{10,... | collective-permute-start | bytes 589832 | tf_op jit(solution)/shard_map/ppermute | solution.py:273
  165.8 38.4 %collective-permute-start.25 = (bf16[2,32,3072]{2,1,0:T(8,128)(2,1)S(1)}, bf16[2,32,3072]{2,1,0:T(8,128)(2,1)S(1)}, u32[]{:S(2)}, u32[]{:S(2)}) collective-permute-start(bf16[2,32,3072]{2,1,0:T(8,128)(2,1)S(1)} %get-tuple-element.65.refs_0_), channel_id=1, source_target_pairs={{0,8},{8,0},{16,24},{24,16},{1,9},{9,1},{17,25},{25,17},{2,10},{10... | collective-permute-start | bytes 1179656 | tf_op jit(solution)/shard_map/ppermute | solution.py:356
  167.9 36.4 %collective-permute-start.27 = (bf16[2,32,3072]{2,1,0:T(8,128)(2,1)S(1)}, bf16[2,32,3072]{2,1,0:T(8,128)(2,1)S(1)}, u32[]{:S(2)}, u32[]{:S(2)}) collective-permute-start(bf16[2,32,3072]{2,1,0:T(8,128)(2,1)S(1)} %collective-permute-done.26.refs_2_), channel_id=1, source_target_pairs={{0,8},{8,0},{16,24},{24,16},{1,9},{9,1},{17,25},{25,17},{2,10},{10... | collective-permute-start | bytes 1179656 | tf_op jit(solution)/shard_map/ppermute | solution.py:356
  169.0 23.1 %collective-permute-start.19 = (bf16[384,256]{1,0:T(8,128)(2,1)S(1)}, bf16[384,256]{1,0:T(8,128)(2,1)S(1)}, u32[]{:S(2)}, u32[]{:S(2)}) collective-permute-start(bf16[384,256]{1,0:T(8,128)(2,1)S(1)} %get-tuple-element.56), channel_id=1, source_target_pairs={{0,5},{1,4},{2,7},{3,6},{4,1},{5,0},{6,3},{7,2},{8,13},{9,12},{10,... | collective-permute-start | bytes 589832 | tf_op jit(solution)/shard_map/ppermute | solution.py:273
  173.5 23.3 %collective-permute-start.20 = (bf16[384,256]{1,0:T(8,128)(2,1)S(1)}, bf16[384,256]{1,0:T(8,128)(2,1)S(1)}, u32[]{:S(2)}, u32[]{:S(2)}) collective-permute-start(bf16[384,256]{1,0:T(8,128)(2,1)S(1)} %get-tuple-element.57), channel_id=1, source_target_pairs={{0,6},{1,7},{2,4},{3,5},{4,2},{5,3},{6,0},{7,1},{8,14},{9,15},{10,... | collective-permute-start | bytes 589832 | tf_op jit(solution)/shard_map/ppermute | solution.py:273
  175.1 27.4 %collective-permute-start.21 = (bf16[384,256]{1,0:T(8,128)(2,1)S(1)}, bf16[384,256]{1,0:T(8,128)(2,1)S(1)}, u32[]{:S(2)}, u32[]{:S(2)}) collective-permute-start(bf16[384,256]{1,0:T(8,128)(2,1)S(1)} %get-tuple-element.58), channel_id=1, source_target_pairs={{0,7},{1,6},{2,5},{3,4},{4,3},{5,2},{6,1},{7,0},{8,15},{9,14},{10,... | collective-permute-start | bytes 589832 | tf_op jit(solution)/shard_map/ppermute | solution.py:273

commit v2 on v1

v2 whole, which is shorter than its diff:
```python
import functools
import math

import jax
import jax.numpy as jnp
from jax import lax
from jax.experimental import pallas as pl
from jax.experimental.pallas import tpu as pltpu
from jax.sharding import PartitionSpec as P

SMALL, LARGE = 16 * 1024 * 1024, 60 * 1024 * 1024
F32 = jnp.float32
BF16 = jnp.bfloat16


def params(limit):
    return pltpu.CompilerParams(vmem_limit_bytes=limit)


def cost(flops, moved):
    return pl.CostEstimate(flops=flops, bytes_accessed=moved, transcendentals=0)


def ring_order(n):
    return [i for i in range(n) if i % 2 == 0] + [i for i in reversed(range(n)) if i % 2]


def ring_member(place, n):
    return jnp.where(place < n // 2, 2 * place, 2 * n - 1 - 2 * place)


def ring_place(member, n):
    return jnp.where(member % 2 == 0, member // 2, (2 * n - 1 - member) // 2)


def dot_nt(a, b):
    return lax.dot_general(a, b, (((1,), (1,)), ((), ())), preferred_element_type=F32)


def dot_tn(a, b):
    return lax.dot_general(a, b, (((0,), (0,)), ((), ())), preferred_element_type=F32)


def pack_kernel(n, x_ref, out_ref):
    rows, heads, size = x_ref.shape
    wide = heads * size // n
    x = x_ref[...].reshape(rows, heads * size)
    for d in range(n):
        out_ref[d] = x[:, d * wide : (d + 1) * wide]


def unpack_kernel(n, blocks, out_ref):
    out_ref[...] = jnp.concatenate([blocks[d] for d in range(n)], axis=1).reshape(out_ref.shape)


def fetch(copies, sems, first=0):
    started = [
        pltpu.make_async_copy(source, target, sems.at[first + i])
        for i, (source, target) in enumerate(copies)
    ]
    for copy in started:
        copy.start()
    return started


def rows_of(tiles, buffer):
    copies, start = [], 0
    for tile in tiles:
        copies.append((tile, buffer.at[pl.ds(start, tile.shape[0])]))
        start += tile.shape[0]
    return copies


def attend_kernel(n, heads_here, per_group, groups, first, earlier, mask_ref, *refs):
    refs = list(refs)
    last = earlier is not None
    count = sum(len(g) for g in groups)
    take = lambda m: [refs.pop(0) for _ in range(m)]
    tiles = take(count)
    w_ref, block_ref = take(2)
    carried = [] if first else take(2)
    query_parts = take(len(earlier)) if last else []
    if last:
        grads, att_out = take(2)
    else:
        query_out, key_out, value_out, att_out = take(4)
    q_all, k_all, v_all, cot_all, tile_all, w_all, key_all, value_all, sems = refs

    me = lax.axis_index("seq")
    sign = 1 - 2 * lax.rem(lax.axis_index("dp"), 2)
    tokens, wide = q_all.shape[1:]
    size = wide // heads_here
    length = n * tokens
    inv_root = 1.0 / math.sqrt(size)
    place = ring_place(me, n)
    tile_of = lambda offset: ring_member(lax.rem(place + sign * offset + n, n), n)

    used = 0

    def start(copies):
        nonlocal used
        used += len(copies)
        return fetch(copies, sems, used - len(copies))

    w_copy, *tile_copies = start([(w_ref, w_all), *rows_of(tiles, tile_all)])
    block_copies = start(
        [
            (block_ref.at[:, pl.ds(i * tokens, tokens)], target)
            for i, target in enumerate((q_all, k_all, v_all))
        ]
    )
    carried_copies = start(list(zip(carried, (key_all, value_all))))
    part_copies = start(
        [
            (part.at[pl.ds(i * tokens, tokens)], grads.at[tile_of(offset), pl.ds(0, tokens)])
            for part, offsets in zip(query_parts, earlier or [])
            for i, offset in enumerate(offsets)
        ]
    )
    w_copy.wait()
    begin = 0
    for number, group in enumerate(groups):
        ids = [tile_of(offset) for offset in group]
        rows = slice(begin, begin + len(ids) * tokens)
        begin += len(ids) * tokens
        for copy in tile_copies[: len(ids)]:
            copy.wait()
        tile_copies = tile_copies[len(ids) :]
        cot_all[rows] = dot_nt(tile_all[rows], w_all[...]).astype(BF16)
        if number == 0:
            for copy in block_copies:
                copy.wait()
        for h in range(heads_here):
            cols = slice(h * size, (h + 1) * size)
            kind = (me * heads_here + h) // per_group
            bias = jnp.concatenate(
                [
                    jnp.broadcast_to(
                        jnp.concatenate(
                            [
                                jnp.full(
                                    (1, tokens),
                                    jnp.where(mask_ref[kind, t, k] == 1, 0.0, -jnp.inf),
                                    F32,
                                )
                                for k in range(n)
                            ],
                            axis=1,
                        ),
                        (tokens, length),
                    )
                    for t in ids
                ],
                axis=0,
            )
            query = jnp.concatenate([q_all[t, :, cols] for t in ids], axis=0)
            keys = k_all[:, :, cols].reshape(length, size)
            values = v_all[:, :, cols].reshape(length, size)
            cot = cot_all[rows, cols]
            scores = dot_nt(query, keys) * inv_root + bias
            expo = jnp.exp(scores - jnp.max(scores, axis=1, keepdims=True))
            probs = expo * (1.0 / jnp.sum(expo, axis=1, keepdims=True))
            probs_b = probs.astype(BF16)
            att = jnp.dot(probs_b, values, preferred_element_type=F32).astype(BF16)
            att_out[rows, cols] = att
            delta = jnp.sum(cot.astype(F32) * att.astype(F32), axis=1, keepdims=True)
            dprobs = dot_nt(cot, values)
            dscores = (probs * (dprobs - delta)).astype(BF16)
            query_grad = (jnp.dot(dscores, keys, preferred_element_type=F32) * inv_root).astype(BF16)
            key_sum = dot_tn(dscores, query)
            value_sum = dot_tn(probs_b, cot)
            if number == 0 and h == 0:
                for copy in carried_copies:
                    copy.wait()
            if number > 0 or not first:
                key_sum = key_all[:, cols] + key_sum
                value_sum = value_all[:, cols] + value_sum
            if last:
                grads[ids[0], 0:tokens, cols] = query_grad
                grads[:, tokens : 2 * tokens, cols] = (
                    (key_sum * inv_root).astype(BF16).reshape(n, tokens, size)
                )
                grads[:, 2 * tokens :, cols] = value_sum.astype(BF16).reshape(n, tokens, size)
            else:
                query_out[rows, cols] = query_grad
                if number == len(groups) - 1:
                    key_out[:, cols] = key_sum
                    value_out[:, cols] = value_sum
                else:
                    key_all[:, cols] = key_sum
                    value_all[:, cols] = value_sum
    for copy in part_copies:
        copy.wait()


def partial_kernel(part_count, tile_count, *refs):
    att_parts, tiles = refs[:part_count], refs[part_count : part_count + tile_count]
    mom_ref, out_ref, att_all, tile_all, mom_all, sems = refs[part_count + tile_count :]
    copies = fetch(
        [(mom_ref, mom_all), *rows_of(att_parts, att_all), *rows_of(tiles, tile_all)], sems
    )
    for copy in copies:
        copy.wait()
    att = att_all[...].T
    wide_d = out_ref.shape[1]
    chunk = math.gcd(wide_d, 512)
    for c in range(0, wide_d, chunk):
        cols = slice(c, c + chunk)
        grad = jnp.dot(att, tile_all[:, cols], preferred_element_type=F32)
        out_ref[:, cols] = 0.9 * mom_all[:, cols] + 0.1 * grad


def worker_kernel(heads_here, workers, part_count, tile_count, *refs):
    att_parts, tiles = refs[:part_count], refs[part_count : part_count + tile_count]
    part_ref, error_ref, *refs = refs[part_count + tile_count :]
    outs, (sent_ref, att_all, tile_all, mom_all, error_all, sems) = refs[:workers], refs[workers:]
    me = lax.axis_index("dp")
    wide, wide_d = mom_all.shape
    size = wide // heads_here
    chunk = math.gcd(wide_d, 512)
    spans = [pl.ds(h * size, size) for h in range(heads_here)]
    copies = fetch([*rows_of(att_parts, att_all), *rows_of(tiles, tile_all)], sems)
    used = len(copies)
    mom_copies = fetch([(part_ref.at[span], mom_all.at[span]) for span in spans], sems, used)
    used += heads_here
    for copy in copies:
        copy.wait()
    att = att_all[...].T
    block = size // workers
    leaving = []
    for h in range(heads_here):
        rows = slice(h * size, (h + 1) * size)
        mom_copies[h].wait()
        total = jnp.zeros((size, chunk), F32)
        for c in range(0, wide_d, chunk):
            cols = slice(c, c + chunk)
            grad = jnp.dot(att[rows], tile_all[:, cols], preferred_element_type=F32)
            mom = mom_all[rows, cols] + 0.1 * grad
            mom_all[rows, cols] = mom
            total = total + jnp.abs(mom)
        scale = jnp.sum(total, keepdims=True) * (1.0 / (size * wide_d)) + 1e-06
        inverse = 1.0 / scale
        for c in range(0, wide_d, chunk):
            cols = slice(c, c + chunk)
            mom = mom_all[rows, cols]
            sent = (scale * jnp.tanh(mom * inverse)).astype(BF16)
            sent_ref[:, cols] = sent
            error_all[rows, cols] = mom - sent.astype(F32)
        leaving += fetch([(error_all.at[spans[h]], error_ref.at[spans[h]])], sems, used + h)
        for k in range(workers):
            start = pl.multiple_of((me ^ k) * block, block)
            outs[k][h] = sent_ref[pl.ds(start, block)]
    for copy in leaving:
        copy.wait()


def server_kernel(workers, *refs):
    blocks, synced_ref, error_ref = refs[:workers], refs[workers], refs[workers + 1]
    heads_here, block, wide_d = synced_ref.shape
    for h in range(heads_here):
        total = blocks[0][h].astype(F32)
        for k in range(1, workers):
            total = total + blocks[k][h].astype(F32)
        averaged = total * (1.0 / workers)
        scale = jnp.sum(jnp.abs(averaged), keepdims=True) * (1.0 / (block * wide_d)) + 1e-06
        synced = (scale * jnp.tanh(averaged * (1.0 / scale))).astype(BF16)
        synced_ref[h] = synced
        error_ref[h] = averaged - synced.astype(F32)


def join_kernel(workers, *refs):
    blocks, out_ref = refs[:workers], refs[workers]
    me = lax.axis_index("dp")
    block = blocks[0].shape[1]
    for k in range(workers):
        start = pl.multiple_of((me ^ k) * block, block)
        out_ref[:, pl.ds(start, block), :] = blocks[k][...]


def body(qkv, tile_mask, d_out, w_out, momentum):
    n = lax.axis_size("seq")
    workers = lax.axis_size("dp")
    tokens, heads, size = qkv.shape[2:]
    heads_here = w_out.shape[0]
    groups = tile_mask.shape[0]
    per_group = heads // groups
    wide = heads_here * size
    wide_d = d_out.shape[2]
    half = n // 2
    shape = jax.ShapeDtypeStruct

    ring = ring_order(n)

    def around(turn):
        pairs = []
        for worker in range(workers):
            way = turn if worker % 2 == 0 else -turn
            pairs += [(worker * n + ring[i], worker * n + ring[(i + way) % n]) for i in range(n)]
        return lambda x: lax.ppermute(x, ("dp", "seq"), pairs)

    forward, backward = around(1), around(-1)
    own = d_out[0]
    packed_shape = (3 * tokens, wide)
    packed = pl.pallas_call(
        functools.partial(pack_kernel, n),
        out_shape=shape((n, *packed_shape), BF16),
        compiler_params=params(SMALL),
        cost_estimate=cost(0, 4 * qkv.size),
        name="pack",
    )(qkv.reshape(3 * tokens, heads, size))

    def send(blocks, k, axis):
        return lax.ppermute(blocks[k], axis, [(i, i ^ k) for i in range(len(blocks))])

    blocks = lax.all_to_all(packed, "seq", split_axis=0, concat_axis=0, tiled=True)
    w_flat = w_out.reshape(wide, wide_d)
    vmem = pl.BlockSpec(memory_space=pltpu.VMEM)
    smem = pl.BlockSpec(memory_space=pltpu.SMEM)
    anywhere = pl.BlockSpec(memory_space=pl.ANY)
    length = n * tokens

    def attend(groups, tiles, carried, earlier=None, parts=()):
        count = len(tiles)
        operands = [tile_mask, *tiles, w_flat, blocks, *carried, *parts]
        sums = shape((length, wide), F32)
        rows = shape((count * tokens, wide), BF16)
        scratch = [
            pltpu.VMEM((n, tokens, wide), BF16),
            pltpu.VMEM((n, tokens, wide), BF16),
            pltpu.VMEM((n, tokens, wide), BF16),
            pltpu.VMEM(rows.shape, BF16),
            pltpu.VMEM((count * tokens, wide_d), BF16),
            pltpu.VMEM((wide, wide_d), BF16),
            pltpu.VMEM(sums.shape, F32),
            pltpu.VMEM(sums.shape, F32),
            pltpu.SemaphoreType.DMA((count + 6 + n,)),
        ]
        if earlier is not None:
            outs = [shape((n, *packed_shape), BF16), rows]
        else:
            outs = [rows, sums, sums, rows]
        flops = count * (14 * tokens * length * wide + 2 * tokens * wide * wide_d)
        return pl.pallas_call(
            functools.partial(
                attend_kernel, n, heads_here, per_group, groups, not carried, earlier
            ),
            in_specs=[smem] + [anywhere] * (len(operands) - 1),
            out_shape=outs,
            scratch_shapes=scratch,
            compiler_params=params(LARGE),
            cost_estimate=cost(flops, count * 2**23),
            name="attend",
        )(*operands)

    fore, aft = forward(own), backward(own)
    sums, queries, listed, atts, tiles = [], [], [], [], []
    groups, fresh = [[0], [-1, 1]], [own, fore, aft]
    for s in range(1, half):
        if s < half - 1:
            next_fore, next_aft = forward(fore), backward(aft)
        else:
            far = forward(fore)
        query, *sums, att = attend(groups, fresh, sums)
        queries.append(query)
        listed.append(sum(groups, []))
        atts.append(att)
        tiles.append(fresh)
        if s == half - 2:
            joined = sum(tiles, [])
            joined_rows = len(joined) * tokens
            part = pl.pallas_call(
                functools.partial(partial_kernel, len(atts), len(joined)),
                in_specs=[anywhere] * (len(atts) + len(joined) + 1),
                out_shape=shape((wide, wide_d), F32),
                scratch_shapes=[
                    pltpu.VMEM((joined_rows, wide), BF16),
                    pltpu.VMEM((joined_rows, wide_d), BF16),
                    pltpu.VMEM((wide, wide_d), F32),
                    pltpu.SemaphoreType.DMA((len(atts) + len(joined) + 1,)),
                ],
                compiler_params=params(LARGE),
                cost_estimate=cost(2 * joined_rows * wide * wide_d, 2**24),
                name="partial",
            )(*atts, *joined, momentum.reshape(wide, wide_d))
            atts, tiles = [], []
            next_fore, next_aft, part, *sums = lax.optimization_barrier(
                [next_fore, next_aft, part, *sums]
            )
        elif s < half - 1:
            next_fore, next_aft, *sums = lax.optimization_barrier([next_fore, next_aft, *sums])
        if s < half - 1:
            fore, aft = next_fore, next_aft
            groups, fresh = [[-(s + 1), s + 1]], [fore, aft]
    grads, att = attend([[half]], [far], sums, listed, queries)
    returned = lax.all_to_all(grads, "seq", split_axis=0, concat_axis=0, tiled=True)

    atts.append(att)
    worker_tiles = [*sum(tiles, []), far]
    worker_rows = len(worker_tiles) * tokens
    error, *sent = pl.pallas_call(
        functools.partial(worker_kernel, heads_here, workers, len(atts), len(worker_tiles)),
        in_specs=[anywhere] * (len(atts) + len(worker_tiles) + 1),
        out_specs=[anywhere] + [vmem] * workers,
        out_shape=[shape((wide, wide_d), F32)]
        + [shape((heads_here, size // workers, wide_d), BF16)] * workers,
        scratch_shapes=[
            pltpu.VMEM((size, wide_d), BF16),
            pltpu.VMEM((worker_rows, wide), BF16),
            pltpu.VMEM((worker_rows, wide_d), BF16),
            pltpu.VMEM((wide, wide_d), F32),
            pltpu.VMEM((wide, wide_d), F32),
            pltpu.SemaphoreType.DMA((len(atts) + len(worker_tiles) + 2 * heads_here,)),
        ],
        compiler_params=params(LARGE),
        cost_estimate=cost(2 * worker_rows * wide * wide_d, 2**24),
        name="worker",
    )(*atts, *worker_tiles, part)
    received = [sent[0]] + [send(sent, k, "dp") for k in range(1, workers)]

    synced, server_error = pl.pallas_call(
        functools.partial(server_kernel, workers),
        out_shape=[
            shape((heads_here, size // workers, wide_d), BF16),
            shape((heads_here, size // workers, wide_d), F32),
        ],
        compiler_params=params(SMALL),
        cost_estimate=cost(0, 2**22),
        name="server",
    )(*received)
    gathered = [synced] + [None] * (workers - 1)
    for k in range(1, workers):
        source, step = (synced, k) if k == 1 or k % 2 == 0 else (gathered[k - 1], 1)
        gathered[k] = lax.ppermute(source, "dp", [(i, i ^ step) for i in range(workers)])

    grad_rows = pl.pallas_call(
        functools.partial(unpack_kernel, n),
        out_shape=shape((3 * tokens, heads, size), BF16),
        compiler_params=params(SMALL),
        cost_estimate=cost(0, 4 * qkv.size),
        name="unpack",
    )(returned)
    synced_momentum = pl.pallas_call(
        functools.partial(join_kernel, workers),
        out_shape=shape((heads_here, size, wide_d), BF16),
        compiler_params=params(SMALL),
        cost_estimate=cost(0, 4 * w_out.size),
        name="join",
    )(*gathered)
    return (
        grad_rows.reshape(qkv.shape),
        synced_momentum,
        error.reshape(1, heads_here, size, wide_d),
        server_error,
    )


def solution(mesh):
    placed = (
        P(None, "dp", "seq", None, None),
        P(),
        P("dp", "seq", None),
        P("seq", None, None),
        P("seq", None, None),
    )
    return jax.shard_map(
        body,
        mesh=mesh,
        in_specs=placed,
        out_specs=(
            P(None, "dp", "seq", None, None),
            P("seq", None, None),
            P("dp", "seq", None, None),
            P("seq", "dp", None),
        ),
        check_vma=False,
    )
```

time: 206 us -> 174 us (0.84)
  waiting for transfers between devices: 118 us -> 90.4 us
  Pallas kernels: 41.5 us -> 54.2 us
  starting transfers between devices: 33.9 us -> 22.7 us
  local copies, waits for them, and re-layouts: 11.5 us -> 4.44 us
    ppermute x25 -> x10, waiting for transfers between devices: 117 us -> 79.6 us  [the longest x7 61.6 us: around(): return lambda x: lax.ppermute(x, ('dp', 'seq'), pairs)]
    ppermute x25 -> x10, starting transfers between devices: 30.5 us -> 10.3 us  [the longest x7 6.55 us: around(): return lambda x: lax.ppermute(x, ('dp', 'seq'), pairs)]
    all_to_all x0 -> x2, starting transfers between devices: none -> 10.3 us  [the longest x1 5.85 us: body(): lax.all_to_all(packed, 'seq', split_axis=0, concat_axis=0, tiled=True)]
    ppermute x3, waiting for transfers between devices: 0.98 us -> 10.8 us  [body(): lax.ppermute(source, 'dp', [(i, i ^ step) for i in range(workers)])]
    pallas_call x2 -> x3, Pallas kernels: 5.21 us -> 14.7 us  [the longest x1 6.92 us: body(): pl.pallas_call(functools.partial(worker_kernel, heads_here, workers, len(...]
    unnamed x30 -> x18, local copies, waits for them, and re-layouts: 10.6 us -> 4.44 us
    pallas_call x3 -> x4, Pallas kernels: 31.8 us -> 35.2 us  [attend(): pl.pallas_call(functools.partial(attend_kernel, n, heads_here, per_group,...]
  transfers between devices with their start and end apart: 28 -> 15, of which waited for: 17 -> 9; matrix products, arithmetic and copies ran while one was open for 0% -> 0% of each run, Pallas kernels for 15% -> 25%
where the time goes in v2:
time: 174 us; the launch traced here: 172 us
  waiting for transfers between devices  90.4 us (52%)
  Pallas kernels  54.2 us (31%)
  starting transfers between devices  22.7 us (13%)
  local copies, waits for them, and re-layouts  4.44 us (3%)
    ppermute x7, waiting for transfers between devices, around(): return lambda x: lax.ppermute(x, ('dp', 'seq'), pairs)  61.6 us
    pallas_call x4, Pallas kernels, attend(): pl.pallas_call(functools.partial(attend_kernel, n, heads_here, per_group,...  35.2 us
    ppermute x3, waiting for transfers between devices, send(): lax.ppermute(blocks[k], axis, [(i, i ^ k) for i in range(len(blocks))])  18.1 us
    ppermute x3, waiting for transfers between devices, body(): lax.ppermute(source, 'dp', [(i, i ^ step) for i in range(workers)])  10.8 us
    pallas_call x1, Pallas kernels, body(): pl.pallas_call(functools.partial(worker_kernel, heads_here, workers, len(...  6.92 us
    ppermute x7, starting transfers between devices, around(): return lambda x: lax.ppermute(x, ('dp', 'seq'), pairs)  6.55 us
    pallas_call x1, Pallas kernels, body(): pl.pallas_call(functools.partial(partial_kernel, len(atts), len(joined)),...  6.27 us
    all_to_all x1, starting transfers between devices, body(): lax.all_to_all(packed, 'seq', split_axis=0, concat_axis=0, tiled=True)  5.85 us
  transfers between devices with their start and end apart: 15, of which 9 were waited for; matrix products, arithmetic and copies ran while one was open for 0% of the time, Pallas kernels for 25%

profile of v2, /device:TPU:9, one launch (start us, length us, event | category | flops | bytes accessed | tf_op | source)
XLA Modules:
  0.0 172.4 jit_solution(7724208383422228465)
XLA Ops:
  0.6 0.0 copy-start
  0.6 1.4 copy-done
  2.0 1.5 pack.1
  3.5 0.0 copy-start.8
  3.5 5.9 %all-to-all-start = ((bf16[8,384,256]{2,1,0:T(8,128)(2,1)}), bf16[8,384,256]{2,1,0:T(8,128)(2,1)S(1)}, u32[]{:S(2)}, u32[]{:S(2)}) async-start(bf16[8,384,256]{2,1,0:T(8,128)(2,1)} %pack.1), calls=%async_computation | async-start | bytes 3145728 | tf_op jit(solution)/shard_map/all_to_all | solution.py:315
  9.4 0.0 copy-done.8
  9.4 0.1 collective-permute-start
  9.5 1.4 collective-permute-start.2
  10.9 50.5 %collective-permute-done.refs_1_.refs_3_ = bf16[128,3072]{1,0:T(8,128)(2,1)} collective-permute-done((bf16[128,3072]{1,0:T(8,128)(2,1)S(1)}, bf16[128,3072]{1,0:T(8,128)(2,1)}, u32[]{:S(2)}, u32[]{:S(2)}) %collective-permute-start) | collective-permute-done | bytes 786464 | tf_op jit(solution)/shard_map/ppermute | solution.py:299
  61.4 0.0 collective-permute-start.1
  61.4 0.0 collective-permute-done.2.refs_2_.refs_4_
  61.4 2.2 %collective-permute-start.3 = (bf16[128,3072]{1,0:T(8,128)(2,1)}, bf16[128,3072]{1,0:T(8,128)(2,1)S(1)}, u32[]{:S(2)}, u32[]{:S(2)}) collective-permute-start(bf16[128,3072]{1,0:T(8,128)(2,1)} %collective-permute-done.2.refs_2_.refs_4_), channel_id=1, source_target_pairs={{0,1},{2,0},{4,2},{6,4},{7,6},{5,7},{3,5},{1,3},{8,10},{10,12},{12... | collective-permute-start | bytes 2359304 | tf_op jit(solution)/shard_map/ppermute | solution.py:299
  63.5 0.0 all-to-all-done.refs_4_.refs_3_.refs_2_
  63.5 0.0 copy-start.2
  63.5 1.1 copy-done.2
  64.7 10.4 %attend.4 = (bf16[384,256]{1,0:T(8,128)(2,1)}, f32[1024,256]{1,0:T(8,128)}, f32[1024,256]{1,0:T(8,128)}, bf16[384,256]{1,0:T(8,128)(2,1)}) custom-call(s32[8,8,8]{2,1,0:T(8,128)} %mask_ref.7, bf16[128,3072]{1,0:T(8,128)(2,1)} %bitcast.15, bf16[128,3072]{1,0:T(8,128)(2,1)} %collective-permute-done.refs_1_.refs_3_, ...), custom_call_target="tpu_custom_call" | custom-call | flops 2013265920 | bytes 25165824 | tf_op jit(solution)/shard_map/attend/pallas_call | solution.py:343
  75.1 2.6 %collective-permute-done.1.refs_0_.refs_5_ = bf16[128,3072]{1,0:T(8,128)(2,1)S(1)} collective-permute-done((bf16[128,3072]{1,0:T(8,128)(2,1)}, bf16[128,3072]{1,0:T(8,128)(2,1)S(1)}, u32[]{:S(2)}, u32[]{:S(2)}) %collective-permute-start.1) | collective-permute-done | bytes 786464 | tf_op jit(solution)/shard_map/ppermute | solution.py:299
  77.7 0.0 copy-start.3
  77.7 2.7 %collective-permute-done.3.refs_1_.refs_6_ = bf16[128,3072]{1,0:T(8,128)(2,1)S(1)} collective-permute-done((bf16[128,3072]{1,0:T(8,128)(2,1)}, bf16[128,3072]{1,0:T(8,128)(2,1)S(1)}, u32[]{:S(2)}, u32[]{:S(2)}) %collective-permute-start.3) | collective-permute-done | bytes 786464 | tf_op jit(solution)/shard_map/ppermute | solution.py:299
  80.4 0.0 copy-start.4
  80.4 0.0 collective-permute-start.4
  80.4 2.0 %collective-permute-start.5 = (bf16[128,3072]{1,0:T(8,128)(2,1)S(1)}, bf16[128,3072]{1,0:T(8,128)(2,1)S(1)}, u32[]{:S(2)}, u32[]{:S(2)}) collective-permute-start(bf16[128,3072]{1,0:T(8,128)(2,1)S(1)} %collective-permute-done.3.refs_1_.refs_6_), channel_id=1, source_target_pairs={{0,1},{2,0},{4,2},{6,4},{7,6},{5,7},{3,5},{1,3},{8,10},{10,12},{12... | collective-permute-start | bytes 2359304 | tf_op jit(solution)/shard_map/ppermute | solution.py:299
  82.4 0.0 copy-done.3
  82.4 0.0 copy-done.4
  82.4 8.6 %attend.5 = (bf16[256,256]{1,0:T(8,128)(2,1)}, f32[1024,256]{1,0:T(8,128)}, f32[1024,256]{1,0:T(8,128)}, bf16[256,256]{1,0:T(8,128)(2,1)}) custom-call(s32[8,8,8]{2,1,0:T(8,128)} %mask_ref.7, bf16[128,3072]{1,0:T(8,128)(2,1)} %copy-done.3, bf16[128,3072]{1,0:T(8,128)(2,1)} %copy-done.4, bf16[256,3072]{1,0:T(8,128)(2,1)} %bitcast.10, ...), custom_call_target="tpu_custom_call" | custom-call | flops 1342177280 | bytes 16777216 | tf_op jit(solution)/shard_map/attend/pallas_call | solution.py:343
  91.0 6.3 %partial.1.refs_5_ = f32[256,3072]{1,0:T(8,128)} custom-call(bf16[384,256]{1,0:T(8,128)(2,1)} %get-tuple-element.38.refs_0_, bf16[256,256]{1,0:T(8,128)(2,1)} %get-tuple-element.41.refs_1_, bf16[128,3072]{1,0:T(8,128)(2,1)} %bitcast.16, bf16[128,3072]{1,0:T(8,128)(2,1)} %collective-permute-done.refs_1_.refs_3_, ...), custom_call_target="tpu_custom_call" | custom-call | flops 1006632960 | bytes 16777216 | tf_op jit(solution)/shard_map/partial/pallas_call | solution.py:371
  97.3 0.0 collective-permute-done.4.refs_0_.refs_2_
  97.3 0.0 copy-start.6
  97.3 4.2 %collective-permute-done.5.refs_1_.refs_3_ = bf16[128,3072]{1,0:T(8,128)(2,1)S(1)} collective-permute-done((bf16[128,3072]{1,0:T(8,128)(2,1)S(1)}, bf16[128,3072]{1,0:T(8,128)(2,1)S(1)}, u32[]{:S(2)}, u32[]{:S(2)}) %collective-permute-start.5) | collective-permute-done | bytes 786464 | tf_op jit(solution)/shard_map/ppermute | solution.py:299
  101.5 0.0 copy-start.7
  101.5 0.9 collective-permute-start.6
  102.4 0.0 copy-done.6
  102.4 0.0 copy-done.7
  102.4 8.6 %attend.6 = (bf16[256,256]{1,0:T(8,128)(2,1)}, f32[1024,256]{1,0:T(8,128)}, f32[1024,256]{1,0:T(8,128)}, bf16[256,256]{1,0:T(8,128)(2,1)}) custom-call(s32[8,8,8]{2,1,0:T(8,128)} %mask_ref.7, bf16[128,3072]{1,0:T(8,128)(2,1)} %copy-done.6, bf16[128,3072]{1,0:T(8,128)(2,1)} %copy-done.7, bf16[256,3072]{1,0:T(8,128)(2,1)} %bitcast.11, ...), custom_call_target="tpu_custom_call" | custom-call | flops 1342177280 | bytes 16777216 | tf_op jit(solution)/shard_map/attend/pallas_call | solution.py:343
  111.0 1.6 collective-permute-done.6.refs_0_.refs_4_
  112.6 0.0 copy-start.5
  112.6 0.9 copy-done.5
  113.5 7.6 %attend.7 = (bf16[8,384,256]{2,1,0:T(8,128)(2,1)}, bf16[128,256]{1,0:T(8,128)(2,1)}) custom-call(s32[8,8,8]{2,1,0:T(8,128)} %mask_ref.7, bf16[128,3072]{1,0:T(8,128)(2,1)} %copy-done.5, bf16[256,3072]{1,0:T(8,128)(2,1)} %bitcast.12, bf16[8,384,256]{2,1,0:T(8,128)(2,1)} %copy-done.2, f32[1024,256]{1,0:T(8,128)} %get-tuple-element.48.refs_3_, ...), custom_call_target="tpu_custom_call" | custom-call | flops 671088640 | bytes 8388608 | tf_op jit(solution)/shard_map/attend/pallas_call | solution.py:343
  121.1 4.4 %all-to-all-start.1 = ((bf16[8,384,256]{2,1,0:T(8,128)(2,1)}), bf16[8,384,256]{2,1,0:T(8,128)(2,1)S(1)}, u32[]{:S(2)}, u32[]{:S(2)}) async-start(bf16[8,384,256]{2,1,0:T(8,128)(2,1)} %get-tuple-element.53), calls=%async_computation.1 | async-start | bytes 3145728 | tf_op jit(solution)/shard_map/all_to_all | solution.py:395
  125.5 6.9 %worker.1 = (f32[256,3072]{1,0:T(8,128)}, bf16[2,32,3072]{2,1,0:T(8,128)(2,1)}, bf16[2,32,3072]{2,1,0:T(8,128)(2,1)}, bf16[2,32,3072]{2,1,0:T(8,128)(2,1)}, bf16[2,32,3072]{2,1,0:T(8,128)(2,1)}) custom-call(bf16[256,256]{1,0:T(8,128)(2,1)} %get-tuple-element.54.refs_0_, bf16[128,256]{1,0:T(8,128)(2,1)} %get-tuple-element.55.refs_1_, ...), custom_call_target="tpu_custom_call" | custom-call | flops 603979776 | bytes 16777216 | tf_op jit(solution)/shard_map/worker/pallas_call | solution.py:400
  132.4 2.0 %collective-permute-start.7 = (bf16[2,32,3072]{2,1,0:T(8,128)(2,1)}, bf16[2,32,3072]{2,1,0:T(8,128)(2,1)S(1)}, u32[]{:S(2)}, u32[]{:S(2)}) collective-permute-start(bf16[2,32,3072]{2,1,0:T(8,128)(2,1)} %get-tuple-element.58), channel_id=1, source_target_pairs={{0,8},{8,0},{16,24},{24,16},{1,9},{9,1},{17,25},{25,17},{2,10},{10... | collective-permute-start | bytes 1179656 | tf_op jit(solution)/shard_map/ppermute | solution.py:313
  134.4 1.2 collective-permute-start.8
  135.7 0.5 collective-permute-start.9
  136.2 0.0 collective-permute-done.7.refs_1_
  136.2 9.2 %collective-permute-done.8.refs_2_ = bf16[2,32,3072]{2,1,0:T(8,128)(2,1)S(1)} collective-permute-done((bf16[2,32,3072]{2,1,0:T(8,128)(2,1)}, bf16[2,32,3072]{2,1,0:T(8,128)(2,1)S(1)}, u32[]{:S(2)}, u32[]{:S(2)}) %collective-permute-start.8) | collective-permute-done | bytes 393248 | tf_op jit(solution)/shard_map/ppermute | solution.py:313
  145.3 8.9 %collective-permute-done.9.refs_3_ = bf16[2,32,3072]{2,1,0:T(8,128)(2,1)S(1)} collective-permute-done((bf16[2,32,3072]{2,1,0:T(8,128)(2,1)}, bf16[2,32,3072]{2,1,0:T(8,128)(2,1)S(1)}, u32[]{:S(2)}, u32[]{:S(2)}) %collective-permute-start.9) | collective-permute-done | bytes 393248 | tf_op jit(solution)/shard_map/ppermute | solution.py:313
  154.2 0.0 copy-start.1
  154.2 1.0 copy-done.1
  155.2 1.5 server.1
  156.7 1.2 collective-permute-start.11
  157.9 0.2 collective-permute-start.10
  158.1 9.4 %collective-permute-done.11.refs_2_ = bf16[2,32,3072]{2,1,0:T(8,128)(2,1)S(1)} collective-permute-done((bf16[2,32,3072]{2,1,0:T(8,128)(2,1)S(1)}, bf16[2,32,3072]{2,1,0:T(8,128)(2,1)S(1)}, u32[]{:S(2)}, u32[]{:S(2)}) %collective-permute-start.11) | collective-permute-done | bytes 393248 | tf_op jit(solution)/shard_map/ppermute | solution.py:433
  167.5 0.7 collective-permute-start.12
  168.2 0.0 collective-permute-done.10.refs_1_
  168.2 1.3 collective-permute-done.12.refs_3_
  169.6 1.3 join.1
  170.8 0.0 all-to-all-done.1.blocks
  170.8 1.6 unpack.1
Async XLA Ops:
  0.6 1.4 copy-start
  3.5 5.9 %copy-start.8 = (bf16[1,128,3072]{2,1,0:T(8,128)(2,1)S(1)}, bf16[1,128,3072]{2,1,0:T(8,128)(2,1)}, u32[]{:S(2)}) copy-start(bf16[1,128,3072]{2,1,0:T(8,128)(2,1)} %param.7) | copy-start | bytes 2359300
  3.5 60.0 %all-to-all-start = ((bf16[8,384,256]{2,1,0:T(8,128)(2,1)}), bf16[8,384,256]{2,1,0:T(8,128)(2,1)S(1)}, u32[]{:S(2)}, u32[]{:S(2)}) async-start(bf16[8,384,256]{2,1,0:T(8,128)(2,1)} %pack.1), calls=%async_computation | async-start | bytes 3145728 | tf_op jit(solution)/shard_map/all_to_all | solution.py:315
  9.4 52.0 %collective-permute-start = (bf16[128,3072]{1,0:T(8,128)(2,1)S(1)}, bf16[128,3072]{1,0:T(8,128)(2,1)}, u32[]{:S(2)}, u32[]{:S(2)}) collective-permute-start(bf16[128,3072]{1,0:T(8,128)(2,1)S(1)} %bitcast.17), channel_id=1, source_target_pairs={{0,2},{2,4},{4,6},{6,7},{7,5},{5,3},{3,1},{1,0},{8,9},{10,8},{12,1... | collective-permute-start | bytes 2359304 | tf_op jit(solution)/shard_map/ppermute | solution.py:299
  9.5 51.9 %collective-permute-start.2 = (bf16[128,3072]{1,0:T(8,128)(2,1)S(1)}, bf16[128,3072]{1,0:T(8,128)(2,1)}, u32[]{:S(2)}, u32[]{:S(2)}) collective-permute-start(bf16[128,3072]{1,0:T(8,128)(2,1)S(1)} %bitcast.18), channel_id=1, source_target_pairs={{0,1},{2,0},{4,2},{6,4},{7,6},{5,7},{3,5},{1,3},{8,10},{10,12},{12... | collective-permute-start | bytes 2359304 | tf_op jit(solution)/shard_map/ppermute | solution.py:299
  61.4 16.3 %collective-permute-start.1 = (bf16[128,3072]{1,0:T(8,128)(2,1)}, bf16[128,3072]{1,0:T(8,128)(2,1)S(1)}, u32[]{:S(2)}, u32[]{:S(2)}) collective-permute-start(bf16[128,3072]{1,0:T(8,128)(2,1)} %collective-permute-done.refs_1_.refs_3_), channel_id=1, source_target_pairs={{0,2},{2,4},{4,6},{6,7},{7,5},{5,3},{3,1},{1,0},{8,9},{10,8},{12,1... | collective-permute-start | bytes 2359304 | tf_op jit(solution)/shard_map/ppermute | solution.py:299
  61.4 19.0 %collective-permute-start.3 = (bf16[128,3072]{1,0:T(8,128)(2,1)}, bf16[128,3072]{1,0:T(8,128)(2,1)S(1)}, u32[]{:S(2)}, u32[]{:S(2)}) collective-permute-start(bf16[128,3072]{1,0:T(8,128)(2,1)} %collective-permute-done.2.refs_2_.refs_4_), channel_id=1, source_target_pairs={{0,1},{2,0},{4,2},{6,4},{7,6},{5,7},{3,5},{1,3},{8,10},{10,12},{12... | collective-permute-start | bytes 2359304 | tf_op jit(solution)/shard_map/ppermute | solution.py:299
  63.5 1.1 copy-start.2
  77.7 4.7 %copy-start.3 = (bf16[128,3072]{1,0:T(8,128)(2,1)}, bf16[128,3072]{1,0:T(8,128)(2,1)S(1)}, u32[]{:S(2)}) copy-start(bf16[128,3072]{1,0:T(8,128)(2,1)S(1)} %collective-permute-done.1.refs_0_.refs_5_) | copy-start | bytes 2359300
  80.4 2.0 %copy-start.4 = (bf16[128,3072]{1,0:T(8,128)(2,1)}, bf16[128,3072]{1,0:T(8,128)(2,1)S(1)}, u32[]{:S(2)}) copy-start(bf16[128,3072]{1,0:T(8,128)(2,1)S(1)} %collective-permute-done.3.refs_1_.refs_6_) | copy-start | bytes 2359300
  80.4 16.9 %collective-permute-start.4 = (bf16[128,3072]{1,0:T(8,128)(2,1)S(1)}, bf16[128,3072]{1,0:T(8,128)(2,1)S(1)}, u32[]{:S(2)}, u32[]{:S(2)}) collective-permute-start(bf16[128,3072]{1,0:T(8,128)(2,1)S(1)} %collective-permute-done.1.refs_0_.refs_5_), channel_id=1, source_target_pairs={{0,2},{2,4},{4,6},{6,7},{7,5},{5,3},{3,1},{1,0},{8,9},{10,8},{12,1... | collective-permute-start | bytes 2359304 | tf_op jit(solution)/shard_map/ppermute | solution.py:299
  80.4 21.1 %collective-permute-start.5 = (bf16[128,3072]{1,0:T(8,128)(2,1)S(1)}, bf16[128,3072]{1,0:T(8,128)(2,1)S(1)}, u32[]{:S(2)}, u32[]{:S(2)}) collective-permute-start(bf16[128,3072]{1,0:T(8,128)(2,1)S(1)} %collective-permute-done.3.refs_1_.refs_6_), channel_id=1, source_target_pairs={{0,1},{2,0},{4,2},{6,4},{7,6},{5,7},{3,5},{1,3},{8,10},{10,12},{12... | collective-permute-start | bytes 2359304 | tf_op jit(solution)/shard_map/ppermute | solution.py:299
  97.3 5.1 %copy-start.6 = (bf16[128,3072]{1,0:T(8,128)(2,1)}, bf16[128,3072]{1,0:T(8,128)(2,1)S(1)}, u32[]{:S(2)}) copy-start(bf16[128,3072]{1,0:T(8,128)(2,1)S(1)} %collective-permute-done.4.refs_0_.refs_2_) | copy-start | bytes 2359300
  101.5 0.9 copy-start.7
  101.5 11.1 %collective-permute-start.6 = (bf16[128,3072]{1,0:T(8,128)(2,1)S(1)}, bf16[128,3072]{1,0:T(8,128)(2,1)S(1)}, u32[]{:S(2)}, u32[]{:S(2)}) collective-permute-start(bf16[128,3072]{1,0:T(8,128)(2,1)S(1)} %collective-permute-done.4.refs_0_.refs_2_), channel_id=1, source_target_pairs={{0,2},{2,4},{4,6},{6,7},{7,5},{5,3},{3,1},{1,0},{8,9},{10,8},{12,1... | collective-permute-start | bytes 2359304 | tf_op jit(solution)/shard_map/ppermute | solution.py:299
  112.6 0.9 copy-start.5
  121.1 49.8 %all-to-all-start.1 = ((bf16[8,384,256]{2,1,0:T(8,128)(2,1)}), bf16[8,384,256]{2,1,0:T(8,128)(2,1)S(1)}, u32[]{:S(2)}, u32[]{:S(2)}) async-start(bf16[8,384,256]{2,1,0:T(8,128)(2,1)} %get-tuple-element.53), calls=%async_computation.1 | async-start | bytes 3145728 | tf_op jit(solution)/shard_map/all_to_all | solution.py:395
  132.4 3.7 %collective-permute-start.7 = (bf16[2,32,3072]{2,1,0:T(8,128)(2,1)}, bf16[2,32,3072]{2,1,0:T(8,128)(2,1)S(1)}, u32[]{:S(2)}, u32[]{:S(2)}) collective-permute-start(bf16[2,32,3072]{2,1,0:T(8,128)(2,1)} %get-tuple-element.58), channel_id=1, source_target_pairs={{0,8},{8,0},{16,24},{24,16},{1,9},{9,1},{17,25},{25,17},{2,10},{10... | collective-permute-start | bytes 1179656 | tf_op jit(solution)/shard_map/ppermute | solution.py:313
  134.4 10.9 %collective-permute-start.8 = (bf16[2,32,3072]{2,1,0:T(8,128)(2,1)}, bf16[2,32,3072]{2,1,0:T(8,128)(2,1)S(1)}, u32[]{:S(2)}, u32[]{:S(2)}) collective-permute-start(bf16[2,32,3072]{2,1,0:T(8,128)(2,1)} %get-tuple-element.59), channel_id=1, source_target_pairs={{0,16},{8,24},{16,0},{24,8},{1,17},{9,25},{17,1},{25,9},{2,18},{10... | collective-permute-start | bytes 1179656 | tf_op jit(solution)/shard_map/ppermute | solution.py:313
  135.7 18.6 %collective-permute-start.9 = (bf16[2,32,3072]{2,1,0:T(8,128)(2,1)}, bf16[2,32,3072]{2,1,0:T(8,128)(2,1)S(1)}, u32[]{:S(2)}, u32[]{:S(2)}) collective-permute-start(bf16[2,32,3072]{2,1,0:T(8,128)(2,1)} %get-tuple-element.60), channel_id=1, source_target_pairs={{0,24},{8,16},{16,8},{24,0},{1,25},{9,17},{17,9},{25,1},{2,26},{10... | collective-permute-start | bytes 1179656 | tf_op jit(solution)/shard_map/ppermute | solution.py:313
  154.2 1.0 copy-start.1
  156.7 10.8 %collective-permute-start.11 = (bf16[2,32,3072]{2,1,0:T(8,128)(2,1)S(1)}, bf16[2,32,3072]{2,1,0:T(8,128)(2,1)S(1)}, u32[]{:S(2)}, u32[]{:S(2)}) collective-permute-start(bf16[2,32,3072]{2,1,0:T(8,128)(2,1)S(1)} %get-tuple-element.61.refs_0_), channel_id=1, source_target_pairs={{0,16},{8,24},{16,0},{24,8},{1,17},{9,25},{17,1},{25,9},{2,18},{10... | collective-permute-start | bytes 1179656 | tf_op jit(solution)/shard_map/ppermute | solution.py:433
  157.9 10.3 %collective-permute-start.10 = (bf16[2,32,3072]{2,1,0:T(8,128)(2,1)S(1)}, bf16[2,32,3072]{2,1,0:T(8,128)(2,1)S(1)}, u32[]{:S(2)}, u32[]{:S(2)}) collective-permute-start(bf16[2,32,3072]{2,1,0:T(8,128)(2,1)S(1)} %get-tuple-element.61.refs_0_), channel_id=1, source_target_pairs={{0,8},{8,0},{16,24},{24,16},{1,9},{9,1},{17,25},{25,17},{2,10},{10... | collective-permute-start | bytes 1179656 | tf_op jit(solution)/shard_map/ppermute | solution.py:433
  167.5 2.1 %collective-permute-start.12 = (bf16[2,32,3072]{2,1,0:T(8,128)(2,1)S(1)}, bf16[2,32,3072]{2,1,0:T(8,128)(2,1)S(1)}, u32[]{:S(2)}, u32[]{:S(2)}) collective-permute-start(bf16[2,32,3072]{2,1,0:T(8,128)(2,1)S(1)} %collective-permute-done.11.refs_2_), channel_id=1, source_target_pairs={{0,8},{8,0},{16,24},{24,16},{1,9},{9,1},{17,25},{25,17},{2,10},{10... | collective-permute-start | bytes 1179656 | tf_op jit(solution)/shard_map/ppermute | solution.py:433

commit v3 on v2

--- a/solution.py
+++ b/solution.py
@@ -33,6 +33,11 @@
     return jnp.where(member % 2 == 0, member // 2, (2 * n - 1 - member) // 2)
 
 
+def waves_of(n):
+    odd, even = list(range(n - 1, 1, -2)), list(range(n - 2, 0, -2))
+    return [[1, *odd], even]
+
+
 def dot_nt(a, b):
     return lax.dot_general(a, b, (((1,), (1,)), ((), ())), preferred_element_type=F32)
 
@@ -41,12 +46,16 @@
     return lax.dot_general(a, b, (((0,), (0,)), ((), ())), preferred_element_type=F32)
 
 
-def pack_kernel(n, x_ref, out_ref):
+def pack_kernel(n, x_ref, *refs):
+    outs, parts = refs[:n], refs[n]
     rows, heads, size = x_ref.shape
     wide = heads * size // n
     x = x_ref[...].reshape(rows, heads * size)
     for d in range(n):
-        out_ref[d] = x[:, d * wide : (d + 1) * wide]
+        parts[d] = x[:, d * wide : (d + 1) * wide]
+    me = lax.axis_index("seq")
+    for k in range(n):
+        outs[k][...] = parts[me ^ k]
 
 
 def unpack_kernel(n, blocks, out_ref):
@@ -71,20 +80,27 @@
     return copies
 
 
-def attend_kernel(n, heads_here, per_group, groups, first, earlier, mask_ref, *refs):
+def attend_kernel(n, heads_here, per_group, groups, first, earlier, far, mask_ref, *refs):
     refs = list(refs)
-    last = earlier is not None
     count = sum(len(g) for g in groups)
     take = lambda m: [refs.pop(0) for _ in range(m)]
     tiles = take(count)
-    w_ref, block_ref = take(2)
+    (w_ref,) = take(1)
+    blocks = take(n)
     carried = [] if first else take(2)
-    query_parts = take(len(earlier)) if last else []
-    if last:
-        grads, att_out = take(2)
+    (mom_ref,) = take(1) if first else [None]
+    query_parts = [] if earlier is None else take(len(earlier))
+    if far:
+        far_probs_ref, far_att_ref, query_ref, grads = take(4)
     else:
         query_out, key_out, value_out, att_out = take(4)
-    q_all, k_all, v_all, cot_all, tile_all, w_all, key_all, value_all, sems = refs
+    if first:
+        far_probs_out, far_att_out, part_out = take(3)
+    q_all, k_all, v_all, cot_all, tile_all, w_all, key_all, value_all, sems = take(9)
+    if far:
+        far_probs, far_att = take(2)
+    if first:
+        (mom_all,) = take(1)
 
     me = lax.axis_index("seq")
     sign = 1 - 2 * lax.rem(lax.axis_index("dp"), 2)
@@ -105,18 +121,52 @@
     w_copy, *tile_copies = start([(w_ref, w_all), *rows_of(tiles, tile_all)])
     block_copies = start(
         [
-            (block_ref.at[:, pl.ds(i * tokens, tokens)], target)
+            (block.at[pl.ds(i * tokens, tokens)], target.at[me ^ k])
+            for k, block in enumerate(blocks)
             for i, target in enumerate((q_all, k_all, v_all))
         ]
     )
     carried_copies = start(list(zip(carried, (key_all, value_all))))
-    part_copies = start(
-        [
-            (part.at[pl.ds(i * tokens, tokens)], grads.at[tile_of(offset), pl.ds(0, tokens)])
-            for part, offsets in zip(query_parts, earlier or [])
-            for i, offset in enumerate(offsets)
+    mom_copies = start([(mom_ref, mom_all)] if first else [])
+    far_copies = start([(far_probs_ref, far_probs), (far_att_ref, far_att)] if far else [])
+    if far:
+        part_copies = start([(query_ref, grads.at[:, pl.ds(0, tokens)])])
+    else:
+        part_copies = start(
+            [
+                (part.at[pl.ds(i * tokens, tokens)], query_out.at[tile_of(offset)])
+                for part, offsets in zip(query_parts, earlier or [])
+                for i, offset in enumerate(offsets)
+            ]
+        )
+    if earlier is not None:
+        query_out[tile_of(n // 2)] = jnp.zeros((tokens, wide), BF16)
+
+    def forward(ids, h):
+        cols = slice(h * size, (h + 1) * size)
+        kind = (me * heads_here + h) // per_group
+        bias = [
+            jnp.concatenate(
+                [
+                    jnp.full(
+                        (1, tokens), jnp.where(mask_ref[kind, t, k] == 1, 0.0, -jnp.inf), F32
+                    )
+                    for k in range(n)
+                ],
+                axis=1,
+            )
+            for t in ids
         ]
-    )
+        bias = jnp.concatenate([jnp.broadcast_to(b, (tokens, length)) for b in bias], axis=0)
+        query = jnp.concatenate([q_all[t, :, cols] for t in ids], axis=0)
+        keys = k_all[:, :, cols].reshape(length, size)
+        values = v_all[:, :, cols].reshape(length, size)
+        scores = dot_nt(query, keys) * inv_root + bias
+        expo = jnp.exp(scores - jnp.max(scores, axis=1, keepdims=True))
+        probs = expo * (1.0 / jnp.sum(expo, axis=1, keepdims=True))
+        att = jnp.dot(probs.astype(BF16), values, preferred_element_type=F32).astype(BF16)
+        return probs, att
+
     w_copy.wait()
     begin = 0
     for number, group in enumerate(groups):
@@ -128,45 +178,33 @@
         tile_copies = tile_copies[len(ids) :]
         cot_all[rows] = dot_nt(tile_all[rows], w_all[...]).astype(BF16)
         if number == 0:
-            for copy in block_copies:
+            for copy in block_copies + far_copies:
                 copy.wait()
         for h in range(heads_here):
             cols = slice(h * size, (h + 1) * size)
-            kind = (me * heads_here + h) // per_group
-            bias = jnp.concatenate(
-                [
-                    jnp.broadcast_to(
-                        jnp.concatenate(
-                            [
-                                jnp.full(
-                                    (1, tokens),
-                                    jnp.where(mask_ref[kind, t, k] == 1, 0.0, -jnp.inf),
-                                    F32,
-                                )
-                                for k in range(n)
-                            ],
-                            axis=1,
-                        ),
-                        (tokens, length),
-                    )
-                    for t in ids
-                ],
-                axis=0,
-            )
+            if far:
+                probs, att = far_probs[h], far_att[:, cols]
+            else:
+                probs, att = forward(ids, h)
+                att_out[rows, cols] = att
+            probs_b = probs.astype(BF16)
             query = jnp.concatenate([q_all[t, :, cols] for t in ids], axis=0)
             keys = k_all[:, :, cols].reshape(length, size)
             values = v_all[:, :, cols].reshape(length, size)
             cot = cot_all[rows, cols]
-            scores = dot_nt(query, keys) * inv_root + bias
-            expo = jnp.exp(scores - jnp.max(scores, axis=1, keepdims=True))
-            probs = expo * (1.0 / jnp.sum(expo, axis=1, keepdims=True))
-            probs_b = probs.astype(BF16)
-            att = jnp.dot(probs_b, values, preferred_element_type=F32).astype(BF16)
-            att_out[rows, cols] = att
             delta = jnp.sum(cot.astype(F32) * att.astype(F32), axis=1, keepdims=True)
             dprobs = dot_nt(cot, values)
             dscores = (probs * (dprobs - delta)).astype(BF16)
             query_grad = (jnp.dot(dscores, keys, preferred_element_type=F32) * inv_root).astype(BF16)
+            if far:
+                if h == 0:
+                    part_copies.pop().wait()
+                grads[ids[0], 0:tokens, cols] = query_grad
+            elif earlier is None:
+                query_out[rows, cols] = query_grad
+            else:
+                for i, t in enumerate(ids):
+                    query_out[t, :, cols] = query_grad[i * tokens : (i + 1) * tokens]
             key_sum = dot_tn(dscores, query)
             value_sum = dot_tn(probs_b, cot)
             if number == 0 and h == 0:
@@ -175,39 +213,38 @@
             if number > 0 or not first:
                 key_sum = key_all[:, cols] + key_sum
                 value_sum = value_all[:, cols] + value_sum
-            if last:
-                grads[ids[0], 0:tokens, cols] = query_grad
+            if far:
                 grads[:, tokens : 2 * tokens, cols] = (
                     (key_sum * inv_root).astype(BF16).reshape(n, tokens, size)
                 )
                 grads[:, 2 * tokens :, cols] = value_sum.astype(BF16).reshape(n, tokens, size)
+            elif number == len(groups) - 1:
+                key_out[:, cols] = key_sum
+                value_out[:, cols] = value_sum
             else:
-                query_out[rows, cols] = query_grad
-                if number == len(groups) - 1:
-                    key_out[:, cols] = key_sum
-                    value_out[:, cols] = value_sum
-                else:
-                    key_all[:, cols] = key_sum
-                    value_all[:, cols] = value_sum
+                key_all[:, cols] = key_sum
+                value_all[:, cols] = value_sum
+    if first:
+        for h in range(heads_here):
+            probs, att = forward([tile_of(n // 2)], h)
+            far_probs_out[h] = probs
+            far_att_out[:, h * size : (h + 1) * size] = att
+        for copy in mom_copies:
+            copy.wait()
+        wide_d = mom_all.shape[1]
+        chunk = math.gcd(wide_d, 512)
+        att = att_out[...].T
+        leaving = []
+        for c in range(0, wide_d, chunk):
+            cols = slice(c, c + chunk)
+            grad = jnp.dot(att, tile_all[:, cols], preferred_element_type=F32)
+            mom_all[:, cols] = 0.9 * mom_all[:, cols] + 0.1 * grad
+            span = pl.ds(c, chunk)
+            leaving += start([(mom_all.at[:, span], part_out.at[:, span])])
+        for copy in leaving:
+            copy.wait()
     for copy in part_copies:
         copy.wait()
-
-
-def partial_kernel(part_count, tile_count, *refs):
-    att_parts, tiles = refs[:part_count], refs[part_count : part_count + tile_count]
-    mom_ref, out_ref, att_all, tile_all, mom_all, sems = refs[part_count + tile_count :]
-    copies = fetch(
-        [(mom_ref, mom_all), *rows_of(att_parts, att_all), *rows_of(tiles, tile_all)], sems
-    )
-    for copy in copies:
-        copy.wait()
-    att = att_all[...].T
-    wide_d = out_ref.shape[1]
-    chunk = math.gcd(wide_d, 512)
-    for c in range(0, wide_d, chunk):
-        cols = slice(c, c + chunk)
-        grad = jnp.dot(att, tile_all[:, cols], preferred_element_type=F32)
-        out_ref[:, cols] = 0.9 * mom_all[:, cols] + 0.1 * grad
 
 
 def worker_kernel(heads_here, workers, part_count, tile_count, *refs):
@@ -218,11 +255,10 @@
     wide, wide_d = mom_all.shape
     size = wide // heads_here
     chunk = math.gcd(wide_d, 512)
+    used = part_count + tile_count + heads_here
     spans = [pl.ds(h * size, size) for h in range(heads_here)]
     copies = fetch([*rows_of(att_parts, att_all), *rows_of(tiles, tile_all)], sems)
-    used = len(copies)
-    mom_copies = fetch([(part_ref.at[span], mom_all.at[span]) for span in spans], sems, used)
-    used += heads_here
+    mom_copies = fetch([(part_ref.at[s], mom_all.at[s]) for s in spans], sems, len(copies))
     for copy in copies:
         copy.wait()
     att = att_all[...].T
@@ -244,12 +280,13 @@
             cols = slice(c, c + chunk)
             mom = mom_all[rows, cols]
             sent = (scale * jnp.tanh(mom * inverse)).astype(BF16)
-            sent_ref[:, cols] = sent
+            sent_ref[h, :, cols] = sent
             error_all[rows, cols] = mom - sent.astype(F32)
-        leaving += fetch([(error_all.at[spans[h]], error_ref.at[spans[h]])], sems, used + h)
+        going = [(error_all.at[spans[h]], error_ref.at[spans[h]])]
         for k in range(workers):
             start = pl.multiple_of((me ^ k) * block, block)
-            outs[k][h] = sent_ref[pl.ds(start, block)]
+            going.append((sent_ref.at[h, pl.ds(start, block)], outs[k].at[h]))
+        leaving += fetch(going, sems, used + h * len(going))
     for copy in leaving:
         copy.wait()
 
@@ -303,7 +340,8 @@
     packed_shape = (3 * tokens, wide)
     packed = pl.pallas_call(
         functools.partial(pack_kernel, n),
-        out_shape=shape((n, *packed_shape), BF16),
+        out_shape=[shape(packed_shape, BF16)] * n,
+        scratch_shapes=[pltpu.VMEM((n, *packed_shape), BF16)],
         compiler_params=params(SMALL),
         cost_estimate=cost(0, 4 * qkv.size),
         name="pack",
@@ -312,18 +350,21 @@
     def send(blocks, k, axis):
         return lax.ppermute(blocks[k], axis, [(i, i ^ k) for i in range(len(blocks))])
 
-    blocks = lax.all_to_all(packed, "seq", split_axis=0, concat_axis=0, tiled=True)
+    blocks = list(packed)
     w_flat = w_out.reshape(wide, wide_d)
     vmem = pl.BlockSpec(memory_space=pltpu.VMEM)
     smem = pl.BlockSpec(memory_space=pltpu.SMEM)
     anywhere = pl.BlockSpec(memory_space=pl.ANY)
     length = n * tokens
 
-    def attend(groups, tiles, carried, earlier=None, parts=()):
+    def attend(groups, tiles, carried, earlier=None, parts=(), far=()):
         count = len(tiles)
-        operands = [tile_mask, *tiles, w_flat, blocks, *carried, *parts]
+        carried = carried or [momentum.reshape(wide, wide_d)]
+        first = len(carried) == 1
+        operands = [tile_mask, *tiles, w_flat, *blocks, *carried, *parts, *far]
         sums = shape((length, wide), F32)
         rows = shape((count * tokens, wide), BF16)
+        probs = shape((heads_here, tokens, length), F32)
         scratch = [
             pltpu.VMEM((n, tokens, wide), BF16),
             pltpu.VMEM((n, tokens, wide), BF16),
@@ -333,18 +374,29 @@
             pltpu.VMEM((wide, wide_d), BF16),
             pltpu.VMEM(sums.shape, F32),
             pltpu.VMEM(sums.shape, F32),
-            pltpu.SemaphoreType.DMA((count + 6 + n,)),
+            pltpu.SemaphoreType.DMA((count + 8 + 4 * n + wide_d // math.gcd(wide_d, 512),)),
         ]
-        if earlier is not None:
-            outs = [shape((n, *packed_shape), BF16), rows]
+        if far:
+            outs = [shape((n, *packed_shape), BF16)]
+            scratch += [pltpu.VMEM(probs.shape, F32), pltpu.VMEM((tokens, wide), BF16)]
         else:
             outs = [rows, sums, sums, rows]
+        if earlier is not None:
+            outs[0] = shape((n, tokens, wide), BF16)
+        out_specs = [vmem] * len(outs)
+        if first:
+            outs += [probs, shape((tokens, wide), BF16), shape((wide, wide_d), F32)]
+            out_specs += [vmem, vmem, anywhere]
+            scratch += [pltpu.VMEM((wide, wide_d), F32)]
         flops = count * (14 * tokens * length * wide + 2 * tokens * wide * wide_d)
+        if len(outs) == 1:
+            outs, out_specs = outs[0], vmem
         return pl.pallas_call(
             functools.partial(
-                attend_kernel, n, heads_here, per_group, groups, not carried, earlier
+                attend_kernel, n, heads_here, per_group, groups, first, earlier, bool(far)
             ),
             in_specs=[smem] + [anywhere] * (len(operands) - 1),
+            out_specs=out_specs,
             out_shape=outs,
             scratch_shapes=scratch,
             compiler_params=params(LARGE),
@@ -352,64 +404,59 @@
             name="attend",
         )(*operands)
 
-    fore, aft = forward(own), backward(own)
-    sums, queries, listed, atts, tiles = [], [], [], [], []
-    groups, fresh = [[0], [-1, 1]], [own, fore, aft]
-    for s in range(1, half):
+    waves = waves_of(n)
+    early = [[0]] + [[-s, s] for s in range(1, len(waves) + 1)]
+    early_tiles, fore, aft = [own], own, own
+    for wave in waves:
+        fore, aft, *got = lax.optimization_barrier(
+            [forward(fore), backward(aft), *[send(packed, k, "seq") for k in wave]]
+        )
+        early_tiles += [fore, aft]
+        for k, block in zip(wave, got):
+            blocks[k] = block
+
+    groups, fresh, sums, queries, listed, atts, tiles = early, early_tiles, [], [], [], [], []
+    for s in range(len(waves), half):
         if s < half - 1:
             next_fore, next_aft = forward(fore), backward(aft)
+            gather = ()
         else:
             far = forward(fore)
-        query, *sums, att = attend(groups, fresh, sums)
-        queries.append(query)
-        listed.append(sum(groups, []))
-        atts.append(att)
-        tiles.append(fresh)
-        if s == half - 2:
-            joined = sum(tiles, [])
-            joined_rows = len(joined) * tokens
-            part = pl.pallas_call(
-                functools.partial(partial_kernel, len(atts), len(joined)),
-                in_specs=[anywhere] * (len(atts) + len(joined) + 1),
-                out_shape=shape((wide, wide_d), F32),
-                scratch_shapes=[
-                    pltpu.VMEM((joined_rows, wide), BF16),
-                    pltpu.VMEM((joined_rows, wide_d), BF16),
-                    pltpu.VMEM((wide, wide_d), F32),
-                    pltpu.SemaphoreType.DMA((len(atts) + len(joined) + 1,)),
-                ],
-                compiler_params=params(LARGE),
-                cost_estimate=cost(2 * joined_rows * wide * wide_d, 2**24),
-                name="partial",
-            )(*atts, *joined, momentum.reshape(wide, wide_d))
-            atts, tiles = [], []
-            next_fore, next_aft, part, *sums = lax.optimization_barrier(
-                [next_fore, next_aft, part, *sums]
+            gather = (listed, queries)
+        query, key_sum, value_sum, att, *saved = attend(groups, fresh, sums, *gather)
+        sums = [key_sum, value_sum]
+        if saved:
+            far_probs, far_att, part = saved
+        else:
+            atts.append(att)
+            tiles += fresh
+        if s < half - 1:
+            fore, aft, query, *sums = lax.optimization_barrier(
+                [next_fore, next_aft, query, *sums]
             )
-        elif s < half - 1:
-            next_fore, next_aft, *sums = lax.optimization_barrier([next_fore, next_aft, *sums])
-        if s < half - 1:
-            fore, aft = next_fore, next_aft
+            listed.append(sum(groups, []))
+            queries.append(query)
             groups, fresh = [[-(s + 1), s + 1]], [fore, aft]
-    grads, att = attend([[half]], [far], sums, listed, queries)
+    grads = attend([[half]], [far], sums, far=(far_probs, far_att, query))
     returned = lax.all_to_all(grads, "seq", split_axis=0, concat_axis=0, tiled=True)
 
-    atts.append(att)
-    worker_tiles = [*sum(tiles, []), far]
+    atts.append(far_att)
+    worker_tiles = [*tiles, far]
     worker_rows = len(worker_tiles) * tokens
+    worker_copies = len(atts) + len(worker_tiles) + heads_here * (workers + 2)
     error, *sent = pl.pallas_call(
         functools.partial(worker_kernel, heads_here, workers, len(atts), len(worker_tiles)),
         in_specs=[anywhere] * (len(atts) + len(worker_tiles) + 1),
-        out_specs=[anywhere] + [vmem] * workers,
+        out_specs=[anywhere] * (1 + workers),
         out_shape=[shape((wide, wide_d), F32)]
         + [shape((heads_here, size // workers, wide_d), BF16)] * workers,
         scratch_shapes=[
-            pltpu.VMEM((size, wide_d), BF16),
+            pltpu.VMEM((heads_here, size, wide_d), BF16),
             pltpu.VMEM((worker_rows, wide), BF16),
             pltpu.VMEM((worker_rows, wide_d), BF16),
             pltpu.VMEM((wide, wide_d), F32),
             pltpu.VMEM((wide, wide_d), F32),
-            pltpu.SemaphoreType.DMA((len(atts) + len(worker_tiles) + 2 * heads_here,)),
+            pltpu.SemaphoreType.DMA((worker_copies,)),
         ],
         compiler_params=params(LARGE),
         cost_estimate=cost(2 * worker_rows * wide * wide_d, 2**24),

time: 174 us -> 169 us (0.971)
  starting transfers between devices: 22.7 us -> 48.3 us
  waiting for transfers between devices: 90.4 us -> 69.3 us
  Pallas kernels: 54.2 us -> 45.2 us
    ppermute x7, waiting for transfers between devices: 61.6 us -> 1.67 us  [around(): return lambda x: lax.ppermute(x, ('dp', 'seq'), pairs)]
    ppermute x3 -> x10, waiting for transfers between devices: 18.1 us -> 56.9 us  [send(): lax.ppermute(blocks[k], axis, [(i, i ^ k) for i in range(len(blocks))])]
    ppermute x3 -> x10, starting transfers between devices: 3.73 us -> 28.6 us  [send(): lax.ppermute(blocks[k], axis, [(i, i ^ k) for i in range(len(blocks))])]
    pallas_call x2 -> x1, Pallas kernels: 7.77 us -> 0.54 us  [body(): pl.pallas_call(functools.partial(pack_kernel, n), out_shape=[shape(packed...]
    all_to_all x1 -> x0, starting transfers between devices: 5.85 us -> none  [body(): lax.all_to_all(packed, 'seq', split_axis=0, concat_axis=0, tiled=True)]
    ppermute x7, starting transfers between devices: 6.55 us -> 12.1 us  [around(): return lambda x: lax.ppermute(x, ('dp', 'seq'), pairs)]
    pallas_call x4 -> x3, Pallas kernels: 35.2 us -> 34.4 us  [attend(): pl.pallas_call(functools.partial(attend_kernel, n, heads_here, per_group,...]
    unnamed x18 -> x30, local copies, waits for them, and re-layouts: 4.44 us -> 4.01 us
  transfers between devices with their start and end apart: 15 -> 21, of which waited for: 9 -> 11; matrix products, arithmetic and copies ran while one was open for 0% -> 0% of each run, Pallas kernels for 25% -> 22%
where the time goes in v3:
time: 169 us; the launch traced here: 168 us
  waiting for transfers between devices  69.3 us (41%)
  starting transfers between devices  48.3 us (29%)
  Pallas kernels  45.2 us (27%)
  local copies, waits for them, and re-layouts  4.01 us (2%)
    ppermute x10, waiting for transfers between devices, send(): lax.ppermute(blocks[k], axis, [(i, i ^ k) for i in range(len(blocks))])  56.9 us
    pallas_call x3, Pallas kernels, attend(): pl.pallas_call(functools.partial(attend_kernel, n, heads_here, per_group,...  34.4 us
    ppermute x10, starting transfers between devices, send(): lax.ppermute(blocks[k], axis, [(i, i ^ k) for i in range(len(blocks))])  28.6 us
    ppermute x7, starting transfers between devices, around(): return lambda x: lax.ppermute(x, ('dp', 'seq'), pairs)  12.1 us
    ppermute x3, waiting for transfers between devices, body(): lax.ppermute(source, 'dp', [(i, i ^ step) for i in range(workers)])  10.7 us
    pallas_call x1, Pallas kernels, body(): pl.pallas_call(functools.partial(worker_kernel, heads_here, workers, len(...  5.98 us
    all_to_all x1, starting transfers between devices, body(): lax.all_to_all(grads, 'seq', split_axis=0, concat_axis=0, tiled=True)  5.45 us
    unnamed x30, local copies, waits for them, and re-layouts  4.01 us
  transfers between devices with their start and end apart: 21, of which 11 were waited for; matrix products, arithmetic and copies ran while one was open for 0% of the time, Pallas kernels for 22%

profile of v3, /device:TPU:9, one launch (start us, length us, event | category | flops | bytes accessed | tf_op | source)
XLA Modules:
  0.0 167.7 jit_solution(8157868784853968802)
XLA Ops:
  0.6 1.3 collective-permute-start.1
  2.0 0.2 collective-permute-start
  2.2 1.4 copy-done
  3.6 0.5 pack.1
  4.1 0.0 copy-start.1
  4.1 0.7 copy-done.1
  4.8 1.2 collective-permute-start.2
  6.0 1.2 collective-permute-start.3
  7.3 1.9 %collective-permute-start.4 = (bf16[384,256]{1,0:T(8,128)(2,1)S(1)}, bf16[384,256]{1,0:T(8,128)(2,1)S(1)}, u32[]{:S(2)}, u32[]{:S(2)}) collective-permute-start(bf16[384,256]{1,0:T(8,128)(2,1)S(1)} %get-tuple-element.47), channel_id=1, source_target_pairs={{0,5},{1,4},{2,7},{3,6},{4,1},{5,0},{6,3},{7,2},{8,13},{9,12},{10,... | collective-permute-start | bytes 589832 | tf_op jit(solution)/shard_map/ppermute | solution.py:351
  9.2 0.8 collective-permute-done.2.refs_7_.refs_4_.refs_3_
  10.0 15.4 %collective-permute-start.5 = (bf16[384,256]{1,0:T(8,128)(2,1)S(1)}, bf16[384,256]{1,0:T(8,128)(2,1)S(1)}, u32[]{:S(2)}, u32[]{:S(2)}) collective-permute-start(bf16[384,256]{1,0:T(8,128)(2,1)S(1)} %get-tuple-element.48), channel_id=1, source_target_pairs={{0,3},{1,2},{2,1},{3,0},{4,7},{5,6},{6,5},{7,4},{8,11},{9,10},{10,... | collective-permute-start | bytes 589832 | tf_op jit(solution)/shard_map/ppermute | solution.py:351
  25.4 6.9 %collective-permute-done.3.refs_13_.refs_10_.refs_9_ = bf16[384,256]{1,0:T(8,128)(2,1)S(1)} collective-permute-done((bf16[384,256]{1,0:T(8,128)(2,1)S(1)}, bf16[384,256]{1,0:T(8,128)(2,1)S(1)}, u32[]{:S(2)}, u32[]{:S(2)}) %collective-permute-start.3) | collective-permute-done | bytes 196640 | tf_op jit(solution)/shard_map/ppermute | solution.py:351
  32.3 2.4 %collective-permute-done.4.refs_11_.refs_8_.refs_7_ = bf16[384,256]{1,0:T(8,128)(2,1)S(1)} collective-permute-done((bf16[384,256]{1,0:T(8,128)(2,1)S(1)}, bf16[384,256]{1,0:T(8,128)(2,1)S(1)}, u32[]{:S(2)}, u32[]{:S(2)}) %collective-permute-start.4) | collective-permute-done | bytes 196640 | tf_op jit(solution)/shard_map/ppermute | solution.py:351
  34.8 0.0 collective-permute-done.5.refs_9_.refs_6_.refs_5_
  34.8 0.0 collective-permute-done.1.refs_2_
  34.8 0.0 copy-start.13
  34.8 0.0 collective-permute-done.refs_1_
  34.8 0.0 copy-start.14
  34.8 2.0 %collective-permute-start.6 = (bf16[128,3072]{1,0:T(8,128)(2,1)S(1)}, bf16[128,3072]{1,0:T(8,128)(2,1)}, u32[]{:S(2)}, u32[]{:S(2)}) collective-permute-start(bf16[128,3072]{1,0:T(8,128)(2,1)S(1)} %collective-permute-done.refs_1_), channel_id=1, source_target_pairs={{0,2},{2,4},{4,6},{6,7},{7,5},{5,3},{3,1},{1,0},{8,9},{10,8},{12,1... | collective-permute-start | bytes 2359304 | tf_op jit(solution)/shard_map/ppermute | solution.py:336
  36.8 5.2 %collective-permute-start.7 = (bf16[128,3072]{1,0:T(8,128)(2,1)S(1)}, bf16[128,3072]{1,0:T(8,128)(2,1)}, u32[]{:S(2)}, u32[]{:S(2)}) collective-permute-start(bf16[128,3072]{1,0:T(8,128)(2,1)S(1)} %collective-permute-done.1.refs_2_), channel_id=1, source_target_pairs={{0,1},{2,0},{4,2},{6,4},{7,6},{5,7},{3,5},{1,3},{8,10},{10,12},{12... | collective-permute-start | bytes 2359304 | tf_op jit(solution)/shard_map/ppermute | solution.py:336
  42.0 2.1 %collective-permute-start.8 = (bf16[384,256]{1,0:T(8,128)(2,1)S(1)}, bf16[384,256]{1,0:T(8,128)(2,1)S(1)}, u32[]{:S(2)}, u32[]{:S(2)}) collective-permute-start(bf16[384,256]{1,0:T(8,128)(2,1)S(1)} %get-tuple-element.51), channel_id=1, source_target_pairs={{0,6},{1,7},{2,4},{3,5},{4,2},{5,3},{6,0},{7,1},{8,14},{9,15},{10,... | collective-permute-start | bytes 589832 | tf_op jit(solution)/shard_map/ppermute | solution.py:351
  44.1 2.8 %collective-permute-start.9 = (bf16[384,256]{1,0:T(8,128)(2,1)S(1)}, bf16[384,256]{1,0:T(8,128)(2,1)S(1)}, u32[]{:S(2)}, u32[]{:S(2)}) collective-permute-start(bf16[384,256]{1,0:T(8,128)(2,1)S(1)} %get-tuple-element.52), channel_id=1, source_target_pairs={{0,4},{1,5},{2,6},{3,7},{4,0},{5,1},{6,2},{7,3},{8,12},{9,13},{10,... | collective-permute-start | bytes 589832 | tf_op jit(solution)/shard_map/ppermute | solution.py:351
  47.0 0.0 collective-permute-start.10
  47.0 24.5 %collective-permute-done.8.refs_12_.refs_9_.refs_8_ = bf16[384,256]{1,0:T(8,128)(2,1)S(1)} collective-permute-done((bf16[384,256]{1,0:T(8,128)(2,1)S(1)}, bf16[384,256]{1,0:T(8,128)(2,1)S(1)}, u32[]{:S(2)}, u32[]{:S(2)}) %collective-permute-start.8) | collective-permute-done | bytes 196640 | tf_op jit(solution)/shard_map/ppermute | solution.py:351
  71.5 4.2 %collective-permute-done.9.refs_10_.refs_7_.refs_6_ = bf16[384,256]{1,0:T(8,128)(2,1)S(1)} collective-permute-done((bf16[384,256]{1,0:T(8,128)(2,1)S(1)}, bf16[384,256]{1,0:T(8,128)(2,1)S(1)}, u32[]{:S(2)}, u32[]{:S(2)}) %collective-permute-start.9) | collective-permute-done | bytes 196640 | tf_op jit(solution)/shard_map/ppermute | solution.py:351
  75.7 0.0 collective-permute-done.10.refs_8_.refs_5_.refs_4_
  75.7 0.0 collective-permute-done.6.refs_3_
  75.7 0.0 copy-done.14
  75.7 0.0 collective-permute-done.7.refs_4_
  75.7 0.1 collective-permute-start.11
  75.8 1.5 collective-permute-start.12
  77.2 0.0 copy-done.6
  77.2 0.0 copy-done.7
  77.3 0.0 copy-done.8
  77.3 0.0 copy-done.9
  77.3 0.0 copy-done.13
  77.3 0.0 copy-done.10
  77.3 17.9 %attend.3 = (bf16[640,256]{1,0:T(8,128)(2,1)}, f32[1024,256]{1,0:T(8,128)}, f32[1024,256]{1,0:T(8,128)}, bf16[640,256]{1,0:T(8,128)(2,1)}, f32[2,128,1024]{2,1,0...) custom-call(s32[8,8,8]{2,1,0:T(8,128)} %mask_ref.5, bf16[128,3072]{1,0:T(8,128)(2,1)} %bitcast.17, ...), custom_call_target="tpu_custom_call" | custom-call | flops 3355443200 | bytes 41943040 | tf_op jit(solution)/shard_map/attend/pallas_call | solution.py:394
  95.2 0.0 collective-permute-done.11.refs_0_.refs_2_
  95.2 1.6 collective-permute-done.12.refs_1_.refs_3_
  96.8 1.8 %collective-permute-start.13 = (bf16[128,3072]{1,0:T(8,128)(2,1)S(1)}, bf16[128,3072]{1,0:T(8,128)(2,1)S(1)}, u32[]{:S(2)}, u32[]{:S(2)}) collective-permute-start(bf16[128,3072]{1,0:T(8,128)(2,1)S(1)} %collective-permute-done.11.refs_0_.refs_2_), channel_id=1, source_target_pairs={{0,2},{2,4},{4,6},{6,7},{7,5},{5,3},{3,1},{1,0},{8,9},{10,8},{12,1... | collective-permute-start | bytes 2359304 | tf_op jit(solution)/shard_map/ppermute | solution.py:336
  98.6 9.2 %attend.4 = (bf16[8,128,256]{2,1,0:T(8,128)(2,1)}, f32[1024,256]{1,0:T(8,128)}, f32[1024,256]{1,0:T(8,128)}, bf16[256,256]{1,0:T(8,128)(2,1)}) custom-call(s32[8,8,8]{2,1,0:T(8,128)} %mask_ref.5, bf16[128,3072]{1,0:T(8,128)(2,1)} %copy-done.3, bf16[128,3072]{1,0:T(8,128)(2,1)} %copy-done.4, bf16[256,3072]{1,0:T(8,128)(2,1)} %bitcast.10, ...), custom_call_target="tpu_custom_call" | custom-call | flops 1342177280 | bytes 16777216 | tf_op jit(solution)/shard_map/attend/pallas_call | solution.py:394
  107.8 0.1 collective-permute-done.13.refs_0_.refs_4_
  107.9 0.9 copy-done.5
  108.8 7.3 %attend.5 = bf16[8,384,256]{2,1,0:T(8,128)(2,1)} custom-call(s32[8,8,8]{2,1,0:T(8,128)} %mask_ref.5, bf16[128,3072]{1,0:T(8,128)(2,1)} %copy-done.5, bf16[256,3072]{1,0:T(8,128)(2,1)} %bitcast.11, bf16[384,256]{1,0:T(8,128)(2,1)} %copy-done.1, bf16[384,256]{1,0:T(8,128)(2,1)} %copy-done.6, bf16[384,256]{1,0:T(8,128)(2,1)} %copy-done.12, ...), custom_call_target="tpu_custom_call" | custom-call | flops 671088640 | bytes 8388608 | tf_op jit(solution)/shard_map/attend/pallas_call | solution.py:394
  116.1 5.5 %all-to-all-start = ((bf16[8,384,256]{2,1,0:T(8,128)(2,1)}), bf16[8,384,256]{2,1,0:T(8,128)(2,1)S(1)}, u32[]{:S(2)}, u32[]{:S(2)}) async-start(bf16[8,384,256]{2,1,0:T(8,128)(2,1)} %attend.5), calls=%async_computation | async-start | bytes 3145728 | tf_op jit(solution)/shard_map/all_to_all | solution.py:441
  121.6 6.0 %worker.1 = (f32[256,3072]{1,0:T(8,128)}, bf16[2,32,3072]{2,1,0:T(8,128)(2,1)}, bf16[2,32,3072]{2,1,0:T(8,128)(2,1)}, bf16[2,32,3072]{2,1,0:T(8,128)(2,1)}, bf16[2,32,3072]{2,1,0:T(8,128)(2,1)}) custom-call(bf16[256,256]{1,0:T(8,128)(2,1)} %get-tuple-element.77.refs_0_, bf16[128,256]{1,0:T(8,128)(2,1)} %get-tuple-element.75.refs_13_.refs_1_, ...), custom_call_target="tpu_custom_call" | custom-call | flops 603979776 | bytes 16777216 | tf_op jit(solution)/shard_map/worker/pallas_call | solution.py:447
  127.6 2.2 %collective-permute-start.14 = (bf16[2,32,3072]{2,1,0:T(8,128)(2,1)}, bf16[2,32,3072]{2,1,0:T(8,128)(2,1)S(1)}, u32[]{:S(2)}, u32[]{:S(2)}) collective-permute-start(bf16[2,32,3072]{2,1,0:T(8,128)(2,1)} %get-tuple-element.80), channel_id=1, source_target_pairs={{0,8},{8,0},{16,24},{24,16},{1,9},{9,1},{17,25},{25,17},{2,10},{10... | collective-permute-start | bytes 1179656 | tf_op jit(solution)/shard_map/ppermute | solution.py:351
  129.8 1.2 collective-permute-start.15
  131.0 0.5 collective-permute-start.16
  131.5 0.0 collective-permute-done.14.refs_1_
  131.5 9.2 %collective-permute-done.15.refs_2_ = bf16[2,32,3072]{2,1,0:T(8,128)(2,1)S(1)} collective-permute-done((bf16[2,32,3072]{2,1,0:T(8,128)(2,1)}, bf16[2,32,3072]{2,1,0:T(8,128)(2,1)S(1)}, u32[]{:S(2)}, u32[]{:S(2)}) %collective-permute-start.15) | collective-permute-done | bytes 393248 | tf_op jit(solution)/shard_map/ppermute | solution.py:351
  140.7 8.9 %collective-permute-done.16.refs_3_ = bf16[2,32,3072]{2,1,0:T(8,128)(2,1)S(1)} collective-permute-done((bf16[2,32,3072]{2,1,0:T(8,128)(2,1)}, bf16[2,32,3072]{2,1,0:T(8,128)(2,1)S(1)}, u32[]{:S(2)}, u32[]{:S(2)}) %collective-permute-start.16) | collective-permute-done | bytes 393248 | tf_op jit(solution)/shard_map/ppermute | solution.py:351
  149.5 1.0 copy-done.2
  150.5 1.5 server.1
  152.0 1.2 collective-permute-start.18
  153.2 0.2 collective-permute-start.17
  153.4 9.4 %collective-permute-done.18.refs_2_ = bf16[2,32,3072]{2,1,0:T(8,128)(2,1)S(1)} collective-permute-done((bf16[2,32,3072]{2,1,0:T(8,128)(2,1)S(1)}, bf16[2,32,3072]{2,1,0:T(8,128)(2,1)S(1)}, u32[]{:S(2)}, u32[]{:S(2)}) %collective-permute-start.18) | collective-permute-done | bytes 393248 | tf_op jit(solution)/shard_map/ppermute | solution.py:480
  162.8 0.7 collective-permute-start.19
  163.5 0.0 collective-permute-done.17.refs_1_
  163.5 1.3 collective-permute-done.19.refs_3_
  164.9 1.3 join.1
  166.1 0.0 all-to-all-done.blocks
  166.1 1.6 unpack.1
  (16 shorter events, 0.0 us)
Async XLA Ops:
  0.6 34.1 %collective-permute-start.1 = (bf16[128,3072]{1,0:T(8,128)(2,1)}, bf16[128,3072]{1,0:T(8,128)(2,1)S(1)}, u32[]{:S(2)}, u32[]{:S(2)}) collective-permute-start(bf16[128,3072]{1,0:T(8,128)(2,1)} %bitcast.15), channel_id=1, source_target_pairs={{0,1},{2,0},{4,2},{6,4},{7,6},{5,7},{3,5},{1,3},{8,10},{10,12},{12... | collective-permute-start | bytes 2359304 | tf_op jit(solution)/shard_map/ppermute | solution.py:336
  2.0 32.8 %collective-permute-start = (bf16[128,3072]{1,0:T(8,128)(2,1)}, bf16[128,3072]{1,0:T(8,128)(2,1)S(1)}, u32[]{:S(2)}, u32[]{:S(2)}) collective-permute-start(bf16[128,3072]{1,0:T(8,128)(2,1)} %bitcast.16), channel_id=1, source_target_pairs={{0,2},{2,4},{4,6},{6,7},{7,5},{5,3},{3,1},{1,0},{8,9},{10,8},{12,1... | collective-permute-start | bytes 2359304 | tf_op jit(solution)/shard_map/ppermute | solution.py:336
  2.1 1.4 copy-start
  4.1 0.7 copy-start.1
  4.8 5.2 %collective-permute-start.2 = (bf16[384,256]{1,0:T(8,128)(2,1)S(1)}, bf16[384,256]{1,0:T(8,128)(2,1)S(1)}, u32[]{:S(2)}, u32[]{:S(2)}) collective-permute-start(bf16[384,256]{1,0:T(8,128)(2,1)S(1)} %get-tuple-element.45), channel_id=1, source_target_pairs={{0,1},{1,0},{2,3},{3,2},{4,5},{5,4},{6,7},{7,6},{8,9},{9,8},{10,11... | collective-permute-start | bytes 589832 | tf_op jit(solution)/shard_map/ppermute | solution.py:351
  6.0 26.3 %collective-permute-start.3 = (bf16[384,256]{1,0:T(8,128)(2,1)S(1)}, bf16[384,256]{1,0:T(8,128)(2,1)S(1)}, u32[]{:S(2)}, u32[]{:S(2)}) collective-permute-start(bf16[384,256]{1,0:T(8,128)(2,1)S(1)} %get-tuple-element.46), channel_id=1, source_target_pairs={{0,7},{1,6},{2,5},{3,4},{4,3},{5,2},{6,1},{7,0},{8,15},{9,14},{10,... | collective-permute-start | bytes 589832 | tf_op jit(solution)/shard_map/ppermute | solution.py:351
  7.3 27.5 %collective-permute-start.4 = (bf16[384,256]{1,0:T(8,128)(2,1)S(1)}, bf16[384,256]{1,0:T(8,128)(2,1)S(1)}, u32[]{:S(2)}, u32[]{:S(2)}) collective-permute-start(bf16[384,256]{1,0:T(8,128)(2,1)S(1)} %get-tuple-element.47), channel_id=1, source_target_pairs={{0,5},{1,4},{2,7},{3,6},{4,1},{5,0},{6,3},{7,2},{8,13},{9,12},{10,... | collective-permute-start | bytes 589832 | tf_op jit(solution)/shard_map/ppermute | solution.py:351
  10.0 67.3 %copy-start.6 = (bf16[384,256]{1,0:T(8,128)(2,1)}, bf16[384,256]{1,0:T(8,128)(2,1)S(1)}, u32[]{:S(2)}) copy-start(bf16[384,256]{1,0:T(8,128)(2,1)S(1)} %collective-permute-done.2.refs_7_.refs_4_.refs_3_) | copy-start | bytes 589828
  10.0 24.8 %collective-permute-start.5 = (bf16[384,256]{1,0:T(8,128)(2,1)S(1)}, bf16[384,256]{1,0:T(8,128)(2,1)S(1)}, u32[]{:S(2)}, u32[]{:S(2)}) collective-permute-start(bf16[384,256]{1,0:T(8,128)(2,1)S(1)} %get-tuple-element.48), channel_id=1, source_target_pairs={{0,3},{1,2},{2,1},{3,0},{4,7},{5,6},{6,5},{7,4},{8,11},{9,10},{10,... | collective-permute-start | bytes 589832 | tf_op jit(solution)/shard_map/ppermute | solution.py:351
  32.3 44.9 %copy-start.7 = (bf16[384,256]{1,0:T(8,128)(2,1)}, bf16[384,256]{1,0:T(8,128)(2,1)S(1)}, u32[]{:S(2)}) copy-start(bf16[384,256]{1,0:T(8,128)(2,1)S(1)} %collective-permute-done.3.refs_13_.refs_10_.refs_9_) | copy-start | bytes 589828
  34.8 42.5 %copy-start.8 = (bf16[384,256]{1,0:T(8,128)(2,1)}, bf16[384,256]{1,0:T(8,128)(2,1)S(1)}, u32[]{:S(2)}) copy-start(bf16[384,256]{1,0:T(8,128)(2,1)S(1)} %collective-permute-done.4.refs_11_.refs_8_.refs_7_) | copy-start | bytes 589828
  34.8 42.5 %copy-start.9 = (bf16[384,256]{1,0:T(8,128)(2,1)}, bf16[384,256]{1,0:T(8,128)(2,1)S(1)}, u32[]{:S(2)}) copy-start(bf16[384,256]{1,0:T(8,128)(2,1)S(1)} %collective-permute-done.5.refs_9_.refs_6_.refs_5_) | copy-start | bytes 589828
  34.8 42.5 %copy-start.13 = (bf16[128,3072]{1,0:T(8,128)(2,1)}, bf16[128,3072]{1,0:T(8,128)(2,1)S(1)}, u32[]{:S(2)}) copy-start(bf16[128,3072]{1,0:T(8,128)(2,1)S(1)} %collective-permute-done.1.refs_2_) | copy-start | bytes 2359300
  34.8 40.9 %copy-start.14 = (bf16[128,3072]{1,0:T(8,128)(2,1)}, bf16[128,3072]{1,0:T(8,128)(2,1)S(1)}, u32[]{:S(2)}) copy-start(bf16[128,3072]{1,0:T(8,128)(2,1)S(1)} %collective-permute-done.refs_1_) | copy-start | bytes 2359300
  34.8 40.9 %collective-permute-start.6 = (bf16[128,3072]{1,0:T(8,128)(2,1)S(1)}, bf16[128,3072]{1,0:T(8,128)(2,1)}, u32[]{:S(2)}, u32[]{:S(2)}) collective-permute-start(bf16[128,3072]{1,0:T(8,128)(2,1)S(1)} %collective-permute-done.refs_1_), channel_id=1, source_target_pairs={{0,2},{2,4},{4,6},{6,7},{7,5},{5,3},{3,1},{1,0},{8,9},{10,8},{12,1... | collective-permute-start | bytes 2359304 | tf_op jit(solution)/shard_map/ppermute | solution.py:336
  36.8 38.9 %collective-permute-start.7 = (bf16[128,3072]{1,0:T(8,128)(2,1)S(1)}, bf16[128,3072]{1,0:T(8,128)(2,1)}, u32[]{:S(2)}, u32[]{:S(2)}) collective-permute-start(bf16[128,3072]{1,0:T(8,128)(2,1)S(1)} %collective-permute-done.1.refs_2_), channel_id=1, source_target_pairs={{0,1},{2,0},{4,2},{6,4},{7,6},{5,7},{3,5},{1,3},{8,10},{10,12},{12... | collective-permute-start | bytes 2359304 | tf_op jit(solution)/shard_map/ppermute | solution.py:336
  42.0 29.4 %collective-permute-start.8 = (bf16[384,256]{1,0:T(8,128)(2,1)S(1)}, bf16[384,256]{1,0:T(8,128)(2,1)S(1)}, u32[]{:S(2)}, u32[]{:S(2)}) collective-permute-start(bf16[384,256]{1,0:T(8,128)(2,1)S(1)} %get-tuple-element.51), channel_id=1, source_target_pairs={{0,6},{1,7},{2,4},{3,5},{4,2},{5,3},{6,0},{7,1},{8,14},{9,15},{10,... | collective-permute-start | bytes 589832 | tf_op jit(solution)/shard_map/ppermute | solution.py:351
  44.1 31.5 %collective-permute-start.9 = (bf16[384,256]{1,0:T(8,128)(2,1)S(1)}, bf16[384,256]{1,0:T(8,128)(2,1)S(1)}, u32[]{:S(2)}, u32[]{:S(2)}) collective-permute-start(bf16[384,256]{1,0:T(8,128)(2,1)S(1)} %get-tuple-element.52), channel_id=1, source_target_pairs={{0,4},{1,5},{2,6},{3,7},{4,0},{5,1},{6,2},{7,3},{8,12},{9,13},{10,... | collective-permute-start | bytes 589832 | tf_op jit(solution)/shard_map/ppermute | solution.py:351
  47.0 28.7 %collective-permute-start.10 = (bf16[384,256]{1,0:T(8,128)(2,1)S(1)}, bf16[384,256]{1,0:T(8,128)(2,1)S(1)}, u32[]{:S(2)}, u32[]{:S(2)}) collective-permute-start(bf16[384,256]{1,0:T(8,128)(2,1)S(1)} %get-tuple-element.53), channel_id=1, source_target_pairs={{0,2},{1,3},{2,0},{3,1},{4,6},{5,7},{6,4},{7,5},{8,10},{9,11},{10,... | collective-permute-start | bytes 589832 | tf_op jit(solution)/shard_map/ppermute | solution.py:351
  71.5 5.8 %copy-start.10 = (bf16[384,256]{1,0:T(8,128)(2,1)}, bf16[384,256]{1,0:T(8,128)(2,1)S(1)}, u32[]{:S(2)}) copy-start(bf16[384,256]{1,0:T(8,128)(2,1)S(1)} %collective-permute-done.8.refs_12_.refs_9_.refs_8_) | copy-start | bytes 589828
  75.7 1.6 copy-start.11
  75.7 1.6 copy-start.12
  75.7 19.5 %collective-permute-start.11 = (bf16[128,3072]{1,0:T(8,128)(2,1)}, bf16[128,3072]{1,0:T(8,128)(2,1)S(1)}, u32[]{:S(2)}, u32[]{:S(2)}) collective-permute-start(bf16[128,3072]{1,0:T(8,128)(2,1)} %collective-permute-done.6.refs_3_), channel_id=1, source_target_pairs={{0,2},{2,4},{4,6},{6,7},{7,5},{5,3},{3,1},{1,0},{8,9},{10,8},{12,1... | collective-permute-start | bytes 2359304 | tf_op jit(solution)/shard_map/ppermute | solution.py:336
  75.8 21.0 %collective-permute-start.12 = (bf16[128,3072]{1,0:T(8,128)(2,1)}, bf16[128,3072]{1,0:T(8,128)(2,1)S(1)}, u32[]{:S(2)}, u32[]{:S(2)}) collective-permute-start(bf16[128,3072]{1,0:T(8,128)(2,1)} %collective-permute-done.7.refs_4_), channel_id=1, source_target_pairs={{0,1},{2,0},{4,2},{6,4},{7,6},{5,7},{3,5},{1,3},{8,10},{10,12},{12... | collective-permute-start | bytes 2359304 | tf_op jit(solution)/shard_map/ppermute | solution.py:336
  95.2 3.4 %copy-start.3 = (bf16[128,3072]{1,0:T(8,128)(2,1)}, bf16[128,3072]{1,0:T(8,128)(2,1)S(1)}, u32[]{:S(2)}) copy-start(bf16[128,3072]{1,0:T(8,128)(2,1)S(1)} %collective-permute-done.11.refs_0_.refs_2_) | copy-start | bytes 2359300
  96.8 1.8 %copy-start.4 = (bf16[128,3072]{1,0:T(8,128)(2,1)}, bf16[128,3072]{1,0:T(8,128)(2,1)S(1)}, u32[]{:S(2)}) copy-start(bf16[128,3072]{1,0:T(8,128)(2,1)S(1)} %collective-permute-done.12.refs_1_.refs_3_) | copy-start | bytes 2359300
  96.8 11.1 %collective-permute-start.13 = (bf16[128,3072]{1,0:T(8,128)(2,1)S(1)}, bf16[128,3072]{1,0:T(8,128)(2,1)S(1)}, u32[]{:S(2)}, u32[]{:S(2)}) collective-permute-start(bf16[128,3072]{1,0:T(8,128)(2,1)S(1)} %collective-permute-done.11.refs_0_.refs_2_), channel_id=1, source_target_pairs={{0,2},{2,4},{4,6},{6,7},{7,5},{5,3},{3,1},{1,0},{8,9},{10,8},{12,1... | collective-permute-start | bytes 2359304 | tf_op jit(solution)/shard_map/ppermute | solution.py:336
  107.9 0.9 copy-start.5
  116.1 50.0 %all-to-all-start = ((bf16[8,384,256]{2,1,0:T(8,128)(2,1)}), bf16[8,384,256]{2,1,0:T(8,128)(2,1)S(1)}, u32[]{:S(2)}, u32[]{:S(2)}) async-start(bf16[8,384,256]{2,1,0:T(8,128)(2,1)} %attend.5), calls=%async_computation | async-start | bytes 3145728 | tf_op jit(solution)/shard_map/all_to_all | solution.py:441
  127.6 3.9 %collective-permute-start.14 = (bf16[2,32,3072]{2,1,0:T(8,128)(2,1)}, bf16[2,32,3072]{2,1,0:T(8,128)(2,1)S(1)}, u32[]{:S(2)}, u32[]{:S(2)}) collective-permute-start(bf16[2,32,3072]{2,1,0:T(8,128)(2,1)} %get-tuple-element.80), channel_id=1, source_target_pairs={{0,8},{8,0},{16,24},{24,16},{1,9},{9,1},{17,25},{25,17},{2,10},{10... | collective-permute-start | bytes 1179656 | tf_op jit(solution)/shard_map/ppermute | solution.py:351
  129.8 10.9 %collective-permute-start.15 = (bf16[2,32,3072]{2,1,0:T(8,128)(2,1)}, bf16[2,32,3072]{2,1,0:T(8,128)(2,1)S(1)}, u32[]{:S(2)}, u32[]{:S(2)}) collective-permute-start(bf16[2,32,3072]{2,1,0:T(8,128)(2,1)} %get-tuple-element.81), channel_id=1, source_target_pairs={{0,16},{8,24},{16,0},{24,8},{1,17},{9,25},{17,1},{25,9},{2,18},{10... | collective-permute-start | bytes 1179656 | tf_op jit(solution)/shard_map/ppermute | solution.py:351
  131.0 18.5 %collective-permute-start.16 = (bf16[2,32,3072]{2,1,0:T(8,128)(2,1)}, bf16[2,32,3072]{2,1,0:T(8,128)(2,1)S(1)}, u32[]{:S(2)}, u32[]{:S(2)}) collective-permute-start(bf16[2,32,3072]{2,1,0:T(8,128)(2,1)} %get-tuple-element.82), channel_id=1, source_target_pairs={{0,24},{8,16},{16,8},{24,0},{1,25},{9,17},{17,9},{25,1},{2,26},{10... | collective-permute-start | bytes 1179656 | tf_op jit(solution)/shard_map/ppermute | solution.py:351
  149.5 1.0 copy-start.2
  152.0 10.8 %collective-permute-start.18 = (bf16[2,32,3072]{2,1,0:T(8,128)(2,1)S(1)}, bf16[2,32,3072]{2,1,0:T(8,128)(2,1)S(1)}, u32[]{:S(2)}, u32[]{:S(2)}) collective-permute-start(bf16[2,32,3072]{2,1,0:T(8,128)(2,1)S(1)} %get-tuple-element.83.refs_0_), channel_id=1, source_target_pairs={{0,16},{8,24},{16,0},{24,8},{1,17},{9,25},{17,1},{25,9},{2,18},{10... | collective-permute-start | bytes 1179656 | tf_op jit(solution)/shard_map/ppermute | solution.py:480
  153.2 10.3 %collective-permute-start.17 = (bf16[2,32,3072]{2,1,0:T(8,128)(2,1)S(1)}, bf16[2,32,3072]{2,1,0:T(8,128)(2,1)S(1)}, u32[]{:S(2)}, u32[]{:S(2)}) collective-permute-start(bf16[2,32,3072]{2,1,0:T(8,128)(2,1)S(1)} %get-tuple-element.83.refs_0_), channel_id=1, source_target_pairs={{0,8},{8,0},{16,24},{24,16},{1,9},{9,1},{17,25},{25,17},{2,10},{10... | collective-permute-start | bytes 1179656 | tf_op jit(solution)/shard_map/ppermute | solution.py:480
  162.8 2.1 %collective-permute-start.19 = (bf16[2,32,3072]{2,1,0:T(8,128)(2,1)S(1)}, bf16[2,32,3072]{2,1,0:T(8,128)(2,1)S(1)}, u32[]{:S(2)}, u32[]{:S(2)}) collective-permute-start(bf16[2,32,3072]{2,1,0:T(8,128)(2,1)S(1)} %collective-permute-done.18.refs_2_), channel_id=1, source_target_pairs={{0,8},{8,0},{16,24},{24,16},{1,9},{9,1},{17,25},{25,17},{2,10},{10... | collective-permute-start | bytes 1179656 | tf_op jit(solution)/shard_map/ppermute | solution.py:480

commit v4 on v3

--- a/solution.py
+++ b/solution.py
@@ -8,8 +8,9 @@
 from jax.experimental.pallas import tpu as pltpu
 from jax.sharding import PartitionSpec as P
 
-SMALL, LARGE = 16 * 1024 * 1024, 60 * 1024 * 1024
+SMALL, LARGE = 16 * 1024 * 1024, 63 * 1024 * 1024
 F32 = jnp.float32
+HEAVY = 10**13, 10**13, 10**13
 BF16 = jnp.bfloat16
 
 
@@ -58,8 +59,28 @@
         outs[k][...] = parts[me ^ k]
 
 
-def unpack_kernel(n, blocks, out_ref):
-    out_ref[...] = jnp.concatenate([blocks[d] for d in range(n)], axis=1).reshape(out_ref.shape)
+def unpack_kernel(n, queries_ref, far_ref, others_ref, out_ref, blocks, far_all, rows, sems):
+    tokens = far_ref.shape[0]
+    me = lax.axis_index("seq")
+    spans = [pl.ds(i * tokens, tokens) for i in range(3)]
+    copies = fetch(
+        [(queries_ref, blocks.at[:, spans[0]]), (far_ref, far_all)]
+        + [(others_ref.at[:, spans[i]], blocks.at[:, spans[i + 1]]) for i in range(2)],
+        sems,
+    )
+    copies.pop(0).wait()
+    leaving = []
+    for i, copy in enumerate(copies):
+        copy.wait()
+        here = slice(i * tokens, (i + 1) * tokens)
+        if i == 0:
+            far_place = ring_member(lax.rem(ring_place(me, n) + n // 2, n), n)
+            blocks[far_place, here] = far_all[...]
+        joined = jnp.concatenate([blocks[d, here] for d in range(n)], axis=1)
+        rows[here] = joined.reshape(tokens, *rows.shape[1:])
+        leaving += fetch([(rows.at[spans[i]], out_ref.at[spans[i]])], sems, 4 + i)
+    for copy in leaving:
+        copy.wait()
 
 
 def fetch(copies, sems, first=0):
@@ -80,7 +101,7 @@
     return copies
 
 
-def attend_kernel(n, heads_here, per_group, groups, first, earlier, far, mask_ref, *refs):
+def attend_kernel(n, heads_here, per_group, groups, first, earlier, far, mask_ref, *refs, beside=None):
     refs = list(refs)
     count = sum(len(g) for g in groups)
     take = lambda m: [refs.pop(0) for _ in range(m)]
@@ -91,22 +112,26 @@
     (mom_ref,) = take(1) if first else [None]
     query_parts = [] if earlier is None else take(len(earlier))
     if far:
-        far_probs_ref, far_att_ref, query_ref, grads = take(4)
+        far_probs_ref, far_att_ref, query_out, grads_out = take(4)
     else:
         query_out, key_out, value_out, att_out = take(4)
     if first:
         far_probs_out, far_att_out, part_out = take(3)
-    q_all, k_all, v_all, cot_all, tile_all, w_all, key_all, value_all, sems = take(9)
+    qkv_all, cot_all, tile_all, w_all, key_all, value_all, sems = take(7)
     if far:
-        far_probs, far_att = take(2)
+        far_probs, far_att, grads = take(3)
     if first:
         (mom_all,) = take(1)
 
     me = lax.axis_index("seq")
     sign = 1 - 2 * lax.rem(lax.axis_index("dp"), 2)
-    tokens, wide = q_all.shape[1:]
+    wide = qkv_all.shape[2]
+    tokens = qkv_all.shape[1] // 3
     size = wide // heads_here
     length = n * tokens
+    queries_of = lambda ids, cols: jnp.concatenate([qkv_all[t, 0:tokens, cols] for t in ids], axis=0)
+    keys_of = lambda cols: qkv_all[:, tokens : 2 * tokens, cols].reshape(length, size)
+    values_of = lambda cols: qkv_all[:, 2 * tokens :, cols].reshape(length, size)
     inv_root = 1.0 / math.sqrt(size)
     place = ring_place(me, n)
     tile_of = lambda offset: ring_member(lax.rem(place + sign * offset + n, n), n)
@@ -119,26 +144,20 @@
         return fetch(copies, sems, used - len(copies))
 
     w_copy, *tile_copies = start([(w_ref, w_all), *rows_of(tiles, tile_all)])
-    block_copies = start(
-        [
-            (block.at[pl.ds(i * tokens, tokens)], target.at[me ^ k])
-            for k, block in enumerate(blocks)
-            for i, target in enumerate((q_all, k_all, v_all))
-        ]
-    )
+    att_copies = start([(far_att_ref, far_att)] if far else [])
+    work = beside(tile_all, far_att) if beside else None
+    far_copies = start([(far_probs_ref, far_probs)] if far else [])
+    block_copies = start([(block, qkv_all.at[me ^ k]) for k, block in enumerate(blocks)])
     carried_copies = start(list(zip(carried, (key_all, value_all))))
     mom_copies = start([(mom_ref, mom_all)] if first else [])
-    far_copies = start([(far_probs_ref, far_probs), (far_att_ref, far_att)] if far else [])
-    if far:
-        part_copies = start([(query_ref, grads.at[:, pl.ds(0, tokens)])])
-    else:
-        part_copies = start(
-            [
-                (part.at[pl.ds(i * tokens, tokens)], query_out.at[tile_of(offset)])
-                for part, offsets in zip(query_parts, earlier or [])
-                for i, offset in enumerate(offsets)
-            ]
-        )
+    part_copies = start(
+        [
+            (part.at[pl.ds(i * tokens, tokens)], query_out.at[tile_of(offset)])
+            for part, offsets in zip(query_parts, earlier or [])
+            for i, offset in enumerate(offsets)
+        ]
+    )
+    leaving = []
     if earlier is not None:
         query_out[tile_of(n // 2)] = jnp.zeros((tokens, wide), BF16)
 
@@ -158,13 +177,10 @@
             for t in ids
         ]
         bias = jnp.concatenate([jnp.broadcast_to(b, (tokens, length)) for b in bias], axis=0)
-        query = jnp.concatenate([q_all[t, :, cols] for t in ids], axis=0)
-        keys = k_all[:, :, cols].reshape(length, size)
-        values = v_all[:, :, cols].reshape(length, size)
-        scores = dot_nt(query, keys) * inv_root + bias
+        scores = dot_nt(queries_of(ids, cols), keys_of(cols)) * inv_root + bias
         expo = jnp.exp(scores - jnp.max(scores, axis=1, keepdims=True))
         probs = expo * (1.0 / jnp.sum(expo, axis=1, keepdims=True))
-        att = jnp.dot(probs.astype(BF16), values, preferred_element_type=F32).astype(BF16)
+        att = jnp.dot(probs.astype(BF16), values_of(cols), preferred_element_type=F32).astype(BF16)
         return probs, att
 
     w_copy.wait()
@@ -177,6 +193,9 @@
             copy.wait()
         tile_copies = tile_copies[len(ids) :]
         cot_all[rows] = dot_nt(tile_all[rows], w_all[...]).astype(BF16)
+        if work:
+            att_copies.pop().wait()
+            leaving += work()
         if number == 0:
             for copy in block_copies + far_copies:
                 copy.wait()
@@ -188,24 +207,18 @@
                 probs, att = forward(ids, h)
                 att_out[rows, cols] = att
             probs_b = probs.astype(BF16)
-            query = jnp.concatenate([q_all[t, :, cols] for t in ids], axis=0)
-            keys = k_all[:, :, cols].reshape(length, size)
-            values = v_all[:, :, cols].reshape(length, size)
             cot = cot_all[rows, cols]
             delta = jnp.sum(cot.astype(F32) * att.astype(F32), axis=1, keepdims=True)
-            dprobs = dot_nt(cot, values)
+            dprobs = dot_nt(cot, values_of(cols))
             dscores = (probs * (dprobs - delta)).astype(BF16)
-            query_grad = (jnp.dot(dscores, keys, preferred_element_type=F32) * inv_root).astype(BF16)
-            if far:
-                if h == 0:
-                    part_copies.pop().wait()
-                grads[ids[0], 0:tokens, cols] = query_grad
-            elif earlier is None:
+            query_grad = jnp.dot(dscores, keys_of(cols), preferred_element_type=F32) * inv_root
+            query_grad = query_grad.astype(BF16)
+            if earlier is None:
                 query_out[rows, cols] = query_grad
             else:
                 for i, t in enumerate(ids):
                     query_out[t, :, cols] = query_grad[i * tokens : (i + 1) * tokens]
-            key_sum = dot_tn(dscores, query)
+            key_sum = dot_tn(dscores, queries_of(ids, cols))
             value_sum = dot_tn(probs_b, cot)
             if number == 0 and h == 0:
                 for copy in carried_copies:
@@ -214,10 +227,12 @@
                 key_sum = key_all[:, cols] + key_sum
                 value_sum = value_all[:, cols] + value_sum
             if far:
-                grads[:, tokens : 2 * tokens, cols] = (
+                grads[:, 0:tokens, cols] = (
                     (key_sum * inv_root).astype(BF16).reshape(n, tokens, size)
                 )
-                grads[:, 2 * tokens :, cols] = value_sum.astype(BF16).reshape(n, tokens, size)
+                grads[:, tokens:, cols] = value_sum.astype(BF16).reshape(n, tokens, size)
+                span = pl.ds(h * size, size)
+                leaving += start([(grads.at[:, :, span], grads_out.at[:, :, span])])
             elif number == len(groups) - 1:
                 key_out[:, cols] = key_sum
                 value_out[:, cols] = value_sum
@@ -234,61 +249,75 @@
         wide_d = mom_all.shape[1]
         chunk = math.gcd(wide_d, 512)
         att = att_out[...].T
-        leaving = []
         for c in range(0, wide_d, chunk):
             cols = slice(c, c + chunk)
             grad = jnp.dot(att, tile_all[:, cols], preferred_element_type=F32)
             mom_all[:, cols] = 0.9 * mom_all[:, cols] + 0.1 * grad
             span = pl.ds(c, chunk)
             leaving += start([(mom_all.at[:, span], part_out.at[:, span])])
-        for copy in leaving:
-            copy.wait()
-    for copy in part_copies:
+    for copy in part_copies + leaving:
         copy.wait()
 
 
-def worker_kernel(heads_here, workers, part_count, tile_count, *refs):
-    att_parts, tiles = refs[:part_count], refs[part_count : part_count + tile_count]
-    part_ref, error_ref, *refs = refs[part_count + tile_count :]
-    outs, (sent_ref, att_all, tile_all, mom_all, error_all, sems) = refs[:workers], refs[workers:]
-    me = lax.axis_index("dp")
-    wide, wide_d = mom_all.shape
-    size = wide // heads_here
-    chunk = math.gcd(wide_d, 512)
-    used = part_count + tile_count + heads_here
-    spans = [pl.ds(h * size, size) for h in range(heads_here)]
-    copies = fetch([*rows_of(att_parts, att_all), *rows_of(tiles, tile_all)], sems)
-    mom_copies = fetch([(part_ref.at[s], mom_all.at[s]) for s in spans], sems, len(copies))
-    for copy in copies:
-        copy.wait()
-    att = att_all[...].T
-    block = size // workers
-    leaving = []
-    for h in range(heads_here):
-        rows = slice(h * size, (h + 1) * size)
-        mom_copies[h].wait()
-        total = jnp.zeros((size, chunk), F32)
-        for c in range(0, wide_d, chunk):
-            cols = slice(c, c + chunk)
-            grad = jnp.dot(att[rows], tile_all[:, cols], preferred_element_type=F32)
-            mom = mom_all[rows, cols] + 0.1 * grad
-            mom_all[rows, cols] = mom
-            total = total + jnp.abs(mom)
-        scale = jnp.sum(total, keepdims=True) * (1.0 / (size * wide_d)) + 1e-06
-        inverse = 1.0 / scale
-        for c in range(0, wide_d, chunk):
-            cols = slice(c, c + chunk)
-            mom = mom_all[rows, cols]
-            sent = (scale * jnp.tanh(mom * inverse)).astype(BF16)
-            sent_ref[h, :, cols] = sent
-            error_all[rows, cols] = mom - sent.astype(F32)
-        going = [(error_all.at[spans[h]], error_ref.at[spans[h]])]
-        for k in range(workers):
-            start = pl.multiple_of((me ^ k) * block, block)
-            going.append((sent_ref.at[h, pl.ds(start, block)], outs[k].at[h]))
-        leaving += fetch(going, sems, used + h * len(going))
-    for copy in leaving:
-        copy.wait()
+def tail_kernel(n, heads_here, per_group, workers, tile_count, *refs):
+    refs = list(refs)
+    take = lambda m: [refs.pop(0) for _ in range(m)]
+    attend_in = take(1 + 2 + n + 2 + 2)
+    att_parts, tiles, (part_ref,) = take(tile_count // 2), take(tile_count), take(1)
+    attend_out, (error_ref,), outs = take(2), take(1), take(workers)
+    sent_ref, att_all, more_tiles, mom_all, error_all, worker_sems, *attend_scratch = refs
+
+    def beside(far_tile, far_att):
+        wide, wide_d = mom_all.shape
+        size = wide // heads_here
+        chunk = math.gcd(wide_d, 512)
+        block = size // workers
+        spans = [pl.ds(h * size, size) for h in range(heads_here)]
+        copies = [*rows_of(att_parts, att_all), *rows_of(tiles, more_tiles)]
+        copies = fetch(copies, worker_sems)
+        mom_copies = fetch(
+            [(part_ref.at[s], mom_all.at[s]) for s in spans], worker_sems, len(copies)
+        )
+        used = len(copies) + heads_here
+
+        def work():
+            for copy in copies:
+                copy.wait()
+            att, late = att_all[...].T, far_att[...].T
+            leaving = []
+            for h in range(heads_here):
+                rows = slice(h * size, (h + 1) * size)
+                mom_copies[h].wait()
+                total = jnp.zeros((size, chunk), F32)
+                for c in range(0, wide_d, chunk):
+                    cols = slice(c, c + chunk)
+                    grad = jnp.dot(att[rows], more_tiles[:, cols], preferred_element_type=F32)
+                    grad += jnp.dot(late[rows], far_tile[:, cols], preferred_element_type=F32)
+                    mom = mom_all[rows, cols] + 0.1 * grad
+                    mom_all[rows, cols] = mom
+                    total = total + jnp.abs(mom)
+                scale = jnp.sum(total, keepdims=True) * (1.0 / (size * wide_d)) + 1e-06
+                inverse = 1.0 / scale
+                for c in range(0, wide_d, chunk):
+                    cols = slice(c, c + chunk)
+                    mom = mom_all[rows, cols]
+                    sent = (scale * jnp.tanh(mom * inverse)).astype(BF16)
+                    sent_ref[h, :, cols] = sent
+                    error_all[rows, cols] = mom - sent.astype(F32)
+                me = lax.axis_index("dp")
+                going = [(error_all.at[spans[h]], error_ref.at[spans[h]])]
+                for k in range(workers):
+                    start = pl.multiple_of((me ^ k) * block, block)
+                    going.append((sent_ref.at[h, pl.ds(start, block)], outs[k].at[h]))
+                leaving.extend(fetch(going, worker_sems, used + h * len(going)))
+            return leaving
+
+        return work
+
+    attend_kernel(
+        n, heads_here, per_group, [[n // 2]], False, None, True,
+        *attend_in, *attend_out, *attend_scratch, beside=beside,
+    )
 
 
 def server_kernel(workers, *refs):
@@ -357,30 +386,24 @@
     anywhere = pl.BlockSpec(memory_space=pl.ANY)
     length = n * tokens
 
-    def attend(groups, tiles, carried, earlier=None, parts=(), far=()):
+    def attend(groups, tiles, carried, earlier=None, parts=()):
         count = len(tiles)
         carried = carried or [momentum.reshape(wide, wide_d)]
         first = len(carried) == 1
-        operands = [tile_mask, *tiles, w_flat, *blocks, *carried, *parts, *far]
+        operands = [tile_mask, *tiles, w_flat, *blocks, *carried, *parts]
         sums = shape((length, wide), F32)
         rows = shape((count * tokens, wide), BF16)
         probs = shape((heads_here, tokens, length), F32)
         scratch = [
-            pltpu.VMEM((n, tokens, wide), BF16),
-            pltpu.VMEM((n, tokens, wide), BF16),
-            pltpu.VMEM((n, tokens, wide), BF16),
+            pltpu.VMEM((n, *packed_shape), BF16),
             pltpu.VMEM(rows.shape, BF16),
             pltpu.VMEM((count * tokens, wide_d), BF16),
             pltpu.VMEM((wide, wide_d), BF16),
             pltpu.VMEM(sums.shape, F32),
             pltpu.VMEM(sums.shape, F32),
-            pltpu.SemaphoreType.DMA((count + 8 + 4 * n + wide_d // math.gcd(wide_d, 512),)),
+            pltpu.SemaphoreType.DMA((count + 8 + 2 * n + wide_d // math.gcd(wide_d, 512),)),
         ]
-        if far:
-            outs = [shape((n, *packed_shape), BF16)]
-            scratch += [pltpu.VMEM(probs.shape, F32), pltpu.VMEM((tokens, wide), BF16)]
-        else:
-            outs = [rows, sums, sums, rows]
+        outs = [rows, sums, sums, rows]
         if earlier is not None:
             outs[0] = shape((n, tokens, wide), BF16)
         out_specs = [vmem] * len(outs)
@@ -389,11 +412,9 @@
             out_specs += [vmem, vmem, anywhere]
             scratch += [pltpu.VMEM((wide, wide_d), F32)]
         flops = count * (14 * tokens * length * wide + 2 * tokens * wide * wide_d)
-        if len(outs) == 1:
-            outs, out_specs = outs[0], vmem
         return pl.pallas_call(
             functools.partial(
-                attend_kernel, n, heads_here, per_group, groups, first, earlier, bool(far)
+                attend_kernel, n, heads_here, per_group, groups, first, earlier, False
             ),
             in_specs=[smem] + [anywhere] * (len(operands) - 1),
             out_specs=out_specs,
@@ -437,33 +458,52 @@
             listed.append(sum(groups, []))
             queries.append(query)
             groups, fresh = [[-(s + 1), s + 1]], [fore, aft]
-    grads = attend([[half]], [far], sums, far=(far_probs, far_att, query))
-    returned = lax.all_to_all(grads, "seq", split_axis=0, concat_axis=0, tiled=True)
-
-    atts.append(far_att)
-    worker_tiles = [*tiles, far]
-    worker_rows = len(worker_tiles) * tokens
-    worker_copies = len(atts) + len(worker_tiles) + heads_here * (workers + 2)
-    error, *sent = pl.pallas_call(
-        functools.partial(worker_kernel, heads_here, workers, len(atts), len(worker_tiles)),
-        in_specs=[anywhere] * (len(atts) + len(worker_tiles) + 1),
-        out_specs=[anywhere] * (1 + workers),
-        out_shape=[shape((wide, wide_d), F32)]
-        + [shape((heads_here, size // workers, wide_d), BF16)] * workers,
+    query_back = lax.all_to_all(query, "seq", split_axis=0, concat_axis=0, tiled=True)
+    tile_count = len(tiles)
+    rows = (tokens, wide)
+    probs_shape = far_probs.shape
+    tail_in = [tile_mask, far, w_flat, *blocks, *sums, far_probs, far_att, *atts, *tiles, part]
+    far_query, grads, error, *sent = pl.pallas_call(
+        functools.partial(tail_kernel, n, heads_here, per_group, workers, tile_count),
+        in_specs=[smem] + [anywhere] * (len(tail_in) - 1),
+        out_specs=[vmem] + [anywhere] * (2 + workers),
+        out_shape=[
+            shape(rows, BF16),
+            shape((n, 2 * tokens, wide), BF16),
+            shape((wide, wide_d), F32),
+            *[shape((heads_here, size // workers, wide_d), BF16)] * workers,
+        ],
         scratch_shapes=[
             pltpu.VMEM((heads_here, size, wide_d), BF16),
-            pltpu.VMEM((worker_rows, wide), BF16),
-            pltpu.VMEM((worker_rows, wide_d), BF16),
+            pltpu.VMEM((tile_count * tokens, wide), BF16),
+            pltpu.VMEM((tile_count * tokens, wide_d), BF16),
             pltpu.VMEM((wide, wide_d), F32),
             pltpu.VMEM((wide, wide_d), F32),
-            pltpu.SemaphoreType.DMA((worker_copies,)),
+            pltpu.SemaphoreType.DMA((2 * tile_count + heads_here * (workers + 2),)),
+            pltpu.VMEM((n, *packed_shape), BF16),
+            pltpu.VMEM(rows, BF16),
+            pltpu.VMEM((tokens, wide_d), BF16),
+            pltpu.VMEM((wide, wide_d), BF16),
+            pltpu.VMEM((length, wide), F32),
+            pltpu.VMEM((length, wide), F32),
+            pltpu.SemaphoreType.DMA((n + 8 + heads_here,)),
+            pltpu.VMEM(probs_shape, F32),
+            pltpu.VMEM(rows, BF16),
+            pltpu.VMEM((n, 2 * tokens, wide), BF16),
         ],
         compiler_params=params(LARGE),
-        cost_estimate=cost(2 * worker_rows * wide * wide_d, 2**24),
-        name="worker",
-    )(*atts, *worker_tiles, part)
+        cost_estimate=cost(HEAVY[2], 2**24),
+        name="tail",
+    )(*tail_in)
+    across = [(ring[i], ring[(i + half) % n]) for i in range(n)]
+    far_back = lax.ppermute(far_query, "seq", across)
+    other_back = lax.all_to_all(grads, "seq", split_axis=0, concat_axis=0, tiled=True)
+
     received = [sent[0]] + [send(sent, k, "dp") for k in range(1, workers)]
 
+    query_back, far_back, *received = lax.optimization_barrier(
+        [query_back, far_back, *received]
+    )
     synced, server_error = pl.pallas_call(
         functools.partial(server_kernel, workers),
         out_shape=[
@@ -471,7 +511,7 @@
             shape((heads_here, size // workers, wide_d), F32),
         ],
         compiler_params=params(SMALL),
-        cost_estimate=cost(0, 2**22),
+        cost_estimate=cost(HEAVY[0], 2**22),
         name="server",
     )(*received)
     gathered = [synced] + [None] * (workers - 1)
@@ -482,10 +522,18 @@
     grad_rows = pl.pallas_call(
         functools.partial(unpack_kernel, n),
         out_shape=shape((3 * tokens, heads, size), BF16),
+        in_specs=[anywhere] * 3,
+        out_specs=anywhere,
+        scratch_shapes=[
+            pltpu.VMEM((n, *packed_shape), BF16),
+            pltpu.VMEM((tokens, wide), BF16),
+            pltpu.VMEM((3 * tokens, heads, size), BF16),
+            pltpu.SemaphoreType.DMA((7,)),
+        ],
         compiler_params=params(SMALL),
         cost_estimate=cost(0, 4 * qkv.size),
         name="unpack",
-    )(returned)
+    )(query_back, far_back, other_back)
     synced_momentum = pl.pallas_call(
         functools.partial(join_kernel, workers),
         out_shape=shape((heads_here, size, wide_d), BF16),

time: 169 us -> 164 us (0.970)
  waiting for transfers between devices: 69.3 us -> 61.4 us
  starting transfers between devices: 48.3 us -> 54.4 us
  Pallas kernels: 45.2 us -> 42.5 us
  local copies, waits for them, and re-layouts: 4.01 us -> 2.15 us
    ppermute x10, waiting for transfers between devices: 56.9 us -> 48.7 us  [send(): lax.ppermute(blocks[k], axis, [(i, i ^ k) for i in range(len(blocks))])]
    pallas_call x3 -> x2, Pallas kernels: 34.4 us -> 26.9 us  [attend(): pl.pallas_call(functools.partial(attend_kernel, n, heads_here, per_group,...]
    all_to_all x0 -> x1, starting transfers between devices: none -> 4.21 us  [body(): lax.all_to_all(query, 'seq', split_axis=0, concat_axis=0, tiled=True)]
    pallas_call x1, Pallas kernels: 5.98 us -> 10 us  [body(): pl.pallas_call(functools.partial(tail_kernel, n, heads_here, per_group, w...]
    ppermute x0 -> x1, starting transfers between devices: none -> 2.1 us  [body(): far_back = lax.ppermute(far_query, 'seq', across)]
    unnamed x30 -> x26, local copies, waits for them, and re-layouts: 4.01 us -> 2.15 us
  transfers between devices with their start and end apart: 21 -> 23, of which waited for: 11 -> 10; matrix products, arithmetic and copies ran while one was open for 0% -> 0% of each run, Pallas kernels for 22% -> 25%
where the time goes in v4:
time: 164 us; the launch traced here: 161 us
  waiting for transfers between devices  61.4 us (37%)
  starting transfers between devices  54.4 us (33%)
  Pallas kernels  42.5 us (26%)
  local copies, waits for them, and re-layouts  2.15 us (1%)
    ppermute x10, waiting for transfers between devices, send(): lax.ppermute(blocks[k], axis, [(i, i ^ k) for i in range(len(blocks))])  48.7 us
    ppermute x10, starting transfers between devices, send(): lax.ppermute(blocks[k], axis, [(i, i ^ k) for i in range(len(blocks))])  27.9 us
    pallas_call x2, Pallas kernels, attend(): pl.pallas_call(functools.partial(attend_kernel, n, heads_here, per_group,...  26.9 us
    ppermute x7, starting transfers between devices, around(): return lambda x: lax.ppermute(x, ('dp', 'seq'), pairs)  12 us
    ppermute x3, waiting for transfers between devices, body(): lax.ppermute(source, 'dp', [(i, i ^ step) for i in range(workers)])  10.9 us
    pallas_call x1, Pallas kernels, body(): pl.pallas_call(functools.partial(tail_kernel, n, heads_here, per_group, w...  10 us
    all_to_all x1, starting transfers between devices, body(): lax.all_to_all(grads, 'seq', split_axis=0, concat_axis=0, tiled=True)  6.21 us
    all_to_all x1, starting transfers between devices, body(): lax.all_to_all(query, 'seq', split_axis=0, concat_axis=0, tiled=True)  4.21 us
  transfers between devices with their start and end apart: 23, of which 10 were waited for; matrix products, arithmetic and copies ran while one was open for 0% of the time, Pallas kernels for 25%

profile of v4, /device:TPU:9, one launch (start us, length us, event | category | flops | bytes accessed | tf_op | source)
XLA Modules:
  0.0 161.5 jit_solution(17797939502351523741)
XLA Ops:
  0.6 1.3 collective-permute-start.1
  2.0 0.2 collective-permute-start
  2.2 1.4 copy-done
  3.6 0.5 pack.1
  4.1 0.0 copy-start.1
  4.1 0.7 copy-done.1
  4.8 1.2 collective-permute-start.2
  6.0 1.2 collective-permute-start.3
  7.3 1.9 %collective-permute-start.4 = (bf16[384,256]{1,0:T(8,128)(2,1)S(1)}, bf16[384,256]{1,0:T(8,128)(2,1)S(1)}, u32[]{:S(2)}, u32[]{:S(2)}) collective-permute-start(bf16[384,256]{1,0:T(8,128)(2,1)S(1)} %get-tuple-element.55), channel_id=1, source_target_pairs={{0,5},{1,4},{2,7},{3,6},{4,1},{5,0},{6,3},{7,2},{8,13},{9,12},{10,... | collective-permute-start | bytes 589832 | tf_op jit(solution)/shard_map/ppermute | solution.py:380
  9.2 0.8 collective-permute-done.2.refs_7_.refs_4_
  10.0 15.4 %collective-permute-start.5 = (bf16[384,256]{1,0:T(8,128)(2,1)S(1)}, bf16[384,256]{1,0:T(8,128)(2,1)S(1)}, u32[]{:S(2)}, u32[]{:S(2)}) collective-permute-start(bf16[384,256]{1,0:T(8,128)(2,1)S(1)} %get-tuple-element.56), channel_id=1, source_target_pairs={{0,3},{1,2},{2,1},{3,0},{4,7},{5,6},{6,5},{7,4},{8,11},{9,10},{10,... | collective-permute-start | bytes 589832 | tf_op jit(solution)/shard_map/ppermute | solution.py:380
  25.4 6.9 %collective-permute-done.3.refs_13_.refs_10_ = bf16[384,256]{1,0:T(8,128)(2,1)S(1)} collective-permute-done((bf16[384,256]{1,0:T(8,128)(2,1)S(1)}, bf16[384,256]{1,0:T(8,128)(2,1)S(1)}, u32[]{:S(2)}, u32[]{:S(2)}) %collective-permute-start.3) | collective-permute-done | bytes 196640 | tf_op jit(solution)/shard_map/ppermute | solution.py:380
  32.3 2.4 %collective-permute-done.4.refs_11_.refs_8_ = bf16[384,256]{1,0:T(8,128)(2,1)S(1)} collective-permute-done((bf16[384,256]{1,0:T(8,128)(2,1)S(1)}, bf16[384,256]{1,0:T(8,128)(2,1)S(1)}, u32[]{:S(2)}, u32[]{:S(2)}) %collective-permute-start.4) | collective-permute-done | bytes 196640 | tf_op jit(solution)/shard_map/ppermute | solution.py:380
  34.8 0.0 collective-permute-done.5.refs_9_.refs_6_
  34.8 0.0 collective-permute-done.1.refs_2_
  34.8 0.0 copy-start.11
  34.8 0.0 collective-permute-done.refs_1_
  34.8 0.0 copy-start.12
  34.8 2.0 %collective-permute-start.6 = (bf16[128,3072]{1,0:T(8,128)(2,1)S(1)}, bf16[128,3072]{1,0:T(8,128)(2,1)}, u32[]{:S(2)}, u32[]{:S(2)}) collective-permute-start(bf16[128,3072]{1,0:T(8,128)(2,1)S(1)} %collective-permute-done.refs_1_), channel_id=1, source_target_pairs={{0,2},{2,4},{4,6},{6,7},{7,5},{5,3},{3,1},{1,0},{8,9},{10,8},{12,1... | collective-permute-start | bytes 2359304 | tf_op jit(solution)/shard_map/ppermute | solution.py:365
  36.8 5.2 %collective-permute-start.7 = (bf16[128,3072]{1,0:T(8,128)(2,1)S(1)}, bf16[128,3072]{1,0:T(8,128)(2,1)}, u32[]{:S(2)}, u32[]{:S(2)}) collective-permute-start(bf16[128,3072]{1,0:T(8,128)(2,1)S(1)} %collective-permute-done.1.refs_2_), channel_id=1, source_target_pairs={{0,1},{2,0},{4,2},{6,4},{7,6},{5,7},{3,5},{1,3},{8,10},{10,12},{12... | collective-permute-start | bytes 2359304 | tf_op jit(solution)/shard_map/ppermute | solution.py:365
  42.0 2.1 %collective-permute-start.8 = (bf16[384,256]{1,0:T(8,128)(2,1)S(1)}, bf16[384,256]{1,0:T(8,128)(2,1)S(1)}, u32[]{:S(2)}, u32[]{:S(2)}) collective-permute-start(bf16[384,256]{1,0:T(8,128)(2,1)S(1)} %get-tuple-element.59), channel_id=1, source_target_pairs={{0,6},{1,7},{2,4},{3,5},{4,2},{5,3},{6,0},{7,1},{8,14},{9,15},{10,... | collective-permute-start | bytes 589832 | tf_op jit(solution)/shard_map/ppermute | solution.py:380
  44.1 2.8 %collective-permute-start.9 = (bf16[384,256]{1,0:T(8,128)(2,1)S(1)}, bf16[384,256]{1,0:T(8,128)(2,1)S(1)}, u32[]{:S(2)}, u32[]{:S(2)}) collective-permute-start(bf16[384,256]{1,0:T(8,128)(2,1)S(1)} %get-tuple-element.60), channel_id=1, source_target_pairs={{0,4},{1,5},{2,6},{3,7},{4,0},{5,1},{6,2},{7,3},{8,12},{9,13},{10,... | collective-permute-start | bytes 589832 | tf_op jit(solution)/shard_map/ppermute | solution.py:380
  47.0 0.0 collective-permute-start.10
  47.0 24.5 %collective-permute-done.8.refs_12_.refs_9_ = bf16[384,256]{1,0:T(8,128)(2,1)S(1)} collective-permute-done((bf16[384,256]{1,0:T(8,128)(2,1)S(1)}, bf16[384,256]{1,0:T(8,128)(2,1)S(1)}, u32[]{:S(2)}, u32[]{:S(2)}) %collective-permute-start.8) | collective-permute-done | bytes 196640 | tf_op jit(solution)/shard_map/ppermute | solution.py:380
  71.5 4.2 %collective-permute-done.9.refs_10_.refs_7_ = bf16[384,256]{1,0:T(8,128)(2,1)S(1)} collective-permute-done((bf16[384,256]{1,0:T(8,128)(2,1)S(1)}, bf16[384,256]{1,0:T(8,128)(2,1)S(1)}, u32[]{:S(2)}, u32[]{:S(2)}) %collective-permute-start.9) | collective-permute-done | bytes 196640 | tf_op jit(solution)/shard_map/ppermute | solution.py:380
  75.7 0.0 collective-permute-done.10.refs_8_.refs_5_
  75.7 0.0 collective-permute-done.6.refs_3_
  75.7 0.0 copy-done.5
  75.7 0.0 collective-permute-done.7.refs_4_
  75.7 0.0 copy-done.6
  75.7 0.1 collective-permute-start.11
  75.8 1.4 collective-permute-start.12
  77.3 0.0 copy-done.9
  77.3 0.0 copy-done.12
  77.3 17.8 %attend.2 = (bf16[640,256]{1,0:T(8,128)(2,1)}, f32[1024,256]{1,0:T(8,128)}, f32[1024,256]{1,0:T(8,128)}, bf16[640,256]{1,0:T(8,128)(2,1)}, f32[2,128,1024]{2,1,0...) custom-call(s32[8,8,8]{2,1,0:T(8,128)} %refs_0_.1, bf16[128,3072]{1,0:T(8,128)(2,1)} %bitcast.16, ...), custom_call_target="tpu_custom_call" | custom-call | flops 3355443200 | bytes 41943040 | tf_op jit(solution)/shard_map/attend/pallas_call | solution.py:415
  95.1 0.0 collective-permute-done.11.refs_0_.refs_16_
  95.1 0.0 copy-start.3
  95.1 1.8 %collective-permute-done.12.refs_1_.refs_17_ = bf16[128,3072]{1,0:T(8,128)(2,1)} collective-permute-done((bf16[128,3072]{1,0:T(8,128)(2,1)}, bf16[128,3072]{1,0:T(8,128)(2,1)}, u32[]{:S(2)}, u32[]{:S(2)}) %collective-permute-start.12) | collective-permute-done | bytes 786464 | tf_op jit(solution)/shard_map/ppermute | solution.py:365
  96.9 1.7 %collective-permute-start.13 = (bf16[128,3072]{1,0:T(8,128)(2,1)S(1)}, bf16[128,3072]{1,0:T(8,128)(2,1)}, u32[]{:S(2)}, u32[]{:S(2)}) collective-permute-start(bf16[128,3072]{1,0:T(8,128)(2,1)S(1)} %collective-permute-done.11.refs_0_.refs_16_), channel_id=1, source_target_pairs={{0,2},{2,4},{4,6},{6,7},{7,5},{5,3},{3,1},{1,0},{8,9},{10,8},{12,1... | collective-permute-start | bytes 2359304 | tf_op jit(solution)/shard_map/ppermute | solution.py:365
  98.6 9.1 %attend.3 = (bf16[8,128,256]{2,1,0:T(8,128)(2,1)}, f32[1024,256]{1,0:T(8,128)}, f32[1024,256]{1,0:T(8,128)}, bf16[256,256]{1,0:T(8,128)(2,1)}) custom-call(s32[8,8,8]{2,1,0:T(8,128)} %refs_0_.1, bf16[128,3072]{1,0:T(8,128)(2,1)} %copy-done.3, bf16[128,3072]{1,0:T(8,128)(2,1)} %collective-permute-done.12.refs_1_.refs_17_, bf16[256,3072]{1,0:T(8,128)(2,1)} %bitcast.10, ...), custom_call_target="tpu_custom_call" | custom-call | flops 1342177280 | bytes 16777216 | tf_op jit(solution)/shard_map/attend/pallas_call | solution.py:415
  107.7 4.2 %all-to-all-start = ((bf16[8,128,256]{2,1,0:T(8,128)(2,1)}), bf16[8,128,256]{2,1,0:T(8,128)(2,1)}, u32[]{:S(2)}, u32[]{:S(2)}) async-start(bf16[8,128,256]{2,1,0:T(8,128)(2,1)} %get-tuple-element.80), calls=%async_computation | async-start | bytes 1048576 | tf_op jit(solution)/shard_map/all_to_all | solution.py:461
  111.9 0.0 collective-permute-done.13.refs_1_
  111.9 10.0 %tail.1 = (bf16[128,256]{1,0:T(8,128)(2,1)}, bf16[8,256,256]{2,1,0:T(8,128)(2,1)}, f32[256,3072]{1,0:T(8,128)}, bf16[2,32,3072]{2,1,0:T(8,128)(2,1)}, bf16[2,32,...) custom-call(s32[8,8,8]{2,1,0:T(8,128)} %refs_0_.1, ...), custom_call_target="tpu_custom_call" | custom-call | flops 9999999827968 | bytes 16777216 | tf_op jit(solution)/shard_map/tail/pallas_call | solution.py:466
  122.0 0.0 copy-start.2
  122.0 1.4 collective-permute-start.15
  123.4 1.3 collective-permute-start.16
  124.7 0.4 collective-permute-start.17
  125.1 2.1 %collective-permute-start.14 = (bf16[128,256]{1,0:T(8,128)(2,1)}, bf16[128,256]{1,0:T(8,128)(2,1)S(1)}, u32[]{:S(2)}, u32[]{:S(2)}) collective-permute-start(bf16[128,256]{1,0:T(8,128)(2,1)} %get-tuple-element.87), channel_id=1, source_target_pairs={{0,7},{2,5},{4,3},{6,1},{7,0},{5,2},{3,4},{1,6},{8,15},{10,13},{12... | collective-permute-start | bytes 196616 | tf_op jit(solution)/shard_map/ppermute | solution.py:499
  127.2 0.0 all-to-all-done.queries_ref
  127.2 6.2 %all-to-all-start.1 = ((bf16[8,256,256]{2,1,0:T(8,128)(2,1)}), bf16[8,256,256]{2,1,0:T(8,128)(2,1)}, u32[]{:S(2)}, u32[]{:S(2)}) async-start(bf16[8,256,256]{2,1,0:T(8,128)(2,1)} %get-tuple-element.94), calls=%async_computation.1 | async-start | bytes 2097152 | tf_op jit(solution)/shard_map/all_to_all | solution.py:500
  133.4 0.0 collective-permute-done.14.far_ref
  133.4 0.0 collective-permute-done.15.refs_1_
  133.4 0.9 collective-permute-done.16.refs_2_
  134.3 9.0 %collective-permute-done.17.refs_3_ = bf16[2,32,3072]{2,1,0:T(8,128)(2,1)S(1)} collective-permute-done((bf16[2,32,3072]{2,1,0:T(8,128)(2,1)}, bf16[2,32,3072]{2,1,0:T(8,128)(2,1)S(1)}, u32[]{:S(2)}, u32[]{:S(2)}) %collective-permute-start.17) | collective-permute-done | bytes 393248 | tf_op jit(solution)/shard_map/ppermute | solution.py:380
  143.3 1.5 server.1
  144.8 1.3 collective-permute-start.19
  146.0 0.1 collective-permute-start.18
  146.1 9.6 %collective-permute-done.19.refs_2_ = bf16[2,32,3072]{2,1,0:T(8,128)(2,1)S(1)} collective-permute-done((bf16[2,32,3072]{2,1,0:T(8,128)(2,1)S(1)}, bf16[2,32,3072]{2,1,0:T(8,128)(2,1)S(1)}, u32[]{:S(2)}, u32[]{:S(2)}) %collective-permute-start.19) | collective-permute-done | bytes 393248 | tf_op jit(solution)/shard_map/ppermute | solution.py:520
  155.7 0.6 collective-permute-start.20
  156.3 0.0 collective-permute-done.18.refs_1_
  156.3 1.3 collective-permute-done.20.refs_3_
  157.6 1.3 join.1
  158.9 0.0 all-to-all-done.1.others_ref
  158.9 2.4 %unpack.1 = bf16[384,16,128]{2,1,0:T(8,128)(2,1)} custom-call(bf16[8,128,256]{2,1,0:T(8,128)(2,1)} %all-to-all-done.queries_ref, bf16[128,256]{1,0:T(8,128)(2,1)S(1)} %collective-permute-done.14.far_ref, bf16[8,256,256]{2,1,0:T(8,128)(2,1)} %all-to-all-done.1.others_ref), custom_call_target="tpu_custom_call" | custom-call | bytes 3145728 | tf_op jit(solution)/shard_map/unpack/pallas_call | solution.py:522
  (15 shorter events, 0.0 us)
Async XLA Ops:
  0.6 34.1 %collective-permute-start.1 = (bf16[128,3072]{1,0:T(8,128)(2,1)}, bf16[128,3072]{1,0:T(8,128)(2,1)S(1)}, u32[]{:S(2)}, u32[]{:S(2)}) collective-permute-start(bf16[128,3072]{1,0:T(8,128)(2,1)} %bitcast.14), channel_id=1, source_target_pairs={{0,1},{2,0},{4,2},{6,4},{7,6},{5,7},{3,5},{1,3},{8,10},{10,12},{12... | collective-permute-start | bytes 2359304 | tf_op jit(solution)/shard_map/ppermute | solution.py:365
  2.0 32.8 %collective-permute-start = (bf16[128,3072]{1,0:T(8,128)(2,1)}, bf16[128,3072]{1,0:T(8,128)(2,1)S(1)}, u32[]{:S(2)}, u32[]{:S(2)}) collective-permute-start(bf16[128,3072]{1,0:T(8,128)(2,1)} %bitcast.15), channel_id=1, source_target_pairs={{0,2},{2,4},{4,6},{6,7},{7,5},{5,3},{3,1},{1,0},{8,9},{10,8},{12,1... | collective-permute-start | bytes 2359304 | tf_op jit(solution)/shard_map/ppermute | solution.py:365
  2.1 1.4 copy-start
  4.1 0.7 copy-start.1
  4.8 5.2 %collective-permute-start.2 = (bf16[384,256]{1,0:T(8,128)(2,1)S(1)}, bf16[384,256]{1,0:T(8,128)(2,1)S(1)}, u32[]{:S(2)}, u32[]{:S(2)}) collective-permute-start(bf16[384,256]{1,0:T(8,128)(2,1)S(1)} %get-tuple-element.53), channel_id=1, source_target_pairs={{0,1},{1,0},{2,3},{3,2},{4,5},{5,4},{6,7},{7,6},{8,9},{9,8},{10,11... | collective-permute-start | bytes 589832 | tf_op jit(solution)/shard_map/ppermute | solution.py:380
  6.0 26.3 %collective-permute-start.3 = (bf16[384,256]{1,0:T(8,128)(2,1)S(1)}, bf16[384,256]{1,0:T(8,128)(2,1)S(1)}, u32[]{:S(2)}, u32[]{:S(2)}) collective-permute-start(bf16[384,256]{1,0:T(8,128)(2,1)S(1)} %get-tuple-element.54), channel_id=1, source_target_pairs={{0,7},{1,6},{2,5},{3,4},{4,3},{5,2},{6,1},{7,0},{8,15},{9,14},{10,... | collective-permute-start | bytes 589832 | tf_op jit(solution)/shard_map/ppermute | solution.py:380
  7.3 27.5 %collective-permute-start.4 = (bf16[384,256]{1,0:T(8,128)(2,1)S(1)}, bf16[384,256]{1,0:T(8,128)(2,1)S(1)}, u32[]{:S(2)}, u32[]{:S(2)}) collective-permute-start(bf16[384,256]{1,0:T(8,128)(2,1)S(1)} %get-tuple-element.55), channel_id=1, source_target_pairs={{0,5},{1,4},{2,7},{3,6},{4,1},{5,0},{6,3},{7,2},{8,13},{9,12},{10,... | collective-permute-start | bytes 589832 | tf_op jit(solution)/shard_map/ppermute | solution.py:380
  10.0 67.3 %copy-start.4 = (bf16[384,256]{1,0:T(8,128)(2,1)}, bf16[384,256]{1,0:T(8,128)(2,1)S(1)}, u32[]{:S(2)}) copy-start(bf16[384,256]{1,0:T(8,128)(2,1)S(1)} %collective-permute-done.2.refs_7_.refs_4_) | copy-start | bytes 589828
  10.0 24.8 %collective-permute-start.5 = (bf16[384,256]{1,0:T(8,128)(2,1)S(1)}, bf16[384,256]{1,0:T(8,128)(2,1)S(1)}, u32[]{:S(2)}, u32[]{:S(2)}) collective-permute-start(bf16[384,256]{1,0:T(8,128)(2,1)S(1)} %get-tuple-element.56), channel_id=1, source_target_pairs={{0,3},{1,2},{2,1},{3,0},{4,7},{5,6},{6,5},{7,4},{8,11},{9,10},{10,... | collective-permute-start | bytes 589832 | tf_op jit(solution)/shard_map/ppermute | solution.py:380
  32.3 43.4 %copy-start.5 = (bf16[384,256]{1,0:T(8,128)(2,1)}, bf16[384,256]{1,0:T(8,128)(2,1)S(1)}, u32[]{:S(2)}) copy-start(bf16[384,256]{1,0:T(8,128)(2,1)S(1)} %collective-permute-done.3.refs_13_.refs_10_) | copy-start | bytes 589828
  34.8 41.0 %copy-start.6 = (bf16[384,256]{1,0:T(8,128)(2,1)}, bf16[384,256]{1,0:T(8,128)(2,1)S(1)}, u32[]{:S(2)}) copy-start(bf16[384,256]{1,0:T(8,128)(2,1)S(1)} %collective-permute-done.4.refs_11_.refs_8_) | copy-start | bytes 589828
  34.8 41.0 %copy-start.7 = (bf16[384,256]{1,0:T(8,128)(2,1)}, bf16[384,256]{1,0:T(8,128)(2,1)S(1)}, u32[]{:S(2)}) copy-start(bf16[384,256]{1,0:T(8,128)(2,1)S(1)} %collective-permute-done.5.refs_9_.refs_6_) | copy-start | bytes 589828
  34.8 42.5 %copy-start.11 = (bf16[128,3072]{1,0:T(8,128)(2,1)}, bf16[128,3072]{1,0:T(8,128)(2,1)S(1)}, u32[]{:S(2)}) copy-start(bf16[128,3072]{1,0:T(8,128)(2,1)S(1)} %collective-permute-done.1.refs_2_) | copy-start | bytes 2359300
  34.8 42.5 %copy-start.12 = (bf16[128,3072]{1,0:T(8,128)(2,1)}, bf16[128,3072]{1,0:T(8,128)(2,1)S(1)}, u32[]{:S(2)}) copy-start(bf16[128,3072]{1,0:T(8,128)(2,1)S(1)} %collective-permute-done.refs_1_) | copy-start | bytes 2359300
  34.8 40.9 %collective-permute-start.6 = (bf16[128,3072]{1,0:T(8,128)(2,1)S(1)}, bf16[128,3072]{1,0:T(8,128)(2,1)}, u32[]{:S(2)}, u32[]{:S(2)}) collective-permute-start(bf16[128,3072]{1,0:T(8,128)(2,1)S(1)} %collective-permute-done.refs_1_), channel_id=1, source_target_pairs={{0,2},{2,4},{4,6},{6,7},{7,5},{5,3},{3,1},{1,0},{8,9},{10,8},{12,1... | collective-permute-start | bytes 2359304 | tf_op jit(solution)/shard_map/ppermute | solution.py:365
  36.8 38.9 %collective-permute-start.7 = (bf16[128,3072]{1,0:T(8,128)(2,1)S(1)}, bf16[128,3072]{1,0:T(8,128)(2,1)}, u32[]{:S(2)}, u32[]{:S(2)}) collective-permute-start(bf16[128,3072]{1,0:T(8,128)(2,1)S(1)} %collective-permute-done.1.refs_2_), channel_id=1, source_target_pairs={{0,1},{2,0},{4,2},{6,4},{7,6},{5,7},{3,5},{1,3},{8,10},{10,12},{12... | collective-permute-start | bytes 2359304 | tf_op jit(solution)/shard_map/ppermute | solution.py:365
  42.0 29.4 %collective-permute-start.8 = (bf16[384,256]{1,0:T(8,128)(2,1)S(1)}, bf16[384,256]{1,0:T(8,128)(2,1)S(1)}, u32[]{:S(2)}, u32[]{:S(2)}) collective-permute-start(bf16[384,256]{1,0:T(8,128)(2,1)S(1)} %get-tuple-element.59), channel_id=1, source_target_pairs={{0,6},{1,7},{2,4},{3,5},{4,2},{5,3},{6,0},{7,1},{8,14},{9,15},{10,... | collective-permute-start | bytes 589832 | tf_op jit(solution)/shard_map/ppermute | solution.py:380
  44.1 31.6 %collective-permute-start.9 = (bf16[384,256]{1,0:T(8,128)(2,1)S(1)}, bf16[384,256]{1,0:T(8,128)(2,1)S(1)}, u32[]{:S(2)}, u32[]{:S(2)}) collective-permute-start(bf16[384,256]{1,0:T(8,128)(2,1)S(1)} %get-tuple-element.60), channel_id=1, source_target_pairs={{0,4},{1,5},{2,6},{3,7},{4,0},{5,1},{6,2},{7,3},{8,12},{9,13},{10,... | collective-permute-start | bytes 589832 | tf_op jit(solution)/shard_map/ppermute | solution.py:380
  47.0 28.7 %collective-permute-start.10 = (bf16[384,256]{1,0:T(8,128)(2,1)S(1)}, bf16[384,256]{1,0:T(8,128)(2,1)S(1)}, u32[]{:S(2)}, u32[]{:S(2)}) collective-permute-start(bf16[384,256]{1,0:T(8,128)(2,1)S(1)} %get-tuple-element.61), channel_id=1, source_target_pairs={{0,2},{1,3},{2,0},{3,1},{4,6},{5,7},{6,4},{7,5},{8,10},{9,11},{10,... | collective-permute-start | bytes 589832 | tf_op jit(solution)/shard_map/ppermute | solution.py:380
  71.5 5.8 %copy-start.8 = (bf16[384,256]{1,0:T(8,128)(2,1)}, bf16[384,256]{1,0:T(8,128)(2,1)S(1)}, u32[]{:S(2)}) copy-start(bf16[384,256]{1,0:T(8,128)(2,1)S(1)} %collective-permute-done.8.refs_12_.refs_9_) | copy-start | bytes 589828
  75.7 1.6 copy-start.9
  75.7 1.6 copy-start.10
  75.7 19.3 %collective-permute-start.11 = (bf16[128,3072]{1,0:T(8,128)(2,1)}, bf16[128,3072]{1,0:T(8,128)(2,1)S(1)}, u32[]{:S(2)}, u32[]{:S(2)}) collective-permute-start(bf16[128,3072]{1,0:T(8,128)(2,1)} %collective-permute-done.6.refs_3_), channel_id=1, source_target_pairs={{0,2},{2,4},{4,6},{6,7},{7,5},{5,3},{3,1},{1,0},{8,9},{10,8},{12,1... | collective-permute-start | bytes 2359304 | tf_op jit(solution)/shard_map/ppermute | solution.py:365
  75.8 21.1 %collective-permute-start.12 = (bf16[128,3072]{1,0:T(8,128)(2,1)}, bf16[128,3072]{1,0:T(8,128)(2,1)}, u32[]{:S(2)}, u32[]{:S(2)}) collective-permute-start(bf16[128,3072]{1,0:T(8,128)(2,1)} %collective-permute-done.7.refs_4_), channel_id=1, source_target_pairs={{0,1},{2,0},{4,2},{6,4},{7,6},{5,7},{3,5},{1,3},{8,10},{10,12},{12... | collective-permute-start | bytes 2359304 | tf_op jit(solution)/shard_map/ppermute | solution.py:365
  95.1 3.5 %copy-start.3 = (bf16[128,3072]{1,0:T(8,128)(2,1)}, bf16[128,3072]{1,0:T(8,128)(2,1)S(1)}, u32[]{:S(2)}) copy-start(bf16[128,3072]{1,0:T(8,128)(2,1)S(1)} %collective-permute-done.11.refs_0_.refs_16_) | copy-start | bytes 2359300
  96.9 15.0 %collective-permute-start.13 = (bf16[128,3072]{1,0:T(8,128)(2,1)S(1)}, bf16[128,3072]{1,0:T(8,128)(2,1)}, u32[]{:S(2)}, u32[]{:S(2)}) collective-permute-start(bf16[128,3072]{1,0:T(8,128)(2,1)S(1)} %collective-permute-done.11.refs_0_.refs_16_), channel_id=1, source_target_pairs={{0,2},{2,4},{4,6},{6,7},{7,5},{5,3},{3,1},{1,0},{8,9},{10,8},{12,1... | collective-permute-start | bytes 2359304 | tf_op jit(solution)/shard_map/ppermute | solution.py:365
  107.7 19.5 %all-to-all-start = ((bf16[8,128,256]{2,1,0:T(8,128)(2,1)}), bf16[8,128,256]{2,1,0:T(8,128)(2,1)}, u32[]{:S(2)}, u32[]{:S(2)}) async-start(bf16[8,128,256]{2,1,0:T(8,128)(2,1)} %get-tuple-element.80), calls=%async_computation | async-start | bytes 1048576 | tf_op jit(solution)/shard_map/all_to_all | solution.py:461
  122.0 21.3 %copy-start.2 = (bf16[2,32,3072]{2,1,0:T(8,128)(2,1)S(1)}, bf16[2,32,3072]{2,1,0:T(8,128)(2,1)}, u32[]{:S(2)}) copy-start(bf16[2,32,3072]{2,1,0:T(8,128)(2,1)} %get-tuple-element.95.refs_0_) | copy-start | bytes 1179652
  122.0 11.5 %collective-permute-start.15 = (bf16[2,32,3072]{2,1,0:T(8,128)(2,1)}, bf16[2,32,3072]{2,1,0:T(8,128)(2,1)S(1)}, u32[]{:S(2)}, u32[]{:S(2)}) collective-permute-start(bf16[2,32,3072]{2,1,0:T(8,128)(2,1)} %get-tuple-element.89), channel_id=1, source_target_pairs={{0,8},{8,0},{16,24},{24,16},{1,9},{9,1},{17,25},{25,17},{2,10},{10... | collective-permute-start | bytes 1179656 | tf_op jit(solution)/shard_map/ppermute | solution.py:380
  123.4 10.9 %collective-permute-start.16 = (bf16[2,32,3072]{2,1,0:T(8,128)(2,1)}, bf16[2,32,3072]{2,1,0:T(8,128)(2,1)S(1)}, u32[]{:S(2)}, u32[]{:S(2)}) collective-permute-start(bf16[2,32,3072]{2,1,0:T(8,128)(2,1)} %get-tuple-element.90), channel_id=1, source_target_pairs={{0,16},{8,24},{16,0},{24,8},{1,17},{9,25},{17,1},{25,9},{2,18},{10... | collective-permute-start | bytes 1179656 | tf_op jit(solution)/shard_map/ppermute | solution.py:380
  124.7 18.6 %collective-permute-start.17 = (bf16[2,32,3072]{2,1,0:T(8,128)(2,1)}, bf16[2,32,3072]{2,1,0:T(8,128)(2,1)S(1)}, u32[]{:S(2)}, u32[]{:S(2)}) collective-permute-start(bf16[2,32,3072]{2,1,0:T(8,128)(2,1)} %get-tuple-element.91), channel_id=1, source_target_pairs={{0,24},{8,16},{16,8},{24,0},{1,25},{9,17},{17,9},{25,1},{2,26},{10... | collective-permute-start | bytes 1179656 | tf_op jit(solution)/shard_map/ppermute | solution.py:380
  125.1 8.3 %collective-permute-start.14 = (bf16[128,256]{1,0:T(8,128)(2,1)}, bf16[128,256]{1,0:T(8,128)(2,1)S(1)}, u32[]{:S(2)}, u32[]{:S(2)}) collective-permute-start(bf16[128,256]{1,0:T(8,128)(2,1)} %get-tuple-element.87), channel_id=1, source_target_pairs={{0,7},{2,5},{4,3},{6,1},{7,0},{5,2},{3,4},{1,6},{8,15},{10,13},{12... | collective-permute-start | bytes 196616 | tf_op jit(solution)/shard_map/ppermute | solution.py:499
  127.2 31.7 %all-to-all-start.1 = ((bf16[8,256,256]{2,1,0:T(8,128)(2,1)}), bf16[8,256,256]{2,1,0:T(8,128)(2,1)}, u32[]{:S(2)}, u32[]{:S(2)}) async-start(bf16[8,256,256]{2,1,0:T(8,128)(2,1)} %get-tuple-element.94), calls=%async_computation.1 | async-start | bytes 2097152 | tf_op jit(solution)/shard_map/all_to_all | solution.py:500
  144.8 10.9 %collective-permute-start.19 = (bf16[2,32,3072]{2,1,0:T(8,128)(2,1)S(1)}, bf16[2,32,3072]{2,1,0:T(8,128)(2,1)S(1)}, u32[]{:S(2)}, u32[]{:S(2)}) collective-permute-start(bf16[2,32,3072]{2,1,0:T(8,128)(2,1)S(1)} %get-tuple-element.99.refs_0_), channel_id=1, source_target_pairs={{0,16},{8,24},{16,0},{24,8},{1,17},{9,25},{17,1},{25,9},{2,18},{10... | collective-permute-start | bytes 1179656 | tf_op jit(solution)/shard_map/ppermute | solution.py:520
  146.0 10.3 %collective-permute-start.18 = (bf16[2,32,3072]{2,1,0:T(8,128)(2,1)S(1)}, bf16[2,32,3072]{2,1,0:T(8,128)(2,1)S(1)}, u32[]{:S(2)}, u32[]{:S(2)}) collective-permute-start(bf16[2,32,3072]{2,1,0:T(8,128)(2,1)S(1)} %get-tuple-element.99.refs_0_), channel_id=1, source_target_pairs={{0,8},{8,0},{16,24},{24,16},{1,9},{9,1},{17,25},{25,17},{2,10},{10... | collective-permute-start | bytes 1179656 | tf_op jit(solution)/shard_map/ppermute | solution.py:520
  155.7 1.9 %collective-permute-start.20 = (bf16[2,32,3072]{2,1,0:T(8,128)(2,1)S(1)}, bf16[2,32,3072]{2,1,0:T(8,128)(2,1)S(1)}, u32[]{:S(2)}, u32[]{:S(2)}) collective-permute-start(bf16[2,32,3072]{2,1,0:T(8,128)(2,1)S(1)} %collective-permute-done.19.refs_2_), channel_id=1, source_target_pairs={{0,8},{8,0},{16,24},{24,16},{1,9},{9,1},{17,25},{25,17},{2,10},{10... | collective-permute-start | bytes 1179656 | tf_op jit(solution)/shard_map/ppermute | solution.py:520

commit v5 on v4

--- a/solution.py
+++ b/solution.py
@@ -8,7 +8,7 @@
 from jax.experimental.pallas import tpu as pltpu
 from jax.sharding import PartitionSpec as P
 
-SMALL, LARGE = 16 * 1024 * 1024, 63 * 1024 * 1024
+SMALL, LARGE = 16 * 1024 * 1024, 127 * 512 * 1024
 F32 = jnp.float32
 HEAVY = 10**13, 10**13, 10**13
 BF16 = jnp.bfloat16
@@ -35,8 +35,8 @@
 
 
 def waves_of(n):
-    odd, even = list(range(n - 1, 1, -2)), list(range(n - 2, 0, -2))
-    return [[1, *odd], even]
+    late = [n - 1] + [k for k in range(n - 2, 1, -1) if k & (k - 1) == 0]
+    return [[1] + [k for k in range(n - 2, 1, -1) if k not in late], late]
 
 
 def dot_nt(a, b):
@@ -48,15 +48,24 @@
 
 
 def pack_kernel(n, x_ref, *refs):
-    outs, parts = refs[:n], refs[n]
+    outs, (x_all, parts, sems) = refs[:n], refs[n:]
     rows, heads, size = x_ref.shape
     wide = heads * size // n
-    x = x_ref[...].reshape(rows, heads * size)
-    for d in range(n):
-        parts[d] = x[:, d * wide : (d + 1) * wide]
+    third = rows // 3
     me = lax.axis_index("seq")
-    for k in range(n):
-        outs[k][...] = parts[me ^ k]
+    spans = [pl.ds(i * third, third) for i in range(3)]
+    arriving = fetch([(x_ref.at[s], x_all.at[s]) for s in spans], sems)
+    leaving = []
+    for i, copy in enumerate(arriving):
+        copy.wait()
+        here = slice(i * third, (i + 1) * third)
+        x = x_all[here].reshape(third, heads * size)
+        for d in range(n):
+            parts[d, here] = x[:, d * wide : (d + 1) * wide]
+        going = [(parts.at[me ^ k, spans[i]], outs[k].at[spans[i]]) for k in range(n)]
+        leaving += fetch(going, sems, 3 + i * n)
+    for copy in leaving:
+        copy.wait()
 
 
 def unpack_kernel(n, queries_ref, far_ref, others_ref, out_ref, blocks, far_all, rows, sems):
@@ -355,6 +364,9 @@
     half = n // 2
     shape = jax.ShapeDtypeStruct
 
+    vmem = pl.BlockSpec(memory_space=pltpu.VMEM)
+    smem = pl.BlockSpec(memory_space=pltpu.SMEM)
+    anywhere = pl.BlockSpec(memory_space=pl.ANY)
     ring = ring_order(n)
 
     def around(turn):
@@ -369,9 +381,15 @@
     packed_shape = (3 * tokens, wide)
     packed = pl.pallas_call(
         functools.partial(pack_kernel, n),
+        in_specs=[anywhere],
+        out_specs=[anywhere] * n,
         out_shape=[shape(packed_shape, BF16)] * n,
-        scratch_shapes=[pltpu.VMEM((n, *packed_shape), BF16)],
-        compiler_params=params(SMALL),
+        scratch_shapes=[
+            pltpu.VMEM((3 * tokens, heads, size), BF16),
+            pltpu.VMEM((n, *packed_shape), BF16),
+            pltpu.SemaphoreType.DMA((3 + 3 * n,)),
+        ],
+        compiler_params=params(LARGE),
         cost_estimate=cost(0, 4 * qkv.size),
         name="pack",
     )(qkv.reshape(3 * tokens, heads, size))
@@ -381,9 +399,6 @@
 
     blocks = list(packed)
     w_flat = w_out.reshape(wide, wide_d)
-    vmem = pl.BlockSpec(memory_space=pltpu.VMEM)
-    smem = pl.BlockSpec(memory_space=pltpu.SMEM)
-    anywhere = pl.BlockSpec(memory_space=pl.ANY)
     length = n * tokens
 
     def attend(groups, tiles, carried, earlier=None, parts=()):

time: 164 us -> 160 us (0.976)
  starting transfers between devices: 54.4 us -> 49 us
  local copies, waits for them, and re-layouts: 2.15 us -> 0.01 us
  Pallas kernels: 42.5 us -> 44.5 us
    ppermute x7, starting transfers between devices: 12 us -> 8.03 us  [around(): return lambda x: lax.ppermute(x, ('dp', 'seq'), pairs)]
    unnamed x26 -> x6, local copies, waits for them, and re-layouts: 2.15 us -> 0.01 us
    pallas_call x1, Pallas kernels: 0.54 us -> 2.59 us  [body(): pl.pallas_call(functools.partial(pack_kernel, n), in_specs=[anywhere], ou...]
  transfers between devices with their start and end apart: 23 -> 23, of which waited for: 10 -> 10; matrix products, arithmetic and copies ran while one was open for 0% -> 0% of each run, Pallas kernels for 25% -> 27%
where the time goes in v5:
time: 160 us; the launch traced here: 157 us
  waiting for transfers between devices  62.6 us (39%)
  starting transfers between devices  49 us (31%)
  Pallas kernels  44.5 us (28%)
    ppermute x10, waiting for transfers between devices, send(): lax.ppermute(blocks[k], axis, [(i, i ^ k) for i in range(len(blocks))])  49.7 us
    pallas_call x2, Pallas kernels, attend(): pl.pallas_call(functools.partial(attend_kernel, n, heads_here, per_group,...  26.7 us
    ppermute x10, starting transfers between devices, send(): lax.ppermute(blocks[k], axis, [(i, i ^ k) for i in range(len(blocks))])  26.6 us
    ppermute x3, waiting for transfers between devices, body(): lax.ppermute(source, 'dp', [(i, i ^ step) for i in range(workers)])  11 us
    pallas_call x1, Pallas kernels, body(): pl.pallas_call(functools.partial(tail_kernel, n, heads_here, per_group, w...  10 us
    ppermute x7, starting transfers between devices, around(): return lambda x: lax.ppermute(x, ('dp', 'seq'), pairs)  8.03 us
    all_to_all x1, starting transfers between devices, body(): lax.all_to_all(grads, 'seq', split_axis=0, concat_axis=0, tiled=True)  6.22 us
    all_to_all x1, starting transfers between devices, body(): lax.all_to_all(query, 'seq', split_axis=0, concat_axis=0, tiled=True)  4.12 us
  transfers between devices with their start and end apart: 23, of which 10 were waited for; matrix products, arithmetic and copies ran while one was open for 0% of the time, Pallas kernels for 27%

profile of v5, /device:TPU:9, one launch (start us, length us, event | category | flops | bytes accessed | tf_op | source)
XLA Modules:
  0.0 157.0 jit_solution(8762586157157130845)
XLA Ops:
  0.6 1.3 collective-permute-start.1
  2.0 0.2 collective-permute-start
  2.1 2.6 %pack.1 = (bf16[384,256]{1,0:T(8,128)(2,1)}, bf16[384,256]{1,0:T(8,128)(2,1)}, bf16[384,256]{1,0:T(8,128)(2,1)}, bf16[384,256]{1,0:T(8,128)(2,1)}, bf16[384,256]...) custom-call(bf16[384,16,128]{2,1,0:T(8,128)(2,1)} %bitcast.11), custom_call_target="tpu_custom_call" | custom-call | bytes 3145728 | tf_op jit(solution)/shard_map/pack/pallas_call | solution.py:382
  4.7 1.3 collective-permute-start.2
  6.1 1.3 collective-permute-start.3
  7.4 1.0 collective-permute-start.4
  8.3 2.0 %collective-permute-done.2.refs_7_.refs_4_ = bf16[384,256]{1,0:T(8,128)(2,1)S(1)} collective-permute-done((bf16[384,256]{1,0:T(8,128)(2,1)}, bf16[384,256]{1,0:T(8,128)(2,1)S(1)}, u32[]{:S(2)}, u32[]{:S(2)}) %collective-permute-start.2) | collective-permute-done | bytes 196640 | tf_op jit(solution)/shard_map/ppermute | solution.py:398
  10.3 0.0 copy-start.1
  10.3 14.5 %collective-permute-start.5 = (bf16[384,256]{1,0:T(8,128)(2,1)}, bf16[384,256]{1,0:T(8,128)(2,1)}, u32[]{:S(2)}, u32[]{:S(2)}) collective-permute-start(bf16[384,256]{1,0:T(8,128)(2,1)} %get-tuple-element.56), channel_id=1, source_target_pairs={{0,3},{1,2},{2,1},{3,0},{4,7},{5,6},{6,5},{7,4},{8,11},{9,10},{10,... | collective-permute-start | bytes 589832 | tf_op jit(solution)/shard_map/ppermute | solution.py:398
  24.8 9.7 %collective-permute-done.3.refs_12_.refs_9_ = bf16[384,256]{1,0:T(8,128)(2,1)S(1)} collective-permute-done((bf16[384,256]{1,0:T(8,128)(2,1)}, bf16[384,256]{1,0:T(8,128)(2,1)S(1)}, u32[]{:S(2)}, u32[]{:S(2)}) %collective-permute-start.3) | collective-permute-done | bytes 196640 | tf_op jit(solution)/shard_map/ppermute | solution.py:398
  34.5 0.0 copy-start.2
  34.5 0.4 collective-permute-done.4.refs_11_.refs_8_
  34.9 0.0 collective-permute-done.5.refs_9_.refs_6_
  34.9 0.0 collective-permute-done.1.refs_2_
  34.9 0.0 collective-permute-done.refs_1_
  34.9 1.7 %collective-permute-start.6 = (bf16[128,3072]{1,0:T(8,128)(2,1)}, bf16[128,3072]{1,0:T(8,128)(2,1)}, u32[]{:S(2)}, u32[]{:S(2)}) collective-permute-start(bf16[128,3072]{1,0:T(8,128)(2,1)} %collective-permute-done.refs_1_), channel_id=1, source_target_pairs={{0,2},{2,4},{4,6},{6,7},{7,5},{5,3},{3,1},{1,0},{8,9},{10,8},{12,1... | collective-permute-start | bytes 2359304 | tf_op jit(solution)/shard_map/ppermute | solution.py:377
  36.5 1.4 collective-permute-start.7
  37.9 1.3 collective-permute-start.8
  39.2 4.9 %collective-permute-start.9 = (bf16[384,256]{1,0:T(8,128)(2,1)}, bf16[384,256]{1,0:T(8,128)(2,1)}, u32[]{:S(2)}, u32[]{:S(2)}) collective-permute-start(bf16[384,256]{1,0:T(8,128)(2,1)} %get-tuple-element.60), channel_id=1, source_target_pairs={{0,4},{1,5},{2,6},{3,7},{4,0},{5,1},{6,2},{7,3},{8,12},{9,13},{10,... | collective-permute-start | bytes 589832 | tf_op jit(solution)/shard_map/ppermute | solution.py:398
  44.1 0.0 collective-permute-start.10
  44.1 25.4 %collective-permute-done.8.refs_13_.refs_10_ = bf16[384,256]{1,0:T(8,128)(2,1)} collective-permute-done((bf16[384,256]{1,0:T(8,128)(2,1)}, bf16[384,256]{1,0:T(8,128)(2,1)}, u32[]{:S(2)}, u32[]{:S(2)}) %collective-permute-start.8) | collective-permute-done | bytes 196640 | tf_op jit(solution)/shard_map/ppermute | solution.py:398
  69.5 2.4 %collective-permute-done.9.refs_10_.refs_7_ = bf16[384,256]{1,0:T(8,128)(2,1)} collective-permute-done((bf16[384,256]{1,0:T(8,128)(2,1)}, bf16[384,256]{1,0:T(8,128)(2,1)}, u32[]{:S(2)}, u32[]{:S(2)}) %collective-permute-start.9) | collective-permute-done | bytes 196640 | tf_op jit(solution)/shard_map/ppermute | solution.py:398
  71.9 0.0 collective-permute-done.10.refs_8_.refs_5_
  71.9 0.0 collective-permute-done.6.refs_3_
  71.9 0.0 collective-permute-done.7.refs_4_
  71.9 0.1 collective-permute-start.11
  72.0 1.5 collective-permute-start.12
  73.4 0.0 copy-done.1
  73.4 0.0 copy-done.2
  73.4 17.8 %attend.2 = (bf16[640,256]{1,0:T(8,128)(2,1)}, f32[1024,256]{1,0:T(8,128)}, f32[1024,256]{1,0:T(8,128)}, bf16[640,256]{1,0:T(8,128)(2,1)}, f32[2,128,1024]{2,1,0...) custom-call(s32[8,8,8]{2,1,0:T(8,128)} %refs_0_.1, bf16[128,3072]{1,0:T(8,128)(2,1)} %bitcast.16, ...), custom_call_target="tpu_custom_call" | custom-call | flops 3355443200 | bytes 41943040 | tf_op jit(solution)/shard_map/attend/pallas_call | solution.py:430
  91.2 0.0 collective-permute-done.11.refs_0_.refs_16_
  91.2 1.9 %collective-permute-done.12.refs_1_.refs_17_ = bf16[128,3072]{1,0:T(8,128)(2,1)} collective-permute-done((bf16[128,3072]{1,0:T(8,128)(2,1)}, bf16[128,3072]{1,0:T(8,128)(2,1)}, u32[]{:S(2)}, u32[]{:S(2)}) %collective-permute-start.12) | collective-permute-done | bytes 786464 | tf_op jit(solution)/shard_map/ppermute | solution.py:377
  93.1 1.9 %collective-permute-start.13 = (bf16[128,3072]{1,0:T(8,128)(2,1)}, bf16[128,3072]{1,0:T(8,128)(2,1)}, u32[]{:S(2)}, u32[]{:S(2)}) collective-permute-start(bf16[128,3072]{1,0:T(8,128)(2,1)} %collective-permute-done.11.refs_0_.refs_16_), channel_id=1, source_target_pairs={{0,2},{2,4},{4,6},{6,7},{7,5},{5,3},{3,1},{1,0},{8,9},{10,8},{12,1... | collective-permute-start | bytes 2359304 | tf_op jit(solution)/shard_map/ppermute | solution.py:377
  95.1 9.0 %attend.3 = (bf16[8,128,256]{2,1,0:T(8,128)(2,1)}, f32[1024,256]{1,0:T(8,128)}, f32[1024,256]{1,0:T(8,128)}, bf16[256,256]{1,0:T(8,128)(2,1)}) custom-call(s32[8,8,8]{2,1,0:T(8,128)} %refs_0_.1, bf16[128,3072]{1,0:T(8,128)(2,1)} %collective-permute-done.11.refs_0_.refs_16_, bf16[128,3072]{1,0:T(8,128)(2,1)} %collective-permute-done.12.refs_1_.refs_17_, ...), custom_call_target="tpu_custom_call" | custom-call | flops 1342177280 | bytes 16777216 | tf_op jit(solution)/shard_map/attend/pallas_call | solution.py:430
  104.1 4.1 %all-to-all-start = ((bf16[8,128,256]{2,1,0:T(8,128)(2,1)}), bf16[8,128,256]{2,1,0:T(8,128)(2,1)}, u32[]{:S(2)}, u32[]{:S(2)}) async-start(bf16[8,128,256]{2,1,0:T(8,128)(2,1)} %get-tuple-element.80), calls=%async_computation | async-start | bytes 1048576 | tf_op jit(solution)/shard_map/all_to_all | solution.py:476
  108.2 0.0 collective-permute-done.13.refs_1_
  108.2 10.0 %tail.1 = (bf16[128,256]{1,0:T(8,128)(2,1)}, bf16[8,256,256]{2,1,0:T(8,128)(2,1)}, f32[256,3072]{1,0:T(8,128)}, bf16[2,32,3072]{2,1,0:T(8,128)(2,1)}, bf16[2,32,...) custom-call(s32[8,8,8]{2,1,0:T(8,128)} %refs_0_.1, ...), custom_call_target="tpu_custom_call" | custom-call | flops 9999999827968 | bytes 16777216 | tf_op jit(solution)/shard_map/tail/pallas_call | solution.py:481
  118.2 0.0 copy-start
  118.3 0.7 collective-permute-start.15
  118.9 1.2 collective-permute-start.16
  120.2 0.5 collective-permute-start.17
  120.6 2.1 %collective-permute-start.14 = (bf16[128,256]{1,0:T(8,128)(2,1)}, bf16[128,256]{1,0:T(8,128)(2,1)S(1)}, u32[]{:S(2)}, u32[]{:S(2)}) collective-permute-start(bf16[128,256]{1,0:T(8,128)(2,1)} %get-tuple-element.87), channel_id=1, source_target_pairs={{0,7},{2,5},{4,3},{6,1},{7,0},{5,2},{3,4},{1,6},{8,15},{10,13},{12... | collective-permute-start | bytes 196616 | tf_op jit(solution)/shard_map/ppermute | solution.py:514
  122.7 0.0 all-to-all-done.queries_ref
  122.8 6.2 %all-to-all-start.1 = ((bf16[8,256,256]{2,1,0:T(8,128)(2,1)}), bf16[8,256,256]{2,1,0:T(8,128)(2,1)}, u32[]{:S(2)}, u32[]{:S(2)}) async-start(bf16[8,256,256]{2,1,0:T(8,128)(2,1)} %get-tuple-element.94), calls=%async_computation.1 | async-start | bytes 2097152 | tf_op jit(solution)/shard_map/all_to_all | solution.py:515
  129.0 0.0 collective-permute-done.14.far_ref
  129.0 0.0 collective-permute-done.15.refs_1_
  129.0 0.9 collective-permute-done.16.refs_2_
  129.8 9.0 %collective-permute-done.17.refs_3_ = bf16[2,32,3072]{2,1,0:T(8,128)(2,1)S(1)} collective-permute-done((bf16[2,32,3072]{2,1,0:T(8,128)(2,1)}, bf16[2,32,3072]{2,1,0:T(8,128)(2,1)S(1)}, u32[]{:S(2)}, u32[]{:S(2)}) %collective-permute-start.17) | collective-permute-done | bytes 393248 | tf_op jit(solution)/shard_map/ppermute | solution.py:398
  138.8 0.0 copy-done
  138.8 1.5 server.1
  140.3 1.2 collective-permute-start.19
  141.5 0.1 collective-permute-start.18
  141.6 9.6 %collective-permute-done.19.refs_2_ = bf16[2,32,3072]{2,1,0:T(8,128)(2,1)S(1)} collective-permute-done((bf16[2,32,3072]{2,1,0:T(8,128)(2,1)S(1)}, bf16[2,32,3072]{2,1,0:T(8,128)(2,1)S(1)}, u32[]{:S(2)}, u32[]{:S(2)}) %collective-permute-start.19) | collective-permute-done | bytes 393248 | tf_op jit(solution)/shard_map/ppermute | solution.py:535
  151.2 0.6 collective-permute-start.20
  151.8 0.0 collective-permute-done.18.refs_1_
  151.8 1.3 collective-permute-done.20.refs_3_
  153.2 1.3 join.1
  154.4 0.0 all-to-all-done.1.others_ref
  154.4 2.4 %unpack.1 = bf16[384,16,128]{2,1,0:T(8,128)(2,1)} custom-call(bf16[8,128,256]{2,1,0:T(8,128)(2,1)} %all-to-all-done.queries_ref, bf16[128,256]{1,0:T(8,128)(2,1)S(1)} %collective-permute-done.14.far_ref, bf16[8,256,256]{2,1,0:T(8,128)(2,1)} %all-to-all-done.1.others_ref), custom_call_target="tpu_custom_call" | custom-call | bytes 3145728 | tf_op jit(solution)/shard_map/unpack/pallas_call | solution.py:537
Async XLA Ops:
  0.6 34.2 %collective-permute-start.1 = (bf16[128,3072]{1,0:T(8,128)(2,1)}, bf16[128,3072]{1,0:T(8,128)(2,1)}, u32[]{:S(2)}, u32[]{:S(2)}) collective-permute-start(bf16[128,3072]{1,0:T(8,128)(2,1)} %bitcast.14), channel_id=1, source_target_pairs={{0,1},{2,0},{4,2},{6,4},{7,6},{5,7},{3,5},{1,3},{8,10},{10,12},{12... | collective-permute-start | bytes 2359304 | tf_op jit(solution)/shard_map/ppermute | solution.py:377
  2.0 32.9 %collective-permute-start = (bf16[128,3072]{1,0:T(8,128)(2,1)}, bf16[128,3072]{1,0:T(8,128)(2,1)}, u32[]{:S(2)}, u32[]{:S(2)}) collective-permute-start(bf16[128,3072]{1,0:T(8,128)(2,1)} %bitcast.15), channel_id=1, source_target_pairs={{0,2},{2,4},{4,6},{6,7},{7,5},{5,3},{3,1},{1,0},{8,9},{10,8},{12,1... | collective-permute-start | bytes 2359304 | tf_op jit(solution)/shard_map/ppermute | solution.py:377
  4.7 5.5 %collective-permute-start.2 = (bf16[384,256]{1,0:T(8,128)(2,1)}, bf16[384,256]{1,0:T(8,128)(2,1)S(1)}, u32[]{:S(2)}, u32[]{:S(2)}) collective-permute-start(bf16[384,256]{1,0:T(8,128)(2,1)} %get-tuple-element.53), channel_id=1, source_target_pairs={{0,1},{1,0},{2,3},{3,2},{4,5},{5,4},{6,7},{7,6},{8,9},{9,8},{10,11... | collective-permute-start | bytes 589832 | tf_op jit(solution)/shard_map/ppermute | solution.py:398
  6.1 28.4 %collective-permute-start.3 = (bf16[384,256]{1,0:T(8,128)(2,1)}, bf16[384,256]{1,0:T(8,128)(2,1)S(1)}, u32[]{:S(2)}, u32[]{:S(2)}) collective-permute-start(bf16[384,256]{1,0:T(8,128)(2,1)} %get-tuple-element.54), channel_id=1, source_target_pairs={{0,6},{1,7},{2,4},{3,5},{4,2},{5,3},{6,0},{7,1},{8,14},{9,15},{10,... | collective-permute-start | bytes 589832 | tf_op jit(solution)/shard_map/ppermute | solution.py:398
  7.4 27.5 %collective-permute-start.4 = (bf16[384,256]{1,0:T(8,128)(2,1)}, bf16[384,256]{1,0:T(8,128)(2,1)}, u32[]{:S(2)}, u32[]{:S(2)}) collective-permute-start(bf16[384,256]{1,0:T(8,128)(2,1)} %get-tuple-element.55), channel_id=1, source_target_pairs={{0,5},{1,4},{2,7},{3,6},{4,1},{5,0},{6,3},{7,2},{8,13},{9,12},{10,... | collective-permute-start | bytes 589832 | tf_op jit(solution)/shard_map/ppermute | solution.py:398
  10.3 63.2 %copy-start.1 = (bf16[384,256]{1,0:T(8,128)(2,1)}, bf16[384,256]{1,0:T(8,128)(2,1)S(1)}, u32[]{:S(2)}) copy-start(bf16[384,256]{1,0:T(8,128)(2,1)S(1)} %collective-permute-done.2.refs_7_.refs_4_) | copy-start | bytes 589828
  10.3 24.6 %collective-permute-start.5 = (bf16[384,256]{1,0:T(8,128)(2,1)}, bf16[384,256]{1,0:T(8,128)(2,1)}, u32[]{:S(2)}, u32[]{:S(2)}) collective-permute-start(bf16[384,256]{1,0:T(8,128)(2,1)} %get-tuple-element.56), channel_id=1, source_target_pairs={{0,3},{1,2},{2,1},{3,0},{4,7},{5,6},{6,5},{7,4},{8,11},{9,10},{10,... | collective-permute-start | bytes 589832 | tf_op jit(solution)/shard_map/ppermute | solution.py:398
  34.5 38.9 %copy-start.2 = (bf16[384,256]{1,0:T(8,128)(2,1)}, bf16[384,256]{1,0:T(8,128)(2,1)S(1)}, u32[]{:S(2)}) copy-start(bf16[384,256]{1,0:T(8,128)(2,1)S(1)} %collective-permute-done.3.refs_12_.refs_9_) | copy-start | bytes 589828
  34.9 37.0 %collective-permute-start.6 = (bf16[128,3072]{1,0:T(8,128)(2,1)}, bf16[128,3072]{1,0:T(8,128)(2,1)}, u32[]{:S(2)}, u32[]{:S(2)}) collective-permute-start(bf16[128,3072]{1,0:T(8,128)(2,1)} %collective-permute-done.refs_1_), channel_id=1, source_target_pairs={{0,2},{2,4},{4,6},{6,7},{7,5},{5,3},{3,1},{1,0},{8,9},{10,8},{12,1... | collective-permute-start | bytes 2359304 | tf_op jit(solution)/shard_map/ppermute | solution.py:377
  36.5 35.4 %collective-permute-start.7 = (bf16[128,3072]{1,0:T(8,128)(2,1)}, bf16[128,3072]{1,0:T(8,128)(2,1)}, u32[]{:S(2)}, u32[]{:S(2)}) collective-permute-start(bf16[128,3072]{1,0:T(8,128)(2,1)} %collective-permute-done.1.refs_2_), channel_id=1, source_target_pairs={{0,1},{2,0},{4,2},{6,4},{7,6},{5,7},{3,5},{1,3},{8,10},{10,12},{12... | collective-permute-start | bytes 2359304 | tf_op jit(solution)/shard_map/ppermute | solution.py:377
  37.9 31.5 %collective-permute-start.8 = (bf16[384,256]{1,0:T(8,128)(2,1)}, bf16[384,256]{1,0:T(8,128)(2,1)}, u32[]{:S(2)}, u32[]{:S(2)}) collective-permute-start(bf16[384,256]{1,0:T(8,128)(2,1)} %get-tuple-element.59), channel_id=1, source_target_pairs={{0,7},{1,6},{2,5},{3,4},{4,3},{5,2},{6,1},{7,0},{8,15},{9,14},{10,... | collective-permute-start | bytes 589832 | tf_op jit(solution)/shard_map/ppermute | solution.py:398
  39.2 32.7 %collective-permute-start.9 = (bf16[384,256]{1,0:T(8,128)(2,1)}, bf16[384,256]{1,0:T(8,128)(2,1)}, u32[]{:S(2)}, u32[]{:S(2)}) collective-permute-start(bf16[384,256]{1,0:T(8,128)(2,1)} %get-tuple-element.60), channel_id=1, source_target_pairs={{0,4},{1,5},{2,6},{3,7},{4,0},{5,1},{6,2},{7,3},{8,12},{9,13},{10,... | collective-permute-start | bytes 589832 | tf_op jit(solution)/shard_map/ppermute | solution.py:398
  44.1 27.8 %collective-permute-start.10 = (bf16[384,256]{1,0:T(8,128)(2,1)}, bf16[384,256]{1,0:T(8,128)(2,1)}, u32[]{:S(2)}, u32[]{:S(2)}) collective-permute-start(bf16[384,256]{1,0:T(8,128)(2,1)} %get-tuple-element.61), channel_id=1, source_target_pairs={{0,2},{1,3},{2,0},{3,1},{4,6},{5,7},{6,4},{7,5},{8,10},{9,11},{10,... | collective-permute-start | bytes 589832 | tf_op jit(solution)/shard_map/ppermute | solution.py:398
  71.9 19.3 %collective-permute-start.11 = (bf16[128,3072]{1,0:T(8,128)(2,1)}, bf16[128,3072]{1,0:T(8,128)(2,1)}, u32[]{:S(2)}, u32[]{:S(2)}) collective-permute-start(bf16[128,3072]{1,0:T(8,128)(2,1)} %collective-permute-done.6.refs_3_), channel_id=1, source_target_pairs={{0,2},{2,4},{4,6},{6,7},{7,5},{5,3},{3,1},{1,0},{8,9},{10,8},{12,1... | collective-permute-start | bytes 2359304 | tf_op jit(solution)/shard_map/ppermute | solution.py:377
  72.0 21.2 %collective-permute-start.12 = (bf16[128,3072]{1,0:T(8,128)(2,1)}, bf16[128,3072]{1,0:T(8,128)(2,1)}, u32[]{:S(2)}, u32[]{:S(2)}) collective-permute-start(bf16[128,3072]{1,0:T(8,128)(2,1)} %collective-permute-done.7.refs_4_), channel_id=1, source_target_pairs={{0,1},{2,0},{4,2},{6,4},{7,6},{5,7},{3,5},{1,3},{8,10},{10,12},{12... | collective-permute-start | bytes 2359304 | tf_op jit(solution)/shard_map/ppermute | solution.py:377
  93.1 15.0 %collective-permute-start.13 = (bf16[128,3072]{1,0:T(8,128)(2,1)}, bf16[128,3072]{1,0:T(8,128)(2,1)}, u32[]{:S(2)}, u32[]{:S(2)}) collective-permute-start(bf16[128,3072]{1,0:T(8,128)(2,1)} %collective-permute-done.11.refs_0_.refs_16_), channel_id=1, source_target_pairs={{0,2},{2,4},{4,6},{6,7},{7,5},{5,3},{3,1},{1,0},{8,9},{10,8},{12,1... | collective-permute-start | bytes 2359304 | tf_op jit(solution)/shard_map/ppermute | solution.py:377
  104.1 18.7 %all-to-all-start = ((bf16[8,128,256]{2,1,0:T(8,128)(2,1)}), bf16[8,128,256]{2,1,0:T(8,128)(2,1)}, u32[]{:S(2)}, u32[]{:S(2)}) async-start(bf16[8,128,256]{2,1,0:T(8,128)(2,1)} %get-tuple-element.80), calls=%async_computation | async-start | bytes 1048576 | tf_op jit(solution)/shard_map/all_to_all | solution.py:476
  118.2 20.6 %copy-start = (bf16[2,32,3072]{2,1,0:T(8,128)(2,1)S(1)}, bf16[2,32,3072]{2,1,0:T(8,128)(2,1)}, u32[]{:S(2)}) copy-start(bf16[2,32,3072]{2,1,0:T(8,128)(2,1)} %get-tuple-element.95.refs_0_) | copy-start | bytes 1179652
  118.3 10.7 %collective-permute-start.15 = (bf16[2,32,3072]{2,1,0:T(8,128)(2,1)}, bf16[2,32,3072]{2,1,0:T(8,128)(2,1)S(1)}, u32[]{:S(2)}, u32[]{:S(2)}) collective-permute-start(bf16[2,32,3072]{2,1,0:T(8,128)(2,1)} %get-tuple-element.89), channel_id=1, source_target_pairs={{0,8},{8,0},{16,24},{24,16},{1,9},{9,1},{17,25},{25,17},{2,10},{10... | collective-permute-start | bytes 1179656 | tf_op jit(solution)/shard_map/ppermute | solution.py:398
  118.9 10.9 %collective-permute-start.16 = (bf16[2,32,3072]{2,1,0:T(8,128)(2,1)}, bf16[2,32,3072]{2,1,0:T(8,128)(2,1)S(1)}, u32[]{:S(2)}, u32[]{:S(2)}) collective-permute-start(bf16[2,32,3072]{2,1,0:T(8,128)(2,1)} %get-tuple-element.90), channel_id=1, source_target_pairs={{0,16},{8,24},{16,0},{24,8},{1,17},{9,25},{17,1},{25,9},{2,18},{10... | collective-permute-start | bytes 1179656 | tf_op jit(solution)/shard_map/ppermute | solution.py:398
  120.2 18.7 %collective-permute-start.17 = (bf16[2,32,3072]{2,1,0:T(8,128)(2,1)}, bf16[2,32,3072]{2,1,0:T(8,128)(2,1)S(1)}, u32[]{:S(2)}, u32[]{:S(2)}) collective-permute-start(bf16[2,32,3072]{2,1,0:T(8,128)(2,1)} %get-tuple-element.91), channel_id=1, source_target_pairs={{0,24},{8,16},{16,8},{24,0},{1,25},{9,17},{17,9},{25,1},{2,26},{10... | collective-permute-start | bytes 1179656 | tf_op jit(solution)/shard_map/ppermute | solution.py:398
  120.6 8.3 %collective-permute-start.14 = (bf16[128,256]{1,0:T(8,128)(2,1)}, bf16[128,256]{1,0:T(8,128)(2,1)S(1)}, u32[]{:S(2)}, u32[]{:S(2)}) collective-permute-start(bf16[128,256]{1,0:T(8,128)(2,1)} %get-tuple-element.87), channel_id=1, source_target_pairs={{0,7},{2,5},{4,3},{6,1},{7,0},{5,2},{3,4},{1,6},{8,15},{10,13},{12... | collective-permute-start | bytes 196616 | tf_op jit(solution)/shard_map/ppermute | solution.py:514
  122.8 31.7 %all-to-all-start.1 = ((bf16[8,256,256]{2,1,0:T(8,128)(2,1)}), bf16[8,256,256]{2,1,0:T(8,128)(2,1)}, u32[]{:S(2)}, u32[]{:S(2)}) async-start(bf16[8,256,256]{2,1,0:T(8,128)(2,1)} %get-tuple-element.94), calls=%async_computation.1 | async-start | bytes 2097152 | tf_op jit(solution)/shard_map/all_to_all | solution.py:515
  140.3 10.9 %collective-permute-start.19 = (bf16[2,32,3072]{2,1,0:T(8,128)(2,1)S(1)}, bf16[2,32,3072]{2,1,0:T(8,128)(2,1)S(1)}, u32[]{:S(2)}, u32[]{:S(2)}) collective-permute-start(bf16[2,32,3072]{2,1,0:T(8,128)(2,1)S(1)} %get-tuple-element.99.refs_0_), channel_id=1, source_target_pairs={{0,16},{8,24},{16,0},{24,8},{1,17},{9,25},{17,1},{25,9},{2,18},{10... | collective-permute-start | bytes 1179656 | tf_op jit(solution)/shard_map/ppermute | solution.py:535
  141.5 10.3 %collective-permute-start.18 = (bf16[2,32,3072]{2,1,0:T(8,128)(2,1)S(1)}, bf16[2,32,3072]{2,1,0:T(8,128)(2,1)S(1)}, u32[]{:S(2)}, u32[]{:S(2)}) collective-permute-start(bf16[2,32,3072]{2,1,0:T(8,128)(2,1)S(1)} %get-tuple-element.99.refs_0_), channel_id=1, source_target_pairs={{0,8},{8,0},{16,24},{24,16},{1,9},{9,1},{17,25},{25,17},{2,10},{10... | collective-permute-start | bytes 1179656 | tf_op jit(solution)/shard_map/ppermute | solution.py:535
  151.2 1.9 %collective-permute-start.20 = (bf16[2,32,3072]{2,1,0:T(8,128)(2,1)S(1)}, bf16[2,32,3072]{2,1,0:T(8,128)(2,1)S(1)}, u32[]{:S(2)}, u32[]{:S(2)}) collective-permute-start(bf16[2,32,3072]{2,1,0:T(8,128)(2,1)S(1)} %collective-permute-done.19.refs_2_), channel_id=1, source_target_pairs={{0,8},{8,0},{16,24},{24,16},{1,9},{9,1},{17,25},{25,17},{2,10},{10... | collective-permute-start | bytes 1179656 | tf_op jit(solution)/shard_map/ppermute | solution.py:535

commit v6 on v5

--- a/solution.py
+++ b/solution.py
@@ -36,7 +36,8 @@
 
 def waves_of(n):
     late = [n - 1] + [k for k in range(n - 2, 1, -1) if k & (k - 1) == 0]
-    return [[1] + [k for k in range(n - 2, 1, -1) if k not in late], late]
+    early = [1] + [k for k in range(n - 2, 1, -1) if k not in late]
+    return [early, late[:1] + late[:0:-1]]
 
 
 def dot_nt(a, b):
@@ -514,7 +515,9 @@
     far_back = lax.ppermute(far_query, "seq", across)
     other_back = lax.all_to_all(grads, "seq", split_axis=0, concat_axis=0, tiled=True)
 
-    received = [sent[0]] + [send(sent, k, "dp") for k in range(1, workers)]
+    received = [sent[0]] + [None] * (workers - 1)
+    for k in range(workers - 1, 0, -1):
+        received[k] = send(sent, k, "dp")
 
     query_back, far_back, *received = lax.optimization_barrier(
         [query_back, far_back, *received]

time: 160 us -> 160 us (level)
  transfers between devices with their start and end apart: 23 -> 23, of which waited for: 10 -> 11; matrix products, arithmetic and copies ran while one was open for 0% -> 0% of each run, Pallas kernels for 27% -> 27%
where the time goes in v6:
time: 160 us; the launch traced here: 157 us
  waiting for transfers between devices  62.6 us (39%)
  starting transfers between devices  49 us (31%)
  Pallas kernels  44.5 us (28%)
    ppermute x10, waiting for transfers between devices, send(): lax.ppermute(blocks[k], axis, [(i, i ^ k) for i in range(len(blocks))])  49.7 us
    pallas_call x2, Pallas kernels, attend(): pl.pallas_call(functools.partial(attend_kernel, n, heads_here, per_group,...  26.7 us
    ppermute x10, starting transfers between devices, send(): lax.ppermute(blocks[k], axis, [(i, i ^ k) for i in range(len(blocks))])  26.6 us
    ppermute x3, waiting for transfers between devices, body(): lax.ppermute(source, 'dp', [(i, i ^ step) for i in range(workers)])  11 us
    pallas_call x1, Pallas kernels, body(): pl.pallas_call(functools.partial(tail_kernel, n, heads_here, per_group, w...  10 us
    ppermute x7, starting transfers between devices, around(): return lambda x: lax.ppermute(x, ('dp', 'seq'), pairs)  8.02 us
    all_to_all x1, starting transfers between devices, body(): lax.all_to_all(grads, 'seq', split_axis=0, concat_axis=0, tiled=True)  6.22 us
    all_to_all x1, starting transfers between devices, body(): lax.all_to_all(query, 'seq', split_axis=0, concat_axis=0, tiled=True)  4.12 us
  transfers between devices with their start and end apart: 23, of which 11 were waited for; matrix products, arithmetic and copies ran while one was open for 0% of the time, Pallas kernels for 27%

profile of v6, /device:TPU:9, one launch (start us, length us, event | category | flops | bytes accessed | tf_op | source)
XLA Modules:
  0.0 156.9 jit_solution(16374968768494079339)
XLA Ops:
  0.6 1.3 collective-permute-start.1
  2.0 0.2 collective-permute-start
  2.1 2.6 %pack.1 = (bf16[384,256]{1,0:T(8,128)(2,1)}, bf16[384,256]{1,0:T(8,128)(2,1)}, bf16[384,256]{1,0:T(8,128)(2,1)}, bf16[384,256]{1,0:T(8,128)(2,1)}, bf16[384,256]...) custom-call(bf16[384,16,128]{2,1,0:T(8,128)(2,1)} %bitcast.11), custom_call_target="tpu_custom_call" | custom-call | bytes 3145728 | tf_op jit(solution)/shard_map/pack/pallas_call | solution.py:383
  4.7 1.3 collective-permute-start.2
  6.1 1.3 collective-permute-start.3
  7.4 1.0 collective-permute-start.4
  8.3 2.0 %collective-permute-done.2.refs_7_.refs_4_ = bf16[384,256]{1,0:T(8,128)(2,1)S(1)} collective-permute-done((bf16[384,256]{1,0:T(8,128)(2,1)}, bf16[384,256]{1,0:T(8,128)(2,1)S(1)}, u32[]{:S(2)}, u32[]{:S(2)}) %collective-permute-start.2) | collective-permute-done | bytes 196640 | tf_op jit(solution)/shard_map/ppermute | solution.py:399
  10.3 0.0 copy-start.1
  10.3 14.5 %collective-permute-start.5 = (bf16[384,256]{1,0:T(8,128)(2,1)}, bf16[384,256]{1,0:T(8,128)(2,1)}, u32[]{:S(2)}, u32[]{:S(2)}) collective-permute-start(bf16[384,256]{1,0:T(8,128)(2,1)} %get-tuple-element.56), channel_id=1, source_target_pairs={{0,3},{1,2},{2,1},{3,0},{4,7},{5,6},{6,5},{7,4},{8,11},{9,10},{10,... | collective-permute-start | bytes 589832 | tf_op jit(solution)/shard_map/ppermute | solution.py:399
  24.8 9.7 %collective-permute-done.3.refs_12_.refs_9_ = bf16[384,256]{1,0:T(8,128)(2,1)S(1)} collective-permute-done((bf16[384,256]{1,0:T(8,128)(2,1)}, bf16[384,256]{1,0:T(8,128)(2,1)S(1)}, u32[]{:S(2)}, u32[]{:S(2)}) %collective-permute-start.3) | collective-permute-done | bytes 196640 | tf_op jit(solution)/shard_map/ppermute | solution.py:399
  34.5 0.0 copy-start.2
  34.5 0.4 collective-permute-done.4.refs_11_.refs_8_
  34.9 0.0 collective-permute-done.5.refs_9_.refs_6_
  34.9 0.0 collective-permute-done.1.refs_2_
  34.9 0.0 collective-permute-done.refs_1_
  34.9 1.7 %collective-permute-start.6 = (bf16[128,3072]{1,0:T(8,128)(2,1)}, bf16[128,3072]{1,0:T(8,128)(2,1)}, u32[]{:S(2)}, u32[]{:S(2)}) collective-permute-start(bf16[128,3072]{1,0:T(8,128)(2,1)} %collective-permute-done.refs_1_), channel_id=1, source_target_pairs={{0,2},{2,4},{4,6},{6,7},{7,5},{5,3},{3,1},{1,0},{8,9},{10,8},{12,1... | collective-permute-start | bytes 2359304 | tf_op jit(solution)/shard_map/ppermute | solution.py:378
  36.5 1.4 collective-permute-start.7
  37.9 1.3 collective-permute-start.8
  39.2 3.0 %collective-permute-start.9 = (bf16[384,256]{1,0:T(8,128)(2,1)}, bf16[384,256]{1,0:T(8,128)(2,1)}, u32[]{:S(2)}, u32[]{:S(2)}) collective-permute-start(bf16[384,256]{1,0:T(8,128)(2,1)} %get-tuple-element.60), channel_id=1, source_target_pairs={{0,2},{1,3},{2,0},{3,1},{4,6},{5,7},{6,4},{7,5},{8,10},{9,11},{10,... | collective-permute-start | bytes 589832 | tf_op jit(solution)/shard_map/ppermute | solution.py:399
  42.2 1.9 %collective-permute-start.10 = (bf16[384,256]{1,0:T(8,128)(2,1)}, bf16[384,256]{1,0:T(8,128)(2,1)}, u32[]{:S(2)}, u32[]{:S(2)}) collective-permute-start(bf16[384,256]{1,0:T(8,128)(2,1)} %get-tuple-element.61), channel_id=1, source_target_pairs={{0,4},{1,5},{2,6},{3,7},{4,0},{5,1},{6,2},{7,3},{8,12},{9,13},{10,... | collective-permute-start | bytes 589832 | tf_op jit(solution)/shard_map/ppermute | solution.py:399
  44.1 21.2 %collective-permute-done.8.refs_13_.refs_10_ = bf16[384,256]{1,0:T(8,128)(2,1)} collective-permute-done((bf16[384,256]{1,0:T(8,128)(2,1)}, bf16[384,256]{1,0:T(8,128)(2,1)}, u32[]{:S(2)}, u32[]{:S(2)}) %collective-permute-start.8) | collective-permute-done | bytes 196640 | tf_op jit(solution)/shard_map/ppermute | solution.py:399
  65.3 2.1 %collective-permute-done.9.refs_8_.refs_5_ = bf16[384,256]{1,0:T(8,128)(2,1)} collective-permute-done((bf16[384,256]{1,0:T(8,128)(2,1)}, bf16[384,256]{1,0:T(8,128)(2,1)}, u32[]{:S(2)}, u32[]{:S(2)}) %collective-permute-start.9) | collective-permute-done | bytes 196640 | tf_op jit(solution)/shard_map/ppermute | solution.py:399
  67.3 4.6 %collective-permute-done.10.refs_10_.refs_7_ = bf16[384,256]{1,0:T(8,128)(2,1)} collective-permute-done((bf16[384,256]{1,0:T(8,128)(2,1)}, bf16[384,256]{1,0:T(8,128)(2,1)}, u32[]{:S(2)}, u32[]{:S(2)}) %collective-permute-start.10) | collective-permute-done | bytes 196640 | tf_op jit(solution)/shard_map/ppermute | solution.py:399
  71.9 0.0 collective-permute-done.6.refs_3_
  71.9 0.0 collective-permute-done.7.refs_4_
  71.9 0.0 collective-permute-start.11
  71.9 1.5 collective-permute-start.12
  73.4 0.0 copy-done.1
  73.4 0.0 copy-done.2
  73.4 17.8 %attend.2 = (bf16[640,256]{1,0:T(8,128)(2,1)}, f32[1024,256]{1,0:T(8,128)}, f32[1024,256]{1,0:T(8,128)}, bf16[640,256]{1,0:T(8,128)(2,1)}, f32[2,128,1024]{2,1,0...) custom-call(s32[8,8,8]{2,1,0:T(8,128)} %refs_0_.1, bf16[128,3072]{1,0:T(8,128)(2,1)} %bitcast.16, ...), custom_call_target="tpu_custom_call" | custom-call | flops 3355443200 | bytes 41943040 | tf_op jit(solution)/shard_map/attend/pallas_call | solution.py:431
  91.1 0.0 collective-permute-done.11.refs_0_.refs_16_
  91.2 1.9 %collective-permute-done.12.refs_1_.refs_17_ = bf16[128,3072]{1,0:T(8,128)(2,1)} collective-permute-done((bf16[128,3072]{1,0:T(8,128)(2,1)}, bf16[128,3072]{1,0:T(8,128)(2,1)}, u32[]{:S(2)}, u32[]{:S(2)}) %collective-permute-start.12) | collective-permute-done | bytes 786464 | tf_op jit(solution)/shard_map/ppermute | solution.py:378
  93.1 2.0 %collective-permute-start.13 = (bf16[128,3072]{1,0:T(8,128)(2,1)}, bf16[128,3072]{1,0:T(8,128)(2,1)}, u32[]{:S(2)}, u32[]{:S(2)}) collective-permute-start(bf16[128,3072]{1,0:T(8,128)(2,1)} %collective-permute-done.11.refs_0_.refs_16_), channel_id=1, source_target_pairs={{0,2},{2,4},{4,6},{6,7},{7,5},{5,3},{3,1},{1,0},{8,9},{10,8},{12,1... | collective-permute-start | bytes 2359304 | tf_op jit(solution)/shard_map/ppermute | solution.py:378
  95.0 9.0 %attend.3 = (bf16[8,128,256]{2,1,0:T(8,128)(2,1)}, f32[1024,256]{1,0:T(8,128)}, f32[1024,256]{1,0:T(8,128)}, bf16[256,256]{1,0:T(8,128)(2,1)}) custom-call(s32[8,8,8]{2,1,0:T(8,128)} %refs_0_.1, bf16[128,3072]{1,0:T(8,128)(2,1)} %collective-permute-done.11.refs_0_.refs_16_, bf16[128,3072]{1,0:T(8,128)(2,1)} %collective-permute-done.12.refs_1_.refs_17_, ...), custom_call_target="tpu_custom_call" | custom-call | flops 1342177280 | bytes 16777216 | tf_op jit(solution)/shard_map/attend/pallas_call | solution.py:431
  104.0 4.1 %all-to-all-start = ((bf16[8,128,256]{2,1,0:T(8,128)(2,1)}), bf16[8,128,256]{2,1,0:T(8,128)(2,1)}, u32[]{:S(2)}, u32[]{:S(2)}) async-start(bf16[8,128,256]{2,1,0:T(8,128)(2,1)} %get-tuple-element.80), calls=%async_computation | async-start | bytes 1048576 | tf_op jit(solution)/shard_map/all_to_all | solution.py:477
  108.2 0.0 collective-permute-done.13.refs_1_
  108.2 10.0 %tail.1 = (bf16[128,256]{1,0:T(8,128)(2,1)}, bf16[8,256,256]{2,1,0:T(8,128)(2,1)}, f32[256,3072]{1,0:T(8,128)}, bf16[2,32,3072]{2,1,0:T(8,128)(2,1)}, bf16[2,32,...) custom-call(s32[8,8,8]{2,1,0:T(8,128)} %refs_0_.1, ...), custom_call_target="tpu_custom_call" | custom-call | flops 9999999827968 | bytes 16777216 | tf_op jit(solution)/shard_map/tail/pallas_call | solution.py:482
  118.2 0.0 copy-start
  118.2 0.7 collective-permute-start.15
  118.9 1.2 collective-permute-start.16
  120.1 0.5 collective-permute-start.17
  120.6 2.1 %collective-permute-start.14 = (bf16[128,256]{1,0:T(8,128)(2,1)}, bf16[128,256]{1,0:T(8,128)(2,1)S(1)}, u32[]{:S(2)}, u32[]{:S(2)}) collective-permute-start(bf16[128,256]{1,0:T(8,128)(2,1)} %get-tuple-element.87), channel_id=1, source_target_pairs={{0,7},{2,5},{4,3},{6,1},{7,0},{5,2},{3,4},{1,6},{8,15},{10,13},{12... | collective-permute-start | bytes 196616 | tf_op jit(solution)/shard_map/ppermute | solution.py:515
  122.7 0.0 all-to-all-done.queries_ref
  122.7 6.2 %all-to-all-start.1 = ((bf16[8,256,256]{2,1,0:T(8,128)(2,1)}), bf16[8,256,256]{2,1,0:T(8,128)(2,1)}, u32[]{:S(2)}, u32[]{:S(2)}) async-start(bf16[8,256,256]{2,1,0:T(8,128)(2,1)} %get-tuple-element.94), calls=%async_computation.1 | async-start | bytes 2097152 | tf_op jit(solution)/shard_map/all_to_all | solution.py:516
  128.9 0.0 collective-permute-done.14.far_ref
  128.9 0.0 collective-permute-done.15.refs_1_
  128.9 0.9 collective-permute-done.16.refs_2_
  129.8 9.0 %collective-permute-done.17.refs_3_ = bf16[2,32,3072]{2,1,0:T(8,128)(2,1)S(1)} collective-permute-done((bf16[2,32,3072]{2,1,0:T(8,128)(2,1)}, bf16[2,32,3072]{2,1,0:T(8,128)(2,1)S(1)}, u32[]{:S(2)}, u32[]{:S(2)}) %collective-permute-start.17) | collective-permute-done | bytes 393248 | tf_op jit(solution)/shard_map/ppermute | solution.py:399
  138.8 0.0 copy-done
  138.8 1.5 server.1
  140.2 1.2 collective-permute-start.19
  141.5 0.1 collective-permute-start.18
  141.6 9.6 %collective-permute-done.19.refs_2_ = bf16[2,32,3072]{2,1,0:T(8,128)(2,1)S(1)} collective-permute-done((bf16[2,32,3072]{2,1,0:T(8,128)(2,1)S(1)}, bf16[2,32,3072]{2,1,0:T(8,128)(2,1)S(1)}, u32[]{:S(2)}, u32[]{:S(2)}) %collective-permute-start.19) | collective-permute-done | bytes 393248 | tf_op jit(solution)/shard_map/ppermute | solution.py:538
  151.2 0.6 collective-permute-start.20
  151.8 0.0 collective-permute-done.18.refs_1_
  151.8 1.3 collective-permute-done.20.refs_3_
  153.1 1.3 join.1
  154.4 0.0 all-to-all-done.1.others_ref
  154.4 2.4 %unpack.1 = bf16[384,16,128]{2,1,0:T(8,128)(2,1)} custom-call(bf16[8,128,256]{2,1,0:T(8,128)(2,1)} %all-to-all-done.queries_ref, bf16[128,256]{1,0:T(8,128)(2,1)S(1)} %collective-permute-done.14.far_ref, bf16[8,256,256]{2,1,0:T(8,128)(2,1)} %all-to-all-done.1.others_ref), custom_call_target="tpu_custom_call" | custom-call | bytes 3145728 | tf_op jit(solution)/shard_map/unpack/pallas_call | solution.py:540
Async XLA Ops:
  0.6 34.2 %collective-permute-start.1 = (bf16[128,3072]{1,0:T(8,128)(2,1)}, bf16[128,3072]{1,0:T(8,128)(2,1)}, u32[]{:S(2)}, u32[]{:S(2)}) collective-permute-start(bf16[128,3072]{1,0:T(8,128)(2,1)} %bitcast.14), channel_id=1, source_target_pairs={{0,1},{2,0},{4,2},{6,4},{7,6},{5,7},{3,5},{1,3},{8,10},{10,12},{12... | collective-permute-start | bytes 2359304 | tf_op jit(solution)/shard_map/ppermute | solution.py:378
  2.0 32.9 %collective-permute-start = (bf16[128,3072]{1,0:T(8,128)(2,1)}, bf16[128,3072]{1,0:T(8,128)(2,1)}, u32[]{:S(2)}, u32[]{:S(2)}) collective-permute-start(bf16[128,3072]{1,0:T(8,128)(2,1)} %bitcast.15), channel_id=1, source_target_pairs={{0,2},{2,4},{4,6},{6,7},{7,5},{5,3},{3,1},{1,0},{8,9},{10,8},{12,1... | collective-permute-start | bytes 2359304 | tf_op jit(solution)/shard_map/ppermute | solution.py:378
  4.7 5.5 %collective-permute-start.2 = (bf16[384,256]{1,0:T(8,128)(2,1)}, bf16[384,256]{1,0:T(8,128)(2,1)S(1)}, u32[]{:S(2)}, u32[]{:S(2)}) collective-permute-start(bf16[384,256]{1,0:T(8,128)(2,1)} %get-tuple-element.53), channel_id=1, source_target_pairs={{0,1},{1,0},{2,3},{3,2},{4,5},{5,4},{6,7},{7,6},{8,9},{9,8},{10,11... | collective-permute-start | bytes 589832 | tf_op jit(solution)/shard_map/ppermute | solution.py:399
  6.1 28.4 %collective-permute-start.3 = (bf16[384,256]{1,0:T(8,128)(2,1)}, bf16[384,256]{1,0:T(8,128)(2,1)S(1)}, u32[]{:S(2)}, u32[]{:S(2)}) collective-permute-start(bf16[384,256]{1,0:T(8,128)(2,1)} %get-tuple-element.54), channel_id=1, source_target_pairs={{0,6},{1,7},{2,4},{3,5},{4,2},{5,3},{6,0},{7,1},{8,14},{9,15},{10,... | collective-permute-start | bytes 589832 | tf_op jit(solution)/shard_map/ppermute | solution.py:399
  7.4 27.5 %collective-permute-start.4 = (bf16[384,256]{1,0:T(8,128)(2,1)}, bf16[384,256]{1,0:T(8,128)(2,1)}, u32[]{:S(2)}, u32[]{:S(2)}) collective-permute-start(bf16[384,256]{1,0:T(8,128)(2,1)} %get-tuple-element.55), channel_id=1, source_target_pairs={{0,5},{1,4},{2,7},{3,6},{4,1},{5,0},{6,3},{7,2},{8,13},{9,12},{10,... | collective-permute-start | bytes 589832 | tf_op jit(solution)/shard_map/ppermute | solution.py:399
  10.3 63.1 %copy-start.1 = (bf16[384,256]{1,0:T(8,128)(2,1)}, bf16[384,256]{1,0:T(8,128)(2,1)S(1)}, u32[]{:S(2)}) copy-start(bf16[384,256]{1,0:T(8,128)(2,1)S(1)} %collective-permute-done.2.refs_7_.refs_4_) | copy-start | bytes 589828
  10.3 24.6 %collective-permute-start.5 = (bf16[384,256]{1,0:T(8,128)(2,1)}, bf16[384,256]{1,0:T(8,128)(2,1)}, u32[]{:S(2)}, u32[]{:S(2)}) collective-permute-start(bf16[384,256]{1,0:T(8,128)(2,1)} %get-tuple-element.56), channel_id=1, source_target_pairs={{0,3},{1,2},{2,1},{3,0},{4,7},{5,6},{6,5},{7,4},{8,11},{9,10},{10,... | collective-permute-start | bytes 589832 | tf_op jit(solution)/shard_map/ppermute | solution.py:399
  34.5 38.9 %copy-start.2 = (bf16[384,256]{1,0:T(8,128)(2,1)}, bf16[384,256]{1,0:T(8,128)(2,1)S(1)}, u32[]{:S(2)}) copy-start(bf16[384,256]{1,0:T(8,128)(2,1)S(1)} %collective-permute-done.3.refs_12_.refs_9_) | copy-start | bytes 589828
  34.9 37.0 %collective-permute-start.6 = (bf16[128,3072]{1,0:T(8,128)(2,1)}, bf16[128,3072]{1,0:T(8,128)(2,1)}, u32[]{:S(2)}, u32[]{:S(2)}) collective-permute-start(bf16[128,3072]{1,0:T(8,128)(2,1)} %collective-permute-done.refs_1_), channel_id=1, source_target_pairs={{0,2},{2,4},{4,6},{6,7},{7,5},{5,3},{3,1},{1,0},{8,9},{10,8},{12,1... | collective-permute-start | bytes 2359304 | tf_op jit(solution)/shard_map/ppermute | solution.py:378
  36.5 35.4 %collective-permute-start.7 = (bf16[128,3072]{1,0:T(8,128)(2,1)}, bf16[128,3072]{1,0:T(8,128)(2,1)}, u32[]{:S(2)}, u32[]{:S(2)}) collective-permute-start(bf16[128,3072]{1,0:T(8,128)(2,1)} %collective-permute-done.1.refs_2_), channel_id=1, source_target_pairs={{0,1},{2,0},{4,2},{6,4},{7,6},{5,7},{3,5},{1,3},{8,10},{10,12},{12... | collective-permute-start | bytes 2359304 | tf_op jit(solution)/shard_map/ppermute | solution.py:378
  37.9 27.3 %collective-permute-start.8 = (bf16[384,256]{1,0:T(8,128)(2,1)}, bf16[384,256]{1,0:T(8,128)(2,1)}, u32[]{:S(2)}, u32[]{:S(2)}) collective-permute-start(bf16[384,256]{1,0:T(8,128)(2,1)} %get-tuple-element.59), channel_id=1, source_target_pairs={{0,7},{1,6},{2,5},{3,4},{4,3},{5,2},{6,1},{7,0},{8,15},{9,14},{10,... | collective-permute-start | bytes 589832 | tf_op jit(solution)/shard_map/ppermute | solution.py:399
  39.2 28.1 %collective-permute-start.9 = (bf16[384,256]{1,0:T(8,128)(2,1)}, bf16[384,256]{1,0:T(8,128)(2,1)}, u32[]{:S(2)}, u32[]{:S(2)}) collective-permute-start(bf16[384,256]{1,0:T(8,128)(2,1)} %get-tuple-element.60), channel_id=1, source_target_pairs={{0,2},{1,3},{2,0},{3,1},{4,6},{5,7},{6,4},{7,5},{8,10},{9,11},{10,... | collective-permute-start | bytes 589832 | tf_op jit(solution)/shard_map/ppermute | solution.py:399
  42.2 29.7 %collective-permute-start.10 = (bf16[384,256]{1,0:T(8,128)(2,1)}, bf16[384,256]{1,0:T(8,128)(2,1)}, u32[]{:S(2)}, u32[]{:S(2)}) collective-permute-start(bf16[384,256]{1,0:T(8,128)(2,1)} %get-tuple-element.61), channel_id=1, source_target_pairs={{0,4},{1,5},{2,6},{3,7},{4,0},{5,1},{6,2},{7,3},{8,12},{9,13},{10,... | collective-permute-start | bytes 589832 | tf_op jit(solution)/shard_map/ppermute | solution.py:399
  71.9 19.2 %collective-permute-start.11 = (bf16[128,3072]{1,0:T(8,128)(2,1)}, bf16[128,3072]{1,0:T(8,128)(2,1)}, u32[]{:S(2)}, u32[]{:S(2)}) collective-permute-start(bf16[128,3072]{1,0:T(8,128)(2,1)} %collective-permute-done.6.refs_3_), channel_id=1, source_target_pairs={{0,2},{2,4},{4,6},{6,7},{7,5},{5,3},{3,1},{1,0},{8,9},{10,8},{12,1... | collective-permute-start | bytes 2359304 | tf_op jit(solution)/shard_map/ppermute | solution.py:378
  71.9 21.1 %collective-permute-start.12 = (bf16[128,3072]{1,0:T(8,128)(2,1)}, bf16[128,3072]{1,0:T(8,128)(2,1)}, u32[]{:S(2)}, u32[]{:S(2)}) collective-permute-start(bf16[128,3072]{1,0:T(8,128)(2,1)} %collective-permute-done.7.refs_4_), channel_id=1, source_target_pairs={{0,1},{2,0},{4,2},{6,4},{7,6},{5,7},{3,5},{1,3},{8,10},{10,12},{12... | collective-permute-start | bytes 2359304 | tf_op jit(solution)/shard_map/ppermute | solution.py:378
  93.1 15.1 %collective-permute-start.13 = (bf16[128,3072]{1,0:T(8,128)(2,1)}, bf16[128,3072]{1,0:T(8,128)(2,1)}, u32[]{:S(2)}, u32[]{:S(2)}) collective-permute-start(bf16[128,3072]{1,0:T(8,128)(2,1)} %collective-permute-done.11.refs_0_.refs_16_), channel_id=1, source_target_pairs={{0,2},{2,4},{4,6},{6,7},{7,5},{5,3},{3,1},{1,0},{8,9},{10,8},{12,1... | collective-permute-start | bytes 2359304 | tf_op jit(solution)/shard_map/ppermute | solution.py:378
  104.0 18.7 %all-to-all-start = ((bf16[8,128,256]{2,1,0:T(8,128)(2,1)}), bf16[8,128,256]{2,1,0:T(8,128)(2,1)}, u32[]{:S(2)}, u32[]{:S(2)}) async-start(bf16[8,128,256]{2,1,0:T(8,128)(2,1)} %get-tuple-element.80), calls=%async_computation | async-start | bytes 1048576 | tf_op jit(solution)/shard_map/all_to_all | solution.py:477
  118.2 20.6 %copy-start = (bf16[2,32,3072]{2,1,0:T(8,128)(2,1)S(1)}, bf16[2,32,3072]{2,1,0:T(8,128)(2,1)}, u32[]{:S(2)}) copy-start(bf16[2,32,3072]{2,1,0:T(8,128)(2,1)} %get-tuple-element.95.refs_0_) | copy-start | bytes 1179652
  118.2 10.7 %collective-permute-start.15 = (bf16[2,32,3072]{2,1,0:T(8,128)(2,1)}, bf16[2,32,3072]{2,1,0:T(8,128)(2,1)S(1)}, u32[]{:S(2)}, u32[]{:S(2)}) collective-permute-start(bf16[2,32,3072]{2,1,0:T(8,128)(2,1)} %get-tuple-element.89), channel_id=1, source_target_pairs={{0,8},{8,0},{16,24},{24,16},{1,9},{9,1},{17,25},{25,17},{2,10},{10... | collective-permute-start | bytes 1179656 | tf_op jit(solution)/shard_map/ppermute | solution.py:399
  118.9 10.9 %collective-permute-start.16 = (bf16[2,32,3072]{2,1,0:T(8,128)(2,1)}, bf16[2,32,3072]{2,1,0:T(8,128)(2,1)S(1)}, u32[]{:S(2)}, u32[]{:S(2)}) collective-permute-start(bf16[2,32,3072]{2,1,0:T(8,128)(2,1)} %get-tuple-element.90), channel_id=1, source_target_pairs={{0,16},{8,24},{16,0},{24,8},{1,17},{9,25},{17,1},{25,9},{2,18},{10... | collective-permute-start | bytes 1179656 | tf_op jit(solution)/shard_map/ppermute | solution.py:399
  120.1 18.7 %collective-permute-start.17 = (bf16[2,32,3072]{2,1,0:T(8,128)(2,1)}, bf16[2,32,3072]{2,1,0:T(8,128)(2,1)S(1)}, u32[]{:S(2)}, u32[]{:S(2)}) collective-permute-start(bf16[2,32,3072]{2,1,0:T(8,128)(2,1)} %get-tuple-element.91), channel_id=1, source_target_pairs={{0,24},{8,16},{16,8},{24,0},{1,25},{9,17},{17,9},{25,1},{2,26},{10... | collective-permute-start | bytes 1179656 | tf_op jit(solution)/shard_map/ppermute | solution.py:399
  120.6 8.3 %collective-permute-start.14 = (bf16[128,256]{1,0:T(8,128)(2,1)}, bf16[128,256]{1,0:T(8,128)(2,1)S(1)}, u32[]{:S(2)}, u32[]{:S(2)}) collective-permute-start(bf16[128,256]{1,0:T(8,128)(2,1)} %get-tuple-element.87), channel_id=1, source_target_pairs={{0,7},{2,5},{4,3},{6,1},{7,0},{5,2},{3,4},{1,6},{8,15},{10,13},{12... | collective-permute-start | bytes 196616 | tf_op jit(solution)/shard_map/ppermute | solution.py:515
  122.7 31.7 %all-to-all-start.1 = ((bf16[8,256,256]{2,1,0:T(8,128)(2,1)}), bf16[8,256,256]{2,1,0:T(8,128)(2,1)}, u32[]{:S(2)}, u32[]{:S(2)}) async-start(bf16[8,256,256]{2,1,0:T(8,128)(2,1)} %get-tuple-element.94), calls=%async_computation.1 | async-start | bytes 2097152 | tf_op jit(solution)/shard_map/all_to_all | solution.py:516
  140.2 10.9 %collective-permute-start.19 = (bf16[2,32,3072]{2,1,0:T(8,128)(2,1)S(1)}, bf16[2,32,3072]{2,1,0:T(8,128)(2,1)S(1)}, u32[]{:S(2)}, u32[]{:S(2)}) collective-permute-start(bf16[2,32,3072]{2,1,0:T(8,128)(2,1)S(1)} %get-tuple-element.99.refs_0_), channel_id=1, source_target_pairs={{0,16},{8,24},{16,0},{24,8},{1,17},{9,25},{17,1},{25,9},{2,18},{10... | collective-permute-start | bytes 1179656 | tf_op jit(solution)/shard_map/ppermute | solution.py:538
  141.5 10.3 %collective-permute-start.18 = (bf16[2,32,3072]{2,1,0:T(8,128)(2,1)S(1)}, bf16[2,32,3072]{2,1,0:T(8,128)(2,1)S(1)}, u32[]{:S(2)}, u32[]{:S(2)}) collective-permute-start(bf16[2,32,3072]{2,1,0:T(8,128)(2,1)S(1)} %get-tuple-element.99.refs_0_), channel_id=1, source_target_pairs={{0,8},{8,0},{16,24},{24,16},{1,9},{9,1},{17,25},{25,17},{2,10},{10... | collective-permute-start | bytes 1179656 | tf_op jit(solution)/shard_map/ppermute | solution.py:538
  151.2 1.9 %collective-permute-start.20 = (bf16[2,32,3072]{2,1,0:T(8,128)(2,1)S(1)}, bf16[2,32,3072]{2,1,0:T(8,128)(2,1)S(1)}, u32[]{:S(2)}, u32[]{:S(2)}) collective-permute-start(bf16[2,32,3072]{2,1,0:T(8,128)(2,1)S(1)} %collective-permute-done.19.refs_2_), channel_id=1, source_target_pairs={{0,8},{8,0},{16,24},{24,16},{1,9},{9,1},{17,25},{25,17},{2,10},{10... | collective-permute-start | bytes 1179656 | tf_op jit(solution)/shard_map/ppermute | solution.py:538
